TPU v7x, 1024 devices: a whole 4x4x32 slice. The times are simulated.
1024 devices in a mesh: user: 64 (over z_lo, y), item: 16 (over z_hi, x, core).
Axes of the slice: x: 4, y: 4, z: 32 (z_hi: 2, z_lo: 16; z = z_hi * 16 + z_lo), core: 2. Of those that a mesh axis runs over, the one named last changes fastest.
Arguments:
- item_features: bfloat16 [65536, 2048], P(('item', 'user')), may hold values from -6 to 6
- layer_one: bfloat16 [2048, 1024], replicated, may hold values from -0.125 to 0.125
- layer_two: bfloat16 [1024, 512], replicated, may hold values from -0.1875 to 0.1875
- log_weight: float32 [65536], P(('item', 'user')), may hold values from 0 to 4.9
- user_vectors: bfloat16 [32768, 512], P('user'), may hold values from -360 to 360
- positive_index: int32 [32768], P('user'), may hold values from 0 to 65535
Outputs:
- row_loss: float32 [32768], P('user')
- col_lse: float32 [65536], P(('item', 'user'))
All inputs are finite; a program needn't handle non-finite values.
Results may differ from a plain program's by a relative error of at most 0.007.
Values may be sent and summed in bfloat16 or wider, within the bound.
No kernel may reach another device: no remote copies, remote signals or barrier semaphores. Data moves between devices by JAX's collectives and lax.ppermute only.
A program may use at most 64 MiB of HBM per device.

v0:
```python
import math

import jax
import jax.numpy as jnp
from jax import lax
from jax.sharding import PartitionSpec as P


def merged(array, axis, combine):
    everything = jax.tree.map(lambda part: lax.all_gather(part, axis), array)
    initial = jax.tree.map(lambda part: part[0], everything)

    def step(k, so_far):
        return combine(so_far, jax.tree.map(lambda part: part[k], everything))

    return lax.fori_loop(1, lax.axis_size(axis), step, initial)


def combined_all(array, axis, combine):
    everything = jax.tree.map(
        lambda part, kind: lax.all_gather(part.astype(kind), axis),
        array,
        (jnp.bfloat16, jnp.bfloat16),
    )

    def take(k):
        return jax.tree.map(lambda part, own: part[k].astype(own.dtype), everything, array)

    return lax.fori_loop(
        1, lax.axis_size(axis), lambda k, so_far: combine(so_far, take(k)), take(0)
    )


def join_pair(first, second):
    top = jnp.maximum(first[0], second[0])
    total = first[1] * jnp.exp(first[0] - top) + second[1] * jnp.exp(second[0] - top)
    return (top, total)


def on_device(item_features, layer_one, layer_two, log_weight, user_vectors, positive_index):
    hidden = jax.nn.relu(
        jnp.dot(item_features, layer_one, preferred_element_type=jnp.float32)
    ).astype(jnp.bfloat16)
    embedded = jnp.dot(hidden, layer_two, preferred_element_type=jnp.float32).astype(jnp.bfloat16)
    users = user_vectors.shape[0]
    per_device = item_features.shape[0]
    inverse_temp = 4.0 / math.sqrt(user_vectors.shape[1])
    user_count = lax.axis_size("user")
    group = per_device * user_count
    group_start = lax.axis_index("item") * group
    row_max = jnp.full((users,), -1e30, jnp.float32)
    row_sum = jnp.zeros((users,), jnp.float32)
    row_positive = jnp.zeros((users,), jnp.float32)
    piece_vectors = lax.all_gather(embedded, "user", axis=0, tiled=True)
    piece_weight = lax.all_gather(
        log_weight.astype(jnp.bfloat16), "user", axis=0, tiled=True
    ).astype(jnp.float32)
    count = piece_vectors.shape[0]
    scores = (
        lax.dot_general(
            user_vectors,
            piece_vectors,
            (((1,), (1,)), ((), ())),
            preferred_element_type=jnp.float32,
        )
        * inverse_temp
    )
    top_col = jnp.max(scores, axis=0)
    sum_col = jnp.sum(jnp.exp(scores - top_col[None, :]), axis=0)
    col_max = top_col
    col_sum = sum_col
    logits = scores + piece_weight[None, :]
    new_max = jnp.maximum(row_max, jnp.max(logits, axis=1))
    row_sum = row_sum * jnp.exp(row_max - new_max) + jnp.sum(
        jnp.exp(logits - new_max[:, None]), axis=1
    )
    columns = group_start + lax.iota(jnp.int32, count)
    hits = positive_index[:, None] == columns[None, :]
    row_positive = row_positive + jnp.sum(jnp.where(hits, logits, 0.0), axis=1)
    row_max, row_sum, row_positive, col_max, col_sum = (
        new_max,
        row_sum,
        row_positive,
        col_max,
        col_sum,
    )
    top, total = merged((row_max, row_sum), "item", join_pair)
    positive = lax.psum(row_positive, "item")
    row_loss = top + jnp.log(total) - positive
    all_max, all_sum = combined_all((col_max, col_sum), "user", join_pair)
    every_lse = all_max + jnp.log(all_sum)
    col_lse = lax.dynamic_slice_in_dim(
        every_lse, lax.axis_index("user") * per_device, per_device, 0
    )
    return (row_loss, col_lse)


def solution(mesh):
    placed = (P(("item", "user"), None), P(), P(), P(("item", "user")), P("user", None), P("user"))
    return jax.shard_map(
        on_device,
        mesh=mesh,
        in_specs=placed,
        out_specs=(P("user"), P(("item", "user"))),
        check_vma=False,
    )
```

profile of v0, /device:TPU:1, one launch (start us, length us, event | category | flops | bytes accessed | tf_op | source)
XLA Modules:
  0.0 1748.4 jit_solution(1590230501841151959)
XLA Ops:
  7.2 0.0 copy-start
  7.2 0.0 all-gather.7.cloned.1.call-start
  7.2 1.2 copy-done
  8.4 3.9 fusion.5
  12.3 0.0 all-gather.7.cloned.1.call-update
  12.4 0.7 convert_element_type.78
  13.0 1.3 dynamic-slice
  15.0 0.2 dynamic-update-slice
  15.2 380.9 %all-reduce = bf16[4096]{0:T(1024)(128)(2,1)S(1)} all-reduce(bf16[4096]{0:T(1024)(128)(2,1)S(1)} %dynamic-update-slice), channel_id=1, replica_groups=mesh['user'=64,'item'=16] {'user'}, use_global_device_ids=true, to_apply=%add | all-reduce | flops 4096 | bytes 16384
  396.1 0.0 copy-start.1
  396.2 294.8 %all-gather.7.cloned.1.call-done = bf16[4096,512]{1,0:T(8,128)(2,1)} async-done(((bf16[64,512]{1,0:T(8,128)(2,1)}), bf16[4096,512]{1,0:T(8,128)(2,1)}) %all-gather.7.cloned.1.call-update) | async-done | bytes 4194320 | tf_op jit(solution)/shard_map/all_gather | solution.py:54
  690.9 4.8 fusion.8
  695.7 2.5 exponential_reduce_fusion
  698.3 116.4 %all-gather.3 = f32[16,1,512]{2,1,0:T(1,128)S(1)} all-gather(f32[1,1,512]{2,1,0:T(1,128)S(1)} %bitcast.45), channel_id=2, replica_groups=mesh['user'=64,'item'=16] {'item'}, dimensions={0}, use_global_device_ids=true | all-gather | bytes 34816 | tf_op jit(solution)/shard_map/all_gather | solution.py:10
  814.7 0.0 copy-done.1
  814.7 3.1 fusion.1
  817.9 53.0 %all-gather.4 = f32[16,1,512]{2,1,0:T(1,128)S(1)} all-gather(f32[1,1,512]{2,1,0:T(1,128)S(1)} %bitcast.46), channel_id=1, replica_groups=mesh['user'=64,'item'=16] {'item'}, dimensions={0}, use_global_device_ids=true | all-gather | bytes 34816 | tf_op jit(solution)/shard_map/all_gather | solution.py:10
  870.9 356.5 %all-gather.1 = bf16[262144]{0:T(1024)(128)(2,1)S(1)} all-gather(bf16[4096]{0:T(1024)(128)(2,1)S(1)} %convert_element_type.80), channel_id=3, replica_groups=mesh['user'=64,'item'=16] {'user'}, dimensions={0}, use_global_device_ids=true | all-gather | bytes 532480 | tf_op jit(solution)/shard_map/all_gather | solution.py:21
  1227.4 0.2 reshape.72
  1227.6 351.0 %all-gather.2 = bf16[262144]{0:T(1024)(128)(2,1)S(1)} all-gather(bf16[4096]{0:T(1024)(128)(2,1)S(1)} %get-tuple-element.274), channel_id=4, replica_groups=mesh['user'=64,'item'=16] {'user'}, dimensions={0}, use_global_device_ids=true | all-gather | bytes 532480 | tf_op jit(solution)/shard_map/all_gather | solution.py:21
  1578.6 0.2 reshape.73
  1578.8 155.1 %psum.7 = f32[512]{0:T(512)S(1)} all-reduce(f32[512]{0:T(512)S(1)} %get-tuple-element.273), channel_id=1, replica_groups=mesh['user'=64,'item'=16] {'item'}, use_global_device_ids=true, to_apply=%region_5.6 | all-reduce | flops 512 | bytes 4096 | tf_op jit(solution)/shard_map/psum | solution.py:88
  1733.9 0.9 while.34
  1734.8 5.6 while.35
  1740.4 0.6 add_subtract_fusion
  1741.0 0.6 dynamic-slice_add_fusion
  (168 shorter events, 4.2 us)
Async XLA Ops:
  7.2 1.2 copy-start
  7.2 683.8 %all-gather.7.cloned.1.call-start = ((), (), s32[]{:S(2)}) async-start(), calls=%async_computation | async-start | bytes 4259840 | tf_op jit(solution)/shard_map/all_gather | solution.py:54
  396.1 418.6 %copy-start.1 = (s32[512]{0:T(512)S(1)}, s32[512]{0:T(512)}, u32[]{:S(2)}) copy-start(s32[512]{0:T(512)} %param.15) | copy-start | bytes 6148
Sparse Core Ops, SparseCore 0:
  12.5 678.4 all-gather.6
where the time goes:
time: 1750 us
  blocking collectives  1410 us (81%)
  waiting for transfers between devices  295 us (17%)
    all_gather x2, blocking collectives, combined_all(): lax.all_gather(part.astype(kind), axis)  707 us
    unnamed x1, blocking collectives  381 us
    all_gather x1, waiting for transfers between devices, on_device(): piece_vectors = lax.all_gather(embedded, 'user', axis=0, tiled=True)  295 us
    all_gather x2, blocking collectives, merged(): everything = jax.tree.map(lambda part: lax.all_gather(part, axis), array)  169 us
    psum x1, blocking collectives, on_device(): positive = lax.psum(row_positive, 'item')  155 us
  transfers between devices with their start and end apart: 1, of which 1 were waited for; matrix products, arithmetic and copies ran while one was open for 0% of the time, Pallas kernels for 0%

commit v1 on v0

v1 whole, which is shorter than its diff:
```python
import functools
import math

import jax
import jax.numpy as jnp
from jax import lax
from jax.experimental import pallas as pl
from jax.experimental.pallas import tpu as pltpu
from jax.sharding import Mesh
from jax.sharding import PartitionSpec as P

F32, BF16 = jnp.float32, jnp.bfloat16
AXES = ("zl", "y", "zh", "x", "c")
SIZES = (16, 4, 2, 4, 2)
ZC = ("zl", "zh", "c")
PLANE = ("y", "x", "c")
RING = 32
BLOCK = 64
USERS = 512
Y = 4
DEPTH = 512
ITEMS = 256
EXTRA = 16
TEMP = 4.0 / math.sqrt(DEPTH)
LOG2E = 1.0 / math.log(2.0)
CHUNK = 32


def ring_index(z, c):
    z = z % RING
    return (z % 16 * 2 + z // 16) * 2 + c


def along(distance):
    return [
        (ring_index(z, c), ring_index(z + (distance if c == 0 else -distance), c))
        for z in range(RING)
        for c in range(2)
    ]


def across(distance):
    return [
        (ring_index(z, c), ring_index(z + (distance if c == 1 else -distance), 1 - c))
        for z in range(RING)
        for c in range(2)
    ]


def high_low(values):
    high = values.astype(BF16)
    return high, (values - high.astype(F32)).astype(BF16)


def score_kernel(first, last, base_ref, items_ref, users_ref, *refs):
    if first:
        item_ref, row_ref, scores, weight, ids, top_item, sum_item = refs
    else:
        past_ref, item_ref, row_ref, scores, weight, ids, top_item, sum_item = refs
    extra = items_ref[ITEMS : ITEMS + EXTRA, 0:256].astype(F32)
    packed = (extra[:, 0:128] + extra[:, 128:256]) * (1.0 / TEMP)
    for half in range(2):
        row = packed[8 * half : 8 * half + 1, :]
        weight[128 * half : 128 * half + 128, :] = jnp.broadcast_to(row, (128, 128)).T
    spot = lax.broadcasted_iota(jnp.int32, (BLOCK, 128), 0)
    for part in range(ITEMS // BLOCK):
        ids[part * BLOCK : (part + 1) * BLOCK, :] = (spot + base_ref[part]).astype(F32)

    chunks = [slice(g, g + CHUNK) for g in range(0, ITEMS, CHUNK)]
    tiles = [slice(k, k + 128) for k in range(0, USERS, 128)]
    tops, positives = [], []
    for y in range(Y):
        start = y * (USERS + EXTRA)
        raw = lax.dot_general(
            items_ref[0:ITEMS, :],
            users_ref[start : start + USERS, :],
            (((1,), (1,)), ((), ())),
            preferred_element_type=F32,
        )
        index_rows = users_ref[start + USERS : start + USERS + EXTRA, :].astype(F32)
        wanted = index_rows[0:1, :] * 256.0 + index_rows[1:2, :]
        top_y, positive_y = [], []
        for k in tiles:
            top, positive = None, None
            for g in chunks:
                piece = raw[g, k]
                scores[g, y * USERS + k.start : y * USERS + k.stop] = piece
                if y == 0 and k.start == 0:
                    top_item[g, :] = piece
                else:
                    top_item[g, :] = jnp.maximum(top_item[g, :], piece)
                logits = piece + weight[g, :]
                found = jnp.where(ids[g, :] == wanted[:, k], logits, 0.0)
                shape = (CHUNK // 8, 8, 128)
                part_top = jnp.max(logits.reshape(shape), axis=0)
                part_positive = jnp.sum(found.reshape(shape), axis=0)
                top = part_top if top is None else jnp.maximum(top, part_top)
                positive = part_positive if positive is None else positive + part_positive
            top_y.append(jnp.max(top, axis=0, keepdims=True))
            positive_y.append(jnp.sum(positive, axis=0, keepdims=True))
        tops.append(top_y)
        positives.append(positive_y)

    for g in chunks:
        top_item[g, :] = jnp.broadcast_to(
            jnp.max(top_item[g, :], axis=1, keepdims=True), (CHUNK, 128)
        )
    for y in range(Y):
        for t, k in enumerate(tiles):
            place = slice(y * USERS + k.start, y * USERS + k.stop)
            top, positive = tops[y][t], positives[y][t]
            if not first:
                old_top = past_ref[0:1, place]
                top = jnp.maximum(old_top, top)
                positive = positive + past_ref[2:3, place]
            total = None
            for g in chunks:
                piece = scores[g, place]
                by_item = jnp.exp2((piece - top_item[g, :]) * (TEMP * LOG2E))
                if y == 0 and t == 0:
                    sum_item[g, :] = by_item
                else:
                    sum_item[g, :] = sum_item[g, :] + by_item
                by_user = jnp.exp2((piece + weight[g, :] - top) * (TEMP * LOG2E))
                part = jnp.sum(by_user.reshape(CHUNK // 8, 8, 128), axis=0)
                total = part if total is None else total + part
            total = jnp.sum(total, axis=0, keepdims=True)
            if not first:
                total = total + past_ref[1:2, place] * jnp.exp2((old_top - top) * (TEMP * LOG2E))
            if last:
                lse = top * TEMP + jnp.log(total)
                for peer in range(8):
                    tile = (y * 8 + peer) * 8
                    row_ref[tile + t : tile + t + 1, :] = lse
                    row_ref[tile + 4 + t : tile + 5 + t, :] = positive * TEMP
            else:
                row_ref[0:1, place] = top
                row_ref[1:2, place] = total
                row_ref[2:3, place] = positive
    for half in range(2):
        g = slice(128 * half, 128 * half + 128)
        total = jnp.broadcast_to(jnp.sum(sum_item[g, :], axis=1, keepdims=True), (128, 128))
        lse = top_item[g, :] * TEMP + jnp.log(total)
        item_ref[0:1, g] = lse.T[0:1, :]


def score_call(first, last, bases, items, users, past):
    vmem = pl.BlockSpec(memory_space=pltpu.VMEM)
    operands = (bases, items, users) + (() if first else (past,))
    row_shape = (32 * 8, 128) if last else (8, Y * USERS)
    return pl.pallas_call(
        functools.partial(score_kernel, first, last),
        out_shape=(
            jax.ShapeDtypeStruct((1, ITEMS), F32),
            jax.ShapeDtypeStruct(row_shape, F32),
        ),
        in_specs=[pl.BlockSpec(memory_space=pltpu.SMEM)] + [vmem] * (len(operands) - 1),
        out_specs=(vmem, vmem),
        scratch_shapes=[
            pltpu.VMEM((ITEMS, Y * USERS), F32),
            pltpu.VMEM((ITEMS, 128), F32),
            pltpu.VMEM((ITEMS, 128), F32),
            pltpu.VMEM((ITEMS, 128), F32),
            pltpu.VMEM((ITEMS, 128), F32),
        ],
        compiler_params=pltpu.CompilerParams(vmem_limit_bytes=24 * 1024 * 1024),
        cost_estimate=pl.CostEstimate(
            flops=2 * ITEMS * Y * USERS * DEPTH,
            bytes_accessed=4 * 1024 * 1024,
            transcendentals=2 * ITEMS * Y * USERS,
        ),
    )(*operands)


def join(*parts):
    top = functools.reduce(jnp.maximum, parts)
    return top + jnp.log(sum(jnp.exp(part - top) for part in parts))


def on_device(item_features, layer_one, layer_two, log_weight, user_vectors, positive_index):
    high = (positive_index // 256).astype(BF16)
    low = (positive_index % 256).astype(BF16)
    index_rows = jnp.pad(jnp.stack([high, low]), ((0, EXTRA - 2), (0, 0)))
    users = lax.all_gather(
        jnp.concatenate([user_vectors, index_rows], axis=0), "y", axis=0, tiled=True
    )

    hidden = jax.nn.relu(
        jnp.dot(item_features, layer_one, preferred_element_type=F32)
    ).astype(BF16)
    embedded = jnp.dot(hidden, layer_two, preferred_element_type=F32).astype(BF16)
    weight_high, weight_low = high_low(log_weight)

    def rows(values):
        return jnp.pad(values[None, :], ((0, 7), (0, DEPTH - values.shape[0])))

    sent = jnp.concatenate([embedded, rows(jnp.concatenate([weight_high, weight_low]))], axis=0)
    came = lax.ppermute(sent, ZC, across(1))
    weights = jnp.concatenate(
        [weight_high, came[BLOCK, 0:BLOCK], weight_low, came[BLOCK, BLOCK : 2 * BLOCK]]
    )
    near = jnp.concatenate([embedded, came[0:BLOCK], rows(weights)], axis=0)
    far = lax.ppermute(near, ZC, along(4))
    pair = jnp.concatenate(
        [near[: 2 * BLOCK], far[: 2 * BLOCK], near[2 * BLOCK :], far[2 * BLOCK :]], axis=0
    )

    zl, y, zh, x, c = (lax.axis_index(name) for name in AXES)
    z = zh * 16 + zl

    def base(place, core):
        place = place % RING
        item = ((place // 16) * 4 + x) * 2 + core
        return (item * 64 + (place % 16) * 4 + y) * BLOCK

    side = jnp.where(c == 0, -1, 1)
    columns, past = [], None
    for step in range(4):
        ahead = lax.ppermute(pair, ZC, along(1)) if step < 3 else None
        bases = jnp.stack(
            [
                base(z + side * (step + more + cross), jnp.where(cross == 0, c, 1 - c))
                for more in (0, 4)
                for cross in (0, 1)
            ]
        ).astype(jnp.int32)
        column, past = score_call(step == 0, step == 3, bases, pair, users, past)
        columns.append(column)
        pair = ahead

    stacked = jnp.concatenate(columns, axis=0)
    came4 = lax.ppermute(stacked[:, 128:], ZC, along(-4))
    four = join(stacked[:, :128], came4)
    came2 = lax.ppermute(four[2:], ZC, along(-2))
    two = join(four[:2], came2)
    one_away = lax.ppermute(two[1, :BLOCK], ZC, along(-1))
    cross_one = lax.ppermute(two[0, BLOCK:], ZC, across(1))
    cross_two = lax.ppermute(two[1, BLOCK:], ZC, across(2))

    plane = lax.all_to_all(past, PLANE, 0, 0, tiled=True).reshape(32, 8, 128)
    lse, positive = plane[:, :4], plane[:, 4:]
    top = jnp.max(lse, axis=0)
    lse = top + jnp.log(jnp.sum(jnp.exp(lse - top), axis=0))
    mine = jnp.concatenate([lse, jnp.sum(positive, axis=0)], axis=0)
    other = lax.ppermute(mine, "zh", [(0, 1), (1, 0)])
    row_loss = join(mine[:4], other[:4]) - (mine[4:] + other[4:])

    col_lse = join(two[0, :BLOCK], one_away, cross_one, cross_two)
    return row_loss.reshape(USERS), col_lse


def solution(mesh):
    fine = Mesh(mesh.devices.reshape(SIZES), AXES)
    by_item = ("zh", "x", "c", "zl", "y")
    by_user = ("zl", "y")
    placed = (P(by_item, None), P(), P(), P(by_item), P(by_user, None), P(by_user))
    return jax.shard_map(
        on_device,
        mesh=fine,
        in_specs=placed,
        out_specs=(P(by_user), P(by_item)),
        check_vma=False,
    )
```

time: 1750 us -> 148 us (0.08)
  blocking collectives: 1410 us -> 0 us
  waiting for transfers between devices: 295 us -> 26.3 us
  starting transfers between devices: 0.04 us -> 84.6 us
    all_gather x4 -> x0, blocking collectives: 877 us -> none  [the longest x2 707 us: combined_all(): lax.all_gather(part.astype(kind), axis)]
    unnamed x1 -> x0, blocking collectives: 381 us -> none
    all_gather x1, waiting for transfers between devices: 295 us -> 0.01 us  [on_device(): lax.all_gather(jnp.concatenate([user_vectors, index_rows], axis=0), 'y',...]
    psum x1 -> x0, blocking collectives: 155 us -> none  [on_device(): positive = lax.psum(row_positive, 'item')]
    ppermute x0 -> x11, starting transfers between devices: none -> 73.6 us  [the longest x1 19.3 us: on_device(): far = lax.ppermute(near, ZC, along(4))]
    ppermute x0 -> x11, waiting for transfers between devices: none -> 26.3 us  [the longest x1 7.64 us: on_device(): other = lax.ppermute(mine, 'zh', [(0, 1), (1, 0)])]
  transfers between devices with their start and end apart: 1 -> 13, of which waited for: 1 -> 6; matrix products, arithmetic and copies ran while one was open for 0% -> 4% of each run, Pallas kernels for 0% -> 4%
where the time goes in v1:
time: 148 us; the launch traced here: 146 us
  starting transfers between devices  84.6 us (57%)
  waiting for transfers between devices  26.3 us (18%)
  between operations  14.8 us (10%)
  Pallas kernels  8.73 us (6%)
  other arithmetic  5.19 us (4%)
  local copies, waits for them, and re-layouts  3.44 us (2%)
  matrix products  3.31 us (2%)
    ppermute x1, starting transfers between devices, on_device(): far = lax.ppermute(near, ZC, along(4))  19.3 us
    ppermute x1, starting transfers between devices, on_device(): other = lax.ppermute(mine, 'zh', [(0, 1), (1, 0)])  14.5 us
    ppermute x3, starting transfers between devices, on_device(): ahead = lax.ppermute(pair, ZC, along(1)) if step < 3 else None  13.6 us
    all_to_all x1, starting transfers between devices, on_device(): plane = lax.all_to_all(past, PLANE, 0, 0, tiled=True).reshape(32, 8, 128)  11 us
    pallas_call x4, Pallas kernels, score_call(): pl.pallas_call(functools.partial(score_kernel, first, last), out_shape=(j...  8.73 us
    ppermute x1, waiting for transfers between devices, on_device(): other = lax.ppermute(mine, 'zh', [(0, 1), (1, 0)])  7.64 us
    ppermute x1, starting transfers between devices, on_device(): came4 = lax.ppermute(stacked[:, 128:], ZC, along(-4))  7.21 us
    ppermute x3, waiting for transfers between devices, on_device(): ahead = lax.ppermute(pair, ZC, along(1)) if step < 3 else None  7 us
  transfers between devices with their start and end apart: 13, of which 6 were waited for; matrix products, arithmetic and copies ran while one was open for 4% of the time, Pallas kernels for 4%

profile of v1, /device:TPU:1, one launch (start us, length us, event | category | flops | bytes accessed | tf_op | source)
XLA Modules:
  0.0 146.4 jit_solution(6997115407101751994)
XLA Ops:
  7.2 0.8 fusion.9
  8.0 1.9 %pad_maximum_fusion = bf16[528,512]{1,0:T(8,128)(2,1)} fusion(bf16[16,512]{1,0:T(8,128)(2,1)S(1)} %fusion.8, bf16[512,512]{1,0:T(8,128)(2,1)} %param.10), kind=kLoop, calls=%fused_computation.4 | loop fusion | flops 1081344 | bytes 1081344 | tf_op jit(solution)/shard_map/concatenate | solution.py:185
  9.9 0.7 fusion.22
  10.8 3.3 %constant_dynamic-update-slice_fusion.3 = (bf16[272,512]{1,0:T(8,128)(2,1)S(1)}, bf16[64,512]{1,0:T(8,128)(2,1)S(1)}) fusion(bf16[1024,512]{1,0:T(8,128)(2,1)S(1)} %copy-done, bf16[64,2048]{1,0:T(8,128)(2,1)} %param.6, bf16[2048,1024]{1,0:T(8,128)(2,1)} %param.7), kind=kOutput, calls=%fused_computation.21 | convolution fusion | flops 335708160 | bytes 5636096 | tf_op jit(solution)/shard_map/dot_general | solution.py:191
  14.1 4.9 %collective-permute-start = (bf16[72,512]{1,0:T(8,128)(2,1)S(1)}, bf16[72,512]{1,0:T(8,128)(2,1)S(1)}, u32[]{:S(2)}, u32[]{:S(2)}) collective-permute-start(bf16[72,512]{1,0:T(8,128)(2,1)S(1)} %fusion.5), channel_id=1, source_target_pairs={{0,969},{1,64},{64,1},{65,128},{128,65},{129,192},{192,129},{193,2... | collective-permute-start | bytes 221192 | tf_op jit(solution)/shard_map/ppermute | solution.py:198
  19.0 2.0 %collective-permute-done = bf16[72,512]{1,0:T(8,128)(2,1)S(1)} collective-permute-done((bf16[72,512]{1,0:T(8,128)(2,1)S(1)}, bf16[72,512]{1,0:T(8,128)(2,1)S(1)}, u32[]{:S(2)}, u32[]{:S(2)}) %collective-permute-start) | collective-permute-done | bytes 73760 | tf_op jit(solution)/shard_map/ppermute | solution.py:198
  21.3 19.3 %collective-permute-start.1 = (bf16[136,512]{1,0:T(8,128)(2,1)S(1)}, bf16[136,512]{1,0:T(8,128)(2,1)S(1)}, u32[]{:S(2)}, u32[]{:S(2)}) collective-permute-start(bf16[136,512]{1,0:T(8,128)(2,1)S(1)} %pad_maximum_fusion.1), channel_id=1, source_target_pairs={{0,256},{1,777},{64,320},{65,841},{128,384},{129,905},{192,448},{1... | collective-permute-start | bytes 417800 | tf_op jit(solution)/shard_map/ppermute | solution.py:203
  40.5 6.5 %collective-permute-done.1 = bf16[136,512]{1,0:T(8,128)(2,1)S(1)} collective-permute-done((bf16[136,512]{1,0:T(8,128)(2,1)S(1)}, bf16[136,512]{1,0:T(8,128)(2,1)S(1)}, u32[]{:S(2)}, u32[]{:S(2)}) %collective-permute-start.1) | collective-permute-done | bytes 139296 | tf_op jit(solution)/shard_map/ppermute | solution.py:203
  47.0 3.5 %collective-permute-start.2 = (bf16[272,512]{1,0:T(8,128)(2,1)S(1)}, bf16[272,512]{1,0:T(8,128)(2,1)S(1)}, u32[]{:S(2)}, u32[]{:S(2)}) collective-permute-start(bf16[272,512]{1,0:T(8,128)(2,1)S(1)} %constant_dynamic-update-slice_fusion.items_ref), channel_id=1, source_target_pairs={{0,64},{1,969},{64,128},{65,1},{128,192},{129,65},{192,256},{193,1... | collective-permute-start | bytes 835592 | tf_op jit(solution)/shard_map/ppermute | solution.py:219
  50.5 4.2 %collective-permute-done.2.items_ref = bf16[272,512]{1,0:T(8,128)(2,1)S(1)} collective-permute-done((bf16[272,512]{1,0:T(8,128)(2,1)S(1)}, bf16[272,512]{1,0:T(8,128)(2,1)S(1)}, u32[]{:S(2)}, u32[]{:S(2)}) %collective-permute-start.2) | collective-permute-done | bytes 278560 | tf_op jit(solution)/shard_map/ppermute | solution.py:219
  54.7 4.7 %collective-permute-start.3 = (bf16[272,512]{1,0:T(8,128)(2,1)S(1)}, bf16[272,512]{1,0:T(8,128)(2,1)S(1)}, u32[]{:S(2)}, u32[]{:S(2)}) collective-permute-start(bf16[272,512]{1,0:T(8,128)(2,1)S(1)} %collective-permute-done.2.items_ref), channel_id=1, source_target_pairs={{0,64},{1,969},{64,128},{65,1},{128,192},{129,65},{192,256},{193,1... | collective-permute-start | bytes 835592 | tf_op jit(solution)/shard_map/ppermute | solution.py:219
  59.9 0.1 pad_add_fusion.3.base_ref
  60.1 2.8 %collective-permute-done.3.items_ref = bf16[272,512]{1,0:T(8,128)(2,1)S(1)} collective-permute-done((bf16[272,512]{1,0:T(8,128)(2,1)S(1)}, bf16[272,512]{1,0:T(8,128)(2,1)S(1)}, u32[]{:S(2)}, u32[]{:S(2)}) %collective-permute-start.3) | collective-permute-done | bytes 278560 | tf_op jit(solution)/shard_map/ppermute | solution.py:219
  62.9 5.4 %collective-permute-start.4 = (bf16[272,512]{1,0:T(8,128)(2,1)S(1)}, bf16[272,512]{1,0:T(8,128)(2,1)S(1)}, u32[]{:S(2)}, u32[]{:S(2)}) collective-permute-start(bf16[272,512]{1,0:T(8,128)(2,1)S(1)} %collective-permute-done.3.items_ref), channel_id=1, source_target_pairs={{0,64},{1,969},{64,128},{65,1},{128,192},{129,65},{192,256},{193,1... | collective-permute-start | bytes 835592 | tf_op jit(solution)/shard_map/ppermute | solution.py:219
  68.3 0.1 pad_add_fusion.1.base_ref
  68.5 1.6 %copy-done.1 = bf16[2112,512]{1,0:T(8,128)(2,1)S(1)} copy-done((bf16[2112,512]{1,0:T(8,128)(2,1)S(1)}, bf16[2112,512]{1,0:T(8,128)(2,1)}, u32[]{:S(2)}) %copy-start.1) | copy-done | bytes 2162712
  70.1 2.0 %shard_map.77 = (f32[1,256]{1,0:T(1,128)S(1)}, f32[8,2048]{1,0:T(8,128)S(1)}) custom-call(s32[4]{0:T(128)S(1)} %pad_add_fusion.3.base_ref, bf16[272,512]{1,0:T(8,128)(2,1)S(1)} %constant_dynamic-update-slice_fusion.items_ref, bf16[2112,512]{1,0:T(8,128)(2,1)S(1)} %copy-done.1), custom_call_target="tpu_custom_call" | custom-call | flops 536870912 | bytes 4194304 | tf_op jit(solution)/shard_map/pallas_call | solution.py:151
  72.1 1.6 %copy-done.2 = bf16[2112,512]{1,0:T(8,128)(2,1)S(1)} copy-done((bf16[2112,512]{1,0:T(8,128)(2,1)S(1)}, bf16[2112,512]{1,0:T(8,128)(2,1)}, u32[]{:S(2)}) %copy-start.2) | copy-done | bytes 2162712
  73.7 2.0 %shard_map.78 = (f32[1,256]{1,0:T(1,128)S(1)}, f32[8,2048]{1,0:T(8,128)S(1)}) custom-call(s32[4]{0:T(128)S(1)} %pad_add_fusion.2.base_ref, bf16[272,512]{1,0:T(8,128)(2,1)S(1)} %collective-permute-done.2.items_ref, bf16[2112,512]{1,0:T(8,128)(2,1)S(1)} %copy-done.2, f32[8,2048]{1,0:T(8,128)S(1)} %get-tuple-element.10.refs_0_), custom_call_target="tpu_custom_call" | custom-call | flops 536870912 | bytes 4194304 | tf_op jit(solution)/shard_map/pallas_call | solution.py:151
  75.8 2.0 %shard_map.79 = (f32[1,256]{1,0:T(1,128)S(1)}, f32[8,2048]{1,0:T(8,128)S(1)}) custom-call(s32[4]{0:T(128)S(1)} %pad_add_fusion.1.base_ref, bf16[272,512]{1,0:T(8,128)(2,1)S(1)} %collective-permute-done.3.items_ref, bf16[2112,512]{1,0:T(8,128)(2,1)S(1)} %copy-done.2, f32[8,2048]{1,0:T(8,128)S(1)} %get-tuple-element.11.refs_0_), custom_call_target="tpu_custom_call" | custom-call | flops 536870912 | bytes 4194304 | tf_op jit(solution)/shard_map/pallas_call | solution.py:151
  77.8 2.7 %shard_map.80 = (f32[1,256]{1,0:T(1,128)S(1)}, f32[256,128]{1,0:T(8,128)}) custom-call(s32[4]{0:T(128)S(1)} %pad_add_fusion.base_ref, bf16[272,512]{1,0:T(8,128)(2,1)S(1)} %collective-permute-done.4.items_ref, bf16[2112,512]{1,0:T(8,128)(2,1)S(1)} %copy-done.2, f32[8,2048]{1,0:T(8,128)S(1)} %get-tuple-element.12.refs_0_), custom_call_target="tpu_custom_call" | custom-call | flops 536870912 | bytes 4194304 | tf_op jit(solution)/shard_map/pallas_call | solution.py:151
  80.5 7.2 %collective-permute-start.6 = (f32[4,128]{1,0:T(4,128)S(1)}, f32[4,128]{1,0:T(4,128)S(1)}, u32[]{:S(2)}, u32[]{:S(2)}) collective-permute-start(f32[4,128]{1,0:T(4,128)S(1)} %slice.78), channel_id=1, source_target_pairs={{0,776},{1,257},{64,840},{65,321},{128,904},{129,385},{192,968},{1... | collective-permute-start | bytes 6152 | tf_op jit(solution)/shard_map/ppermute | solution.py:232
  87.7 3.2 %collective-permute-done.6 = f32[4,128]{1,0:T(4,128)S(1)} collective-permute-done((f32[4,128]{1,0:T(4,128)S(1)}, f32[4,128]{1,0:T(4,128)S(1)}, u32[]{:S(2)}, u32[]{:S(2)}) %collective-permute-start.6) | collective-permute-done | bytes 2080 | tf_op jit(solution)/shard_map/ppermute | solution.py:232
  90.9 2.4 %collective-permute-start.7 = (f32[2,128]{1,0:T(2,128)S(1)}, f32[2,128]{1,0:T(2,128)S(1)}, u32[]{:S(2)}, u32[]{:S(2)}) collective-permute-start(f32[2,128]{1,0:T(2,128)S(1)} %slice.65), channel_id=1, source_target_pairs={{0,904},{1,129},{64,968},{65,193},{128,0},{129,257},{192,64},{193,... | collective-permute-start | bytes 3080 | tf_op jit(solution)/shard_map/ppermute | solution.py:234
  93.3 11.0 %all-to-all-start = ((f32[32,8,128]{2,1,0:T(8,128)}), f32[32,8,128]{2,1,0:T(8,128)S(1)}, u32[]{:S(2)}, u32[]{:S(2)}) async-start(f32[32,8,128]{2,1,0:T(8,128)} %bitcast.19), calls=%async_computation | async-start | bytes 262144 | tf_op jit(solution)/shard_map/all_to_all | solution.py:240
  104.4 2.2 %collective-permute-start.10 = (f32[64]{0:T(128)S(1)}, f32[64]{0:T(128)S(1)}, u32[]{:S(2)}, u32[]{:S(2)}) collective-permute-start(f32[64]{0:T(128)S(1)} %get-tuple-element.27), channel_id=1, source_target_pairs={{0,905},{1,128},{64,969},{65,192},{128,1},{129,256},{192,65},{193,... | collective-permute-start | bytes 776 | tf_op jit(solution)/shard_map/ppermute | solution.py:238
  106.6 3.6 %collective-permute-start.8 = (f32[64]{0:T(128)S(1)}, f32[64]{0:T(128)S(1)}, u32[]{:S(2)}, u32[]{:S(2)}) collective-permute-start(f32[64]{0:T(128)S(1)} %get-tuple-element.26), channel_id=1, source_target_pairs={{0,968},{1,65},{64,0},{65,129},{128,64},{129,193},{192,128},{193,2... | collective-permute-start | bytes 776 | tf_op jit(solution)/shard_map/ppermute | solution.py:236
  110.2 6.0 %collective-permute-start.9 = (f32[64]{0:T(128)S(1)}, f32[64]{0:T(128)S(1)}, u32[]{:S(2)}, u32[]{:S(2)}) collective-permute-start(f32[64]{0:T(128)S(1)} %get-tuple-element.28), channel_id=1, source_target_pairs={{0,969},{1,64},{64,1},{65,128},{128,65},{129,192},{192,129},{193,2... | collective-permute-start | bytes 776 | tf_op jit(solution)/shard_map/ppermute | solution.py:237
  116.3 14.5 %collective-permute-start.5 = (f32[8,128]{1,0:T(8,128)S(1)}, f32[8,128]{1,0:T(8,128)S(1)}, u32[]{:S(2)}, u32[]{:S(2)}) collective-permute-start(f32[8,128]{1,0:T(8,128)S(1)} %pad_maximum_fusion.2), channel_id=1, source_target_pairs={{0,8},{8,0},{1,9},{9,1},{2,10},{10,2},{3,11},{11,3},{4,12},{12,4},... | collective-permute-start | bytes 12296 | tf_op jit(solution)/shard_map/ppermute | solution.py:245
  130.8 0.5 log_add_fusion.3
  131.3 7.6 %collective-permute-done.5 = f32[8,128]{1,0:T(8,128)S(1)} collective-permute-done((f32[8,128]{1,0:T(8,128)S(1)}, f32[8,128]{1,0:T(8,128)S(1)}, u32[]{:S(2)}, u32[]{:S(2)}) %collective-permute-start.5) | collective-permute-done | bytes 4128 | tf_op jit(solution)/shard_map/ppermute | solution.py:245
  139.0 0.6 subtract_bitcast_fusion
  (39 shorter events, 0.8 us)
Async XLA Ops:
  7.2 3.6 %copy-start = (bf16[1024,512]{1,0:T(8,128)(2,1)S(1)}, bf16[1024,512]{1,0:T(8,128)(2,1)}, u32[]{:S(2)}) copy-start(bf16[1024,512]{1,0:T(8,128)(2,1)} %param.8) | copy-start | bytes 3145732
  7.2 61.3 %all-gather.2.cloned.1.call-start = ((), (), s32[]{:S(2)}) async-start(), calls=%async_computation.1 | async-start | bytes 2703360 | tf_op jit(solution)/shard_map/all_gather | solution.py:184
  14.1 7.0 %collective-permute-start = (bf16[72,512]{1,0:T(8,128)(2,1)S(1)}, bf16[72,512]{1,0:T(8,128)(2,1)S(1)}, u32[]{:S(2)}, u32[]{:S(2)}) collective-permute-start(bf16[72,512]{1,0:T(8,128)(2,1)S(1)} %fusion.5), channel_id=1, source_target_pairs={{0,969},{1,64},{64,1},{65,128},{128,65},{129,192},{192,129},{193,2... | collective-permute-start | bytes 221192 | tf_op jit(solution)/shard_map/ppermute | solution.py:198
  21.3 25.7 %collective-permute-start.1 = (bf16[136,512]{1,0:T(8,128)(2,1)S(1)}, bf16[136,512]{1,0:T(8,128)(2,1)S(1)}, u32[]{:S(2)}, u32[]{:S(2)}) collective-permute-start(bf16[136,512]{1,0:T(8,128)(2,1)S(1)} %pad_maximum_fusion.1), channel_id=1, source_target_pairs={{0,256},{1,777},{64,320},{65,841},{128,384},{129,905},{192,448},{1... | collective-permute-start | bytes 417800 | tf_op jit(solution)/shard_map/ppermute | solution.py:203
  47.0 7.7 %collective-permute-start.2 = (bf16[272,512]{1,0:T(8,128)(2,1)S(1)}, bf16[272,512]{1,0:T(8,128)(2,1)S(1)}, u32[]{:S(2)}, u32[]{:S(2)}) collective-permute-start(bf16[272,512]{1,0:T(8,128)(2,1)S(1)} %constant_dynamic-update-slice_fusion.items_ref), channel_id=1, source_target_pairs={{0,64},{1,969},{64,128},{65,1},{128,192},{129,65},{192,256},{193,1... | collective-permute-start | bytes 835592 | tf_op jit(solution)/shard_map/ppermute | solution.py:219
  54.7 8.2 %collective-permute-start.3 = (bf16[272,512]{1,0:T(8,128)(2,1)S(1)}, bf16[272,512]{1,0:T(8,128)(2,1)S(1)}, u32[]{:S(2)}, u32[]{:S(2)}) collective-permute-start(bf16[272,512]{1,0:T(8,128)(2,1)S(1)} %collective-permute-done.2.items_ref), channel_id=1, source_target_pairs={{0,64},{1,969},{64,128},{65,1},{128,192},{129,65},{192,256},{193,1... | collective-permute-start | bytes 835592 | tf_op jit(solution)/shard_map/ppermute | solution.py:219
  62.9 14.9 %collective-permute-start.4 = (bf16[272,512]{1,0:T(8,128)(2,1)S(1)}, bf16[272,512]{1,0:T(8,128)(2,1)S(1)}, u32[]{:S(2)}, u32[]{:S(2)}) collective-permute-start(bf16[272,512]{1,0:T(8,128)(2,1)S(1)} %collective-permute-done.3.items_ref), channel_id=1, source_target_pairs={{0,64},{1,969},{64,128},{65,1},{128,192},{129,65},{192,256},{193,1... | collective-permute-start | bytes 835592 | tf_op jit(solution)/shard_map/ppermute | solution.py:219
  68.5 1.6 %copy-start.1 = (bf16[2112,512]{1,0:T(8,128)(2,1)S(1)}, bf16[2112,512]{1,0:T(8,128)(2,1)}, u32[]{:S(2)}) copy-start(bf16[2112,512]{1,0:T(8,128)(2,1)} %all-gather.2.cloned.1.call-done.users_ref) | copy-start | bytes 6488068
  72.1 1.6 %copy-start.2 = (bf16[2112,512]{1,0:T(8,128)(2,1)S(1)}, bf16[2112,512]{1,0:T(8,128)(2,1)}, u32[]{:S(2)}) copy-start(bf16[2112,512]{1,0:T(8,128)(2,1)} %all-gather.2.cloned.1.call-done.users_ref) | copy-start | bytes 6488068
  80.5 10.4 %collective-permute-start.6 = (f32[4,128]{1,0:T(4,128)S(1)}, f32[4,128]{1,0:T(4,128)S(1)}, u32[]{:S(2)}, u32[]{:S(2)}) collective-permute-start(f32[4,128]{1,0:T(4,128)S(1)} %slice.78), channel_id=1, source_target_pairs={{0,776},{1,257},{64,840},{65,321},{128,904},{129,385},{192,968},{1... | collective-permute-start | bytes 6152 | tf_op jit(solution)/shard_map/ppermute | solution.py:232
  90.9 13.4 %collective-permute-start.7 = (f32[2,128]{1,0:T(2,128)S(1)}, f32[2,128]{1,0:T(2,128)S(1)}, u32[]{:S(2)}, u32[]{:S(2)}) collective-permute-start(f32[2,128]{1,0:T(2,128)S(1)} %slice.65), channel_id=1, source_target_pairs={{0,904},{1,129},{64,968},{65,193},{128,0},{129,257},{192,64},{193,... | collective-permute-start | bytes 3080 | tf_op jit(solution)/shard_map/ppermute | solution.py:234
  93.3 22.9 %all-to-all-start = ((f32[32,8,128]{2,1,0:T(8,128)}), f32[32,8,128]{2,1,0:T(8,128)S(1)}, u32[]{:S(2)}, u32[]{:S(2)}) async-start(f32[32,8,128]{2,1,0:T(8,128)} %bitcast.19), calls=%async_computation | async-start | bytes 262144 | tf_op jit(solution)/shard_map/all_to_all | solution.py:240
  104.4 26.4 %collective-permute-start.10 = (f32[64]{0:T(128)S(1)}, f32[64]{0:T(128)S(1)}, u32[]{:S(2)}, u32[]{:S(2)}) collective-permute-start(f32[64]{0:T(128)S(1)} %get-tuple-element.27), channel_id=1, source_target_pairs={{0,905},{1,128},{64,969},{65,192},{128,1},{129,256},{192,65},{193,... | collective-permute-start | bytes 776 | tf_op jit(solution)/shard_map/ppermute | solution.py:238
  106.6 24.2 %collective-permute-start.8 = (f32[64]{0:T(128)S(1)}, f32[64]{0:T(128)S(1)}, u32[]{:S(2)}, u32[]{:S(2)}) collective-permute-start(f32[64]{0:T(128)S(1)} %get-tuple-element.26), channel_id=1, source_target_pairs={{0,968},{1,65},{64,0},{65,129},{128,64},{129,193},{192,128},{193,2... | collective-permute-start | bytes 776 | tf_op jit(solution)/shard_map/ppermute | solution.py:236
  110.2 20.6 %collective-permute-start.9 = (f32[64]{0:T(128)S(1)}, f32[64]{0:T(128)S(1)}, u32[]{:S(2)}, u32[]{:S(2)}) collective-permute-start(f32[64]{0:T(128)S(1)} %get-tuple-element.28), channel_id=1, source_target_pairs={{0,969},{1,64},{64,1},{65,128},{128,65},{129,192},{192,129},{193,2... | collective-permute-start | bytes 776 | tf_op jit(solution)/shard_map/ppermute | solution.py:237
  116.3 22.7 %collective-permute-start.5 = (f32[8,128]{1,0:T(8,128)S(1)}, f32[8,128]{1,0:T(8,128)S(1)}, u32[]{:S(2)}, u32[]{:S(2)}) collective-permute-start(f32[8,128]{1,0:T(8,128)S(1)} %pad_maximum_fusion.2), channel_id=1, source_target_pairs={{0,8},{8,0},{1,9},{9,1},{2,10},{10,2},{3,11},{11,3},{4,12},{12,4},... | collective-permute-start | bytes 12296 | tf_op jit(solution)/shard_map/ppermute | solution.py:245
Sparse Core Ops, SparseCore 0:
  10.7 57.6 all-gather.1

commit v2 on v1

--- a/solution.py
+++ b/solution.py
@@ -20,6 +20,7 @@
 Y = 4
 DEPTH = 512
 ITEMS = 256
+HALF = ITEMS // 2
 EXTRA = 16
 TEMP = 4.0 / math.sqrt(DEPTH)
 LOG2E = 1.0 / math.log(2.0)
@@ -52,32 +53,35 @@
     return high, (values - high.astype(F32)).astype(BF16)
 
 
-def score_kernel(first, last, base_ref, items_ref, users_ref, *refs):
+def score_kernel(first, last, base_ref, items_ref, *refs):
+    users_refs, refs = refs[:Y], refs[Y:]
     if first:
         item_ref, row_ref, scores, weight, ids, top_item, sum_item = refs
     else:
         past_ref, item_ref, row_ref, scores, weight, ids, top_item, sum_item = refs
-    extra = items_ref[ITEMS : ITEMS + EXTRA, 0:256].astype(F32)
-    packed = (extra[:, 0:128] + extra[:, 128:256]) * (1.0 / TEMP)
     for half in range(2):
-        row = packed[8 * half : 8 * half + 1, :]
-        weight[128 * half : 128 * half + 128, :] = jnp.broadcast_to(row, (128, 128)).T
+        start = half * (HALF + EXTRA) + HALF
+        extra = items_ref[start : start + EXTRA, 0:256].astype(F32)
+        row = (extra[0:1, 0:128] + extra[0:1, 128:256]) * (1.0 / TEMP)
+        weight[HALF * half : HALF * (half + 1), :] = jnp.broadcast_to(row, (HALF, 128)).T
     spot = lax.broadcasted_iota(jnp.int32, (BLOCK, 128), 0)
     for part in range(ITEMS // BLOCK):
         ids[part * BLOCK : (part + 1) * BLOCK, :] = (spot + base_ref[part]).astype(F32)
 
     chunks = [slice(g, g + CHUNK) for g in range(0, ITEMS, CHUNK)]
     tiles = [slice(k, k + 128) for k in range(0, USERS, 128)]
+    items = jnp.concatenate(
+        [items_ref[0:HALF, :], items_ref[HALF + EXTRA : 2 * HALF + EXTRA, :]], axis=0
+    )
     tops, positives = [], []
     for y in range(Y):
-        start = y * (USERS + EXTRA)
         raw = lax.dot_general(
-            items_ref[0:ITEMS, :],
-            users_ref[start : start + USERS, :],
+            items,
+            users_refs[y][0:USERS, :],
             (((1,), (1,)), ((), ())),
             preferred_element_type=F32,
         )
-        index_rows = users_ref[start + USERS : start + USERS + EXTRA, :].astype(F32)
+        index_rows = users_refs[y][USERS : USERS + EXTRA, :].astype(F32)
         wanted = index_rows[0:1, :] * 256.0 + index_rows[1:2, :]
         top_y, positive_y = [], []
         for k in tiles:
@@ -106,6 +110,7 @@
             jnp.max(top_item[g, :], axis=1, keepdims=True), (CHUNK, 128)
         )
     for y in range(Y):
+        ready = []
         for t, k in enumerate(tiles):
             place = slice(y * USERS + k.start, y * USERS + k.stop)
             top, positive = tops[y][t], positives[y][t]
@@ -129,14 +134,16 @@
                 total = total + past_ref[1:2, place] * jnp.exp2((old_top - top) * (TEMP * LOG2E))
             if last:
                 lse = top * TEMP + jnp.log(total)
-                for peer in range(8):
-                    tile = (y * 8 + peer) * 8
-                    row_ref[tile + t : tile + t + 1, :] = lse
-                    row_ref[tile + 4 + t : tile + 5 + t, :] = positive * TEMP
+                ready.append((lse, positive * TEMP))
             else:
                 row_ref[0:1, place] = top
                 row_ref[1:2, place] = total
                 row_ref[2:3, place] = positive
+        if last:
+            tile = jnp.concatenate([lse for lse, _ in ready] + [pos for _, pos in ready], axis=0)
+            block = (base_ref[4] + y) % Y
+            for peer in range(8):
+                row_ref[pl.ds(pl.multiple_of((block * 8 + peer) * 8, 8), 8), :] = tile
     for half in range(2):
         g = slice(128 * half, 128 * half + 128)
         total = jnp.broadcast_to(jnp.sum(sum_item[g, :], axis=1, keepdims=True), (128, 128))
@@ -146,7 +153,7 @@
 
 def score_call(first, last, bases, items, users, past):
     vmem = pl.BlockSpec(memory_space=pltpu.VMEM)
-    operands = (bases, items, users) + (() if first else (past,))
+    operands = (bases, items, *users) + (() if first else (past,))
     row_shape = (32 * 8, 128) if last else (8, Y * USERS)
     return pl.pallas_call(
         functools.partial(score_kernel, first, last),
@@ -172,38 +179,59 @@
     )(*operands)
 
 
+def stack_kernel(near_ref, far_ref, pair_ref):
+    pair_ref[0 : HALF + EXTRA, :] = near_ref[...]
+    pair_ref[HALF + EXTRA :, :] = far_ref[...]
+
+
+def stack_call(near, far):
+    vmem = pl.BlockSpec(memory_space=pltpu.VMEM)
+    return pl.pallas_call(
+        stack_kernel,
+        out_shape=jax.ShapeDtypeStruct((2 * (HALF + EXTRA), DEPTH), BF16),
+        in_specs=[vmem, vmem],
+        out_specs=vmem,
+        cost_estimate=pl.CostEstimate(flops=60 * 10**9, bytes_accessed=600_000, transcendentals=0),
+    )(near, far)
+
+
 def join(*parts):
     top = functools.reduce(jnp.maximum, parts)
     return top + jnp.log(sum(jnp.exp(part - top) for part in parts))
 
 
 def on_device(item_features, layer_one, layer_two, log_weight, user_vectors, positive_index):
-    high = (positive_index // 256).astype(BF16)
-    low = (positive_index % 256).astype(BF16)
-    index_rows = jnp.pad(jnp.stack([high, low]), ((0, EXTRA - 2), (0, 0)))
-    users = lax.all_gather(
-        jnp.concatenate([user_vectors, index_rows], axis=0), "y", axis=0, tiled=True
-    )
-
     hidden = jax.nn.relu(
         jnp.dot(item_features, layer_one, preferred_element_type=F32)
     ).astype(BF16)
     embedded = jnp.dot(hidden, layer_two, preferred_element_type=F32).astype(BF16)
     weight_high, weight_low = high_low(log_weight)
 
-    def rows(values):
-        return jnp.pad(values[None, :], ((0, 7), (0, DEPTH - values.shape[0])))
-
-    sent = jnp.concatenate([embedded, rows(jnp.concatenate([weight_high, weight_low]))], axis=0)
+    def rows(values, count):
+        return jnp.pad(values[None, :], ((0, count - 1), (0, DEPTH - values.shape[0])))
+
+    sent = jnp.concatenate(
+        [embedded, rows(jnp.concatenate([weight_high, weight_low]), 8)], axis=0
+    )
     came = lax.ppermute(sent, ZC, across(1))
     weights = jnp.concatenate(
         [weight_high, came[BLOCK, 0:BLOCK], weight_low, came[BLOCK, BLOCK : 2 * BLOCK]]
     )
-    near = jnp.concatenate([embedded, came[0:BLOCK], rows(weights)], axis=0)
+    near = jnp.concatenate([embedded, came[0:BLOCK], rows(weights, EXTRA)], axis=0)
+
+    high = (positive_index // 256).astype(BF16)
+    low = (positive_index % 256).astype(BF16)
+    index_rows = jnp.pad(jnp.stack([high, low]), ((0, EXTRA - 2), (0, 0)))
+    own = jnp.concatenate([user_vectors, index_rows], axis=0)
+
     far = lax.ppermute(near, ZC, along(4))
-    pair = jnp.concatenate(
-        [near[: 2 * BLOCK], far[: 2 * BLOCK], near[2 * BLOCK :], far[2 * BLOCK :]], axis=0
-    )
+    own, near = lax.optimization_barrier((own, near))
+    users = [own] + [
+        lax.ppermute(own, "y", [(k, (k - r) % Y) for k in range(Y)]) for r in (1, 3, 2)
+    ]
+    users = [users[0], users[1], users[3], users[2]]
+    pair = stack_call(near, far)
+    pairs = [pair] + [lax.ppermute(pair, ZC, along(step)) for step in (1, 2, 3)]
 
     zl, y, zh, x, c = (lax.axis_index(name) for name in AXES)
     z = zh * 16 + zl
@@ -216,35 +244,35 @@
     side = jnp.where(c == 0, -1, 1)
     columns, past = [], None
     for step in range(4):
-        ahead = lax.ppermute(pair, ZC, along(1)) if step < 3 else None
         bases = jnp.stack(
             [
                 base(z + side * (step + more + cross), jnp.where(cross == 0, c, 1 - c))
                 for more in (0, 4)
                 for cross in (0, 1)
             ]
+            + [y]
         ).astype(jnp.int32)
-        column, past = score_call(step == 0, step == 3, bases, pair, users, past)
+        column, past = score_call(step == 0, step == 3, bases, pairs[step], users, past)
         columns.append(column)
-        pair = ahead
 
     stacked = jnp.concatenate(columns, axis=0)
-    came4 = lax.ppermute(stacked[:, 128:], ZC, along(-4))
-    four = join(stacked[:, :128], came4)
+    plane = lax.all_to_all(past, PLANE, 0, 0, tiled=True).reshape(32, 8, 128)
+    came4 = lax.ppermute(stacked[:, HALF:], ZC, along(-4))
+
+    lse, positive = plane[:, :4], plane[:, 4:]
+    top = jnp.max(lse, axis=0)
+    lse = top + jnp.log(jnp.sum(jnp.exp(lse - top), axis=0))
+    mine = jnp.concatenate([lse, jnp.sum(positive, axis=0)], axis=0)
+    came4, mine = lax.optimization_barrier((came4, mine))
+    four = join(stacked[:, :HALF], came4)
+    other = lax.ppermute(mine, "zh", [(0, 1), (1, 0)])
     came2 = lax.ppermute(four[2:], ZC, along(-2))
     two = join(four[:2], came2)
     one_away = lax.ppermute(two[1, :BLOCK], ZC, along(-1))
     cross_one = lax.ppermute(two[0, BLOCK:], ZC, across(1))
     cross_two = lax.ppermute(two[1, BLOCK:], ZC, across(2))
-
-    plane = lax.all_to_all(past, PLANE, 0, 0, tiled=True).reshape(32, 8, 128)
-    lse, positive = plane[:, :4], plane[:, 4:]
-    top = jnp.max(lse, axis=0)
-    lse = top + jnp.log(jnp.sum(jnp.exp(lse - top), axis=0))
-    mine = jnp.concatenate([lse, jnp.sum(positive, axis=0)], axis=0)
-    other = lax.ppermute(mine, "zh", [(0, 1), (1, 0)])
     row_loss = join(mine[:4], other[:4]) - (mine[4:] + other[4:])
-
+    one_away, row_loss = lax.optimization_barrier((one_away, row_loss))
     col_lse = join(two[0, :BLOCK], one_away, cross_one, cross_two)
     return row_loss.reshape(USERS), col_lse
 

time: 148 us -> 126 us (0.85)
  between operations: 14.8 us -> 1.55 us
  waiting for transfers between devices: 26.3 us -> 20.9 us
  other arithmetic: 5.19 us -> 2.32 us
  Pallas kernels: 8.73 us -> 10.4 us
    ppermute x1, waiting for transfers between devices: 7.64 us -> 0.01 us  [on_device(): other = lax.ppermute(mine, 'zh', [(0, 1), (1, 0)])]
    ppermute x1, waiting for transfers between devices: 6.45 us -> 0.01 us  [on_device(): far = lax.ppermute(near, ZC, along(4))]
    all_to_all x1, waiting for transfers between devices: 0.01 us -> 5.67 us  [on_device(): plane = lax.all_to_all(past, PLANE, 0, 0, tiled=True).reshape(32, 8, 128)]
    ppermute x1, starting transfers between devices: 5.98 us -> 2.15 us  [on_device(): cross_one = lax.ppermute(two[0, BLOCK:], ZC, across(1))]
    ppermute x1, starting transfers between devices: 2.17 us -> 5.77 us  [on_device(): cross_two = lax.ppermute(two[1, BLOCK:], ZC, across(2))]
    all_to_all x1, starting transfers between devices: 11 us -> 8.02 us  [on_device(): plane = lax.all_to_all(past, PLANE, 0, 0, tiled=True).reshape(32, 8, 128)]
    ppermute x4 -> x7, starting transfers between devices: 20.8 us -> 23.4 us  [the longest x3 12 us: on_device(): pairs = [pair] + [lax.ppermute(pair, ZC, along(step)) for step in (1, 2, 3)]]
    ppermute x4 -> x7, waiting for transfers between devices: 10.2 us -> 12.7 us  [the longest x3 7.71 us: on_device(): lax.ppermute(own, 'y', [(k, (k - r) % Y) for k in range(Y)])]
  transfers between devices with their start and end apart: 13 -> 15, of which waited for: 6 -> 7; matrix products, arithmetic and copies ran while one was open for 4% -> 1% of each run, Pallas kernels for 4% -> 7%
where the time goes in v2:
time: 126 us; the launch traced here: 125 us
  starting transfers between devices  83.8 us (67%)
  waiting for transfers between devices  20.9 us (17%)
  Pallas kernels  10.4 us (8%)
  matrix products  3.3 us (3%)
  local copies, waits for them, and re-layouts  2.5 us (2%)
  other arithmetic  2.32 us (2%)
  between operations  1.55 us (1%)
    ppermute x1, starting transfers between devices, on_device(): far = lax.ppermute(near, ZC, along(4))  19.3 us
    ppermute x1, starting transfers between devices, on_device(): other = lax.ppermute(mine, 'zh', [(0, 1), (1, 0)])  15.1 us
    ppermute x3, starting transfers between devices, on_device(): pairs = [pair] + [lax.ppermute(pair, ZC, along(step)) for step in (1, 2, 3)]  12 us
    ppermute x3, starting transfers between devices, on_device(): lax.ppermute(own, 'y', [(k, (k - r) % Y) for k in range(Y)])  9.5 us
    pallas_call x4, Pallas kernels, score_call(): pl.pallas_call(functools.partial(score_kernel, first, last), out_shape=(j...  8.7 us
    all_to_all x1, starting transfers between devices, on_device(): plane = lax.all_to_all(past, PLANE, 0, 0, tiled=True).reshape(32, 8, 128)  8.02 us
    ppermute x3, waiting for transfers between devices, on_device(): lax.ppermute(own, 'y', [(k, (k - r) % Y) for k in range(Y)])  7.71 us
    ppermute x1, starting transfers between devices, on_device(): cross_two = lax.ppermute(two[1, BLOCK:], ZC, across(2))  5.77 us
  transfers between devices with their start and end apart: 15, of which 7 were waited for; matrix products, arithmetic and copies ran while one was open for 1% of the time, Pallas kernels for 7%

profile of v2, /device:TPU:1, one launch (start us, length us, event | category | flops | bytes accessed | tf_op | source)
XLA Modules:
  0.0 124.8 jit_solution(15357797222379206794)
XLA Ops:
  0.7 0.8 fusion.23
  1.9 3.3 %fusion.2 = bf16[64,512]{1,0:T(8,128)(2,1)S(1)} fusion(bf16[1024,512]{1,0:T(8,128)(2,1)S(1)} %copy-done, bf16[64,2048]{1,0:T(8,128)(2,1)} %param.6, bf16[2048,1024]{1,0:T(8,128)(2,1)} %param.7), kind=kOutput, calls=%fused_computation.3 | convolution fusion | flops 335708160 | bytes 5570560 | tf_op jit(solution)/shard_map/dot_general | solution.py:207
  5.2 4.9 %collective-permute-start = (bf16[72,512]{1,0:T(8,128)(2,1)S(1)}, bf16[72,512]{1,0:T(8,128)(2,1)S(1)}, u32[]{:S(2)}, u32[]{:S(2)}) collective-permute-start(bf16[72,512]{1,0:T(8,128)(2,1)S(1)} %fusion.7), channel_id=1, source_target_pairs={{0,969},{1,64},{64,1},{65,128},{128,65},{129,192},{192,129},{193,2... | collective-permute-start | bytes 221192 | tf_op jit(solution)/shard_map/ppermute | solution.py:216
  10.2 2.0 %collective-permute-done = bf16[72,512]{1,0:T(8,128)(2,1)S(1)} collective-permute-done((bf16[72,512]{1,0:T(8,128)(2,1)S(1)}, bf16[72,512]{1,0:T(8,128)(2,1)S(1)}, u32[]{:S(2)}, u32[]{:S(2)}) %collective-permute-start) | collective-permute-done | bytes 73760 | tf_op jit(solution)/shard_map/ppermute | solution.py:216
  12.4 19.3 %collective-permute-start.1 = (bf16[144,512]{1,0:T(8,128)(2,1)S(1)}, bf16[144,512]{1,0:T(8,128)(2,1)}, u32[]{:S(2)}, u32[]{:S(2)}) collective-permute-start(bf16[144,512]{1,0:T(8,128)(2,1)S(1)} %fusion.4.near_ref), channel_id=1, source_target_pairs={{0,256},{1,777},{64,320},{65,841},{128,384},{129,905},{192,448},{1... | collective-permute-start | bytes 442376 | tf_op jit(solution)/shard_map/ppermute | solution.py:227
  31.7 4.6 %collective-permute-start.2 = (bf16[528,512]{1,0:T(8,128)(2,1)S(1)}, bf16[528,512]{1,0:T(8,128)(2,1)S(1)}, u32[]{:S(2)}, u32[]{:S(2)}) collective-permute-start(bf16[528,512]{1,0:T(8,128)(2,1)S(1)} %pad_maximum_fusion.refs_0_), channel_id=1, source_target_pairs={{0,48},{16,0},{32,16},{48,32},{1,49},{17,1},{33,17},{49,33},{2,50}... | collective-permute-start | bytes 1622024 | tf_op jit(solution)/shard_map/ppermute | solution.py:230
  36.4 2.3 %collective-permute-start.3 = (bf16[528,512]{1,0:T(8,128)(2,1)S(1)}, bf16[528,512]{1,0:T(8,128)(2,1)S(1)}, u32[]{:S(2)}, u32[]{:S(2)}) collective-permute-start(bf16[528,512]{1,0:T(8,128)(2,1)S(1)} %pad_maximum_fusion.refs_0_), channel_id=1, source_target_pairs={{0,32},{16,48},{32,0},{48,16},{1,33},{17,49},{33,1},{49,17},{2,34}... | collective-permute-start | bytes 1622024 | tf_op jit(solution)/shard_map/ppermute | solution.py:230
  38.7 2.6 %collective-permute-start.4 = (bf16[528,512]{1,0:T(8,128)(2,1)S(1)}, bf16[528,512]{1,0:T(8,128)(2,1)S(1)}, u32[]{:S(2)}, u32[]{:S(2)}) collective-permute-start(bf16[528,512]{1,0:T(8,128)(2,1)S(1)} %pad_maximum_fusion.refs_0_), channel_id=1, source_target_pairs={{0,16},{16,32},{32,48},{48,0},{1,17},{17,33},{33,49},{49,1},{2,18}... | collective-permute-start | bytes 1622024 | tf_op jit(solution)/shard_map/ppermute | solution.py:230
  41.3 1.7 %shard_map.77.items_ref = bf16[288,512]{1,0:T(8,128)(2,1)} custom-call(bf16[144,512]{1,0:T(8,128)(2,1)} %copy-done.4, bf16[144,512]{1,0:T(8,128)(2,1)} %collective-permute-done.1.far_ref), custom_call_target="tpu_custom_call" | custom-call | flops 60000002048 | bytes 600000 | tf_op jit(solution)/shard_map/pallas_call | solution.py:189
  43.0 5.0 %collective-permute-start.5 = (bf16[288,512]{1,0:T(8,128)(2,1)}, bf16[288,512]{1,0:T(8,128)(2,1)}, u32[]{:S(2)}, u32[]{:S(2)}) collective-permute-start(bf16[288,512]{1,0:T(8,128)(2,1)} %shard_map.77.items_ref), channel_id=1, source_target_pairs={{0,64},{1,969},{64,128},{65,1},{128,192},{129,65},{192,256},{193,1... | collective-permute-start | bytes 884744 | tf_op jit(solution)/shard_map/ppermute | solution.py:234
  48.1 2.2 %collective-permute-start.6 = (bf16[288,512]{1,0:T(8,128)(2,1)}, bf16[288,512]{1,0:T(8,128)(2,1)}, u32[]{:S(2)}, u32[]{:S(2)}) collective-permute-start(bf16[288,512]{1,0:T(8,128)(2,1)} %shard_map.77.items_ref), channel_id=1, source_target_pairs={{0,128},{1,905},{64,192},{65,969},{128,256},{129,1},{192,320},{193... | collective-permute-start | bytes 884744 | tf_op jit(solution)/shard_map/ppermute | solution.py:234
  50.2 7.6 %collective-permute-done.2.refs_1_ = bf16[528,512]{1,0:T(8,128)(2,1)S(1)} collective-permute-done((bf16[528,512]{1,0:T(8,128)(2,1)S(1)}, bf16[528,512]{1,0:T(8,128)(2,1)S(1)}, u32[]{:S(2)}, u32[]{:S(2)}) %collective-permute-start.2) | collective-permute-done | bytes 540704 | tf_op jit(solution)/shard_map/ppermute | solution.py:230
  57.8 4.8 %collective-permute-start.7 = (bf16[288,512]{1,0:T(8,128)(2,1)}, bf16[288,512]{1,0:T(8,128)(2,1)S(1)}, u32[]{:S(2)}, u32[]{:S(2)}) collective-permute-start(bf16[288,512]{1,0:T(8,128)(2,1)} %shard_map.77.items_ref), channel_id=1, source_target_pairs={{0,192},{1,841},{64,256},{65,905},{128,320},{129,969},{192,384},{1... | collective-permute-start | bytes 884744 | tf_op jit(solution)/shard_map/ppermute | solution.py:234
  63.6 1.0 copy-done.1
  64.6 1.9 %shard_map.78 = (f32[1,256]{1,0:T(1,128)S(1)}, f32[8,2048]{1,0:T(8,128)S(1)}) custom-call(s32[5]{0:T(128)S(1)} %stack.80.base_ref, bf16[288,512]{1,0:T(8,128)(2,1)S(1)} %copy-done.1, bf16[528,512]{1,0:T(8,128)(2,1)S(1)} %pad_maximum_fusion.refs_0_, bf16[528,512]{1,0:T(8,128)(2,1)S(1)} %collective-permute-done.2.refs_1_, ...), custom_call_target="tpu_custom_call" | custom-call | flops 536870912 | bytes 4194304 | tf_op jit(solution)/shard_map/pallas_call | solution.py:158
  66.6 2.4 %shard_map.79 = (f32[1,256]{1,0:T(1,128)S(1)}, f32[8,2048]{1,0:T(8,128)S(1)}) custom-call(s32[5]{0:T(128)S(1)} %stack.88.base_ref, bf16[288,512]{1,0:T(8,128)(2,1)} %collective-permute-done.5.items_ref, bf16[528,512]{1,0:T(8,128)(2,1)S(1)} %pad_maximum_fusion.refs_0_, bf16[528,512]{1,0:T(8,128)(2,1)S(1)} %collective-permute-done.2.refs_1_, ...), custom_call_target="tpu_custom_call" | custom-call | flops 536870912 | bytes 4194304 | tf_op jit(solution)/shard_map/pallas_call | solution.py:158
  69.0 2.4 %shard_map.80 = (f32[1,256]{1,0:T(1,128)S(1)}, f32[8,2048]{1,0:T(8,128)S(1)}) custom-call(s32[5]{0:T(128)S(1)} %stack.93.base_ref, bf16[288,512]{1,0:T(8,128)(2,1)} %collective-permute-done.6.items_ref, bf16[528,512]{1,0:T(8,128)(2,1)S(1)} %pad_maximum_fusion.refs_0_, bf16[528,512]{1,0:T(8,128)(2,1)S(1)} %collective-permute-done.2.refs_1_, ...), custom_call_target="tpu_custom_call" | custom-call | flops 536870912 | bytes 4194304 | tf_op jit(solution)/shard_map/pallas_call | solution.py:158
  71.4 1.1 collective-permute-done.7.items_ref
  72.5 2.0 %shard_map.81 = (f32[1,256]{1,0:T(1,128)S(1)}, f32[256,128]{1,0:T(8,128)S(1)}) custom-call(s32[5]{0:T(128)S(1)} %stack.98.base_ref, bf16[288,512]{1,0:T(8,128)(2,1)S(1)} %collective-permute-done.7.items_ref, bf16[528,512]{1,0:T(8,128)(2,1)S(1)} %pad_maximum_fusion.refs_0_, bf16[528,512]{1,0:T(8,128)(2,1)S(1)} %collective-permute-done.2.refs_1_, ...), custom_call_target="tpu_custom_call" | custom-call | flops 536870912 | bytes 4194304 | tf_op jit(solution)/shard_map/pallas_call | solution.py:158
  74.5 0.6 copy-done.2
  75.1 8.0 %all-to-all-start = ((f32[32,8,128]{2,1,0:T(8,128)}), f32[32,8,128]{2,1,0:T(8,128)S(1)}, u32[]{:S(2)}, u32[]{:S(2)}) async-start(f32[32,8,128]{2,1,0:T(8,128)} %bitcast.51), calls=%async_computation | async-start | bytes 262144 | tf_op jit(solution)/shard_map/all_to_all | solution.py:259
  83.2 1.9 %collective-permute-start.8 = (f32[4,128]{1,0:T(4,128)S(1)}, f32[4,128]{1,0:T(4,128)S(1)}, u32[]{:S(2)}, u32[]{:S(2)}) collective-permute-start(f32[4,128]{1,0:T(4,128)S(1)} %slice.72), channel_id=1, source_target_pairs={{0,776},{1,257},{64,840},{65,321},{128,904},{129,385},{192,968},{1... | collective-permute-start | bytes 6152 | tf_op jit(solution)/shard_map/ppermute | solution.py:260
  85.1 5.7 %all-to-all-done = f32[32,8,128]{2,1,0:T(8,128)S(1)} async-done(((f32[32,8,128]{2,1,0:T(8,128)}), f32[32,8,128]{2,1,0:T(8,128)S(1)}, u32[]{:S(2)}, u32[]{:S(2)}) %all-to-all-start) | async-done | bytes 131104 | tf_op jit(solution)/shard_map/all_to_all | solution.py:259
  90.9 3.8 %collective-permute-done.8 = f32[4,128]{1,0:T(4,128)S(1)} collective-permute-done((f32[4,128]{1,0:T(4,128)S(1)}, f32[4,128]{1,0:T(4,128)S(1)}, u32[]{:S(2)}, u32[]{:S(2)}) %collective-permute-start.8) | collective-permute-done | bytes 2080 | tf_op jit(solution)/shard_map/ppermute | solution.py:260
  94.8 1.9 %collective-permute-start.9 = (f32[2,128]{1,0:T(2,128)S(1)}, f32[2,128]{1,0:T(2,128)S(1)}, u32[]{:S(2)}, u32[]{:S(2)}) collective-permute-start(f32[2,128]{1,0:T(2,128)S(1)} %slice.59), channel_id=1, source_target_pairs={{0,904},{1,129},{64,968},{65,193},{128,0},{129,257},{192,64},{193,... | collective-permute-start | bytes 3080 | tf_op jit(solution)/shard_map/ppermute | solution.py:269
  96.7 15.1 %collective-permute-start.11 = (f32[8,128]{1,0:T(8,128)S(1)}, f32[8,128]{1,0:T(8,128)S(1)}, u32[]{:S(2)}, u32[]{:S(2)}) collective-permute-start(f32[8,128]{1,0:T(8,128)S(1)} %pad_maximum_fusion.2), channel_id=1, source_target_pairs={{0,8},{8,0},{1,9},{9,1},{2,10},{10,2},{3,11},{11,3},{4,12},{12,4},... | collective-permute-start | bytes 12296 | tf_op jit(solution)/shard_map/ppermute | solution.py:268
  111.9 3.2 %collective-permute-start.10 = (f32[64]{0:T(128)S(1)}, f32[64]{0:T(128)S(1)}, u32[]{:S(2)}, u32[]{:S(2)}) collective-permute-start(f32[64]{0:T(128)S(1)} %get-tuple-element.38), channel_id=1, source_target_pairs={{0,968},{1,65},{64,0},{65,129},{128,64},{129,193},{192,128},{193,2... | collective-permute-start | bytes 776 | tf_op jit(solution)/shard_map/ppermute | solution.py:271
  115.1 2.1 %collective-permute-start.12 = (f32[64]{0:T(128)S(1)}, f32[64]{0:T(128)S(1)}, u32[]{:S(2)}, u32[]{:S(2)}) collective-permute-start(f32[64]{0:T(128)S(1)} %get-tuple-element.36), channel_id=1, source_target_pairs={{0,969},{1,64},{64,1},{65,128},{128,65},{129,192},{192,129},{193,2... | collective-permute-start | bytes 776 | tf_op jit(solution)/shard_map/ppermute | solution.py:272
  117.3 5.8 %collective-permute-start.13 = (f32[64]{0:T(128)S(1)}, f32[64]{0:T(128)S(1)}, u32[]{:S(2)}, u32[]{:S(2)}) collective-permute-start(f32[64]{0:T(128)S(1)} %get-tuple-element.37), channel_id=1, source_target_pairs={{0,905},{1,128},{64,969},{65,192},{128,1},{129,256},{192,65},{193,... | collective-permute-start | bytes 776 | tf_op jit(solution)/shard_map/ppermute | solution.py:273
  123.1 0.6 add_subtract_fusion
  123.7 0.6 collective-permute-done.13
  124.3 0.5 log_add_fusion.3
  (45 shorter events, 1.4 us)
Async XLA Ops:
  0.6 1.3 %copy-start = (bf16[1024,512]{1,0:T(8,128)(2,1)S(1)}, bf16[1024,512]{1,0:T(8,128)(2,1)}, u32[]{:S(2)}) copy-start(bf16[1024,512]{1,0:T(8,128)(2,1)} %param.8) | copy-start | bytes 3145732
  0.6 9.5 %copy-start.5 = (s32[512]{0:T(512)S(1)}, s32[512]{0:T(512)}, u32[]{:S(2)}) copy-start(s32[512]{0:T(512)} %param.11) | copy-start | bytes 6148
  0.7 31.0 %copy-start.3 = (bf16[512,512]{1,0:T(8,128)(2,1)S(1)}, bf16[512,512]{1,0:T(8,128)(2,1)}, u32[]{:S(2)}) copy-start(bf16[512,512]{1,0:T(8,128)(2,1)} %param.10) | copy-start | bytes 1572868
  5.2 7.0 %collective-permute-start = (bf16[72,512]{1,0:T(8,128)(2,1)S(1)}, bf16[72,512]{1,0:T(8,128)(2,1)S(1)}, u32[]{:S(2)}, u32[]{:S(2)}) collective-permute-start(bf16[72,512]{1,0:T(8,128)(2,1)S(1)} %fusion.7), channel_id=1, source_target_pairs={{0,969},{1,64},{64,1},{65,128},{128,65},{129,192},{192,129},{193,2... | collective-permute-start | bytes 221192 | tf_op jit(solution)/shard_map/ppermute | solution.py:216
  12.4 28.9 %copy-start.4 = (bf16[144,512]{1,0:T(8,128)(2,1)}, bf16[144,512]{1,0:T(8,128)(2,1)S(1)}, u32[]{:S(2)}) copy-start(bf16[144,512]{1,0:T(8,128)(2,1)S(1)} %fusion.4.near_ref) | copy-start | bytes 442372
  12.4 28.9 %collective-permute-start.1 = (bf16[144,512]{1,0:T(8,128)(2,1)S(1)}, bf16[144,512]{1,0:T(8,128)(2,1)}, u32[]{:S(2)}, u32[]{:S(2)}) collective-permute-start(bf16[144,512]{1,0:T(8,128)(2,1)S(1)} %fusion.4.near_ref), channel_id=1, source_target_pairs={{0,256},{1,777},{64,320},{65,841},{128,384},{129,905},{192,448},{1... | collective-permute-start | bytes 442376 | tf_op jit(solution)/shard_map/ppermute | solution.py:227
  31.7 26.1 %collective-permute-start.2 = (bf16[528,512]{1,0:T(8,128)(2,1)S(1)}, bf16[528,512]{1,0:T(8,128)(2,1)S(1)}, u32[]{:S(2)}, u32[]{:S(2)}) collective-permute-start(bf16[528,512]{1,0:T(8,128)(2,1)S(1)} %pad_maximum_fusion.refs_0_), channel_id=1, source_target_pairs={{0,48},{16,0},{32,16},{48,32},{1,49},{17,1},{33,17},{49,33},{2,50}... | collective-permute-start | bytes 1622024 | tf_op jit(solution)/shard_map/ppermute | solution.py:230
  36.4 27.2 %collective-permute-start.3 = (bf16[528,512]{1,0:T(8,128)(2,1)S(1)}, bf16[528,512]{1,0:T(8,128)(2,1)S(1)}, u32[]{:S(2)}, u32[]{:S(2)}) collective-permute-start(bf16[528,512]{1,0:T(8,128)(2,1)S(1)} %pad_maximum_fusion.refs_0_), channel_id=1, source_target_pairs={{0,32},{16,48},{32,0},{48,16},{1,33},{17,49},{33,1},{49,17},{2,34}... | collective-permute-start | bytes 1622024 | tf_op jit(solution)/shard_map/ppermute | solution.py:230
  38.7 25.0 %collective-permute-start.4 = (bf16[528,512]{1,0:T(8,128)(2,1)S(1)}, bf16[528,512]{1,0:T(8,128)(2,1)S(1)}, u32[]{:S(2)}, u32[]{:S(2)}) collective-permute-start(bf16[528,512]{1,0:T(8,128)(2,1)S(1)} %pad_maximum_fusion.refs_0_), channel_id=1, source_target_pairs={{0,16},{16,32},{32,48},{48,0},{1,17},{17,33},{33,49},{49,1},{2,18}... | collective-permute-start | bytes 1622024 | tf_op jit(solution)/shard_map/ppermute | solution.py:230
  43.0 23.6 %collective-permute-start.5 = (bf16[288,512]{1,0:T(8,128)(2,1)}, bf16[288,512]{1,0:T(8,128)(2,1)}, u32[]{:S(2)}, u32[]{:S(2)}) collective-permute-start(bf16[288,512]{1,0:T(8,128)(2,1)} %shard_map.77.items_ref), channel_id=1, source_target_pairs={{0,64},{1,969},{64,128},{65,1},{128,192},{129,65},{192,256},{193,1... | collective-permute-start | bytes 884744 | tf_op jit(solution)/shard_map/ppermute | solution.py:234
  48.1 20.9 %collective-permute-start.6 = (bf16[288,512]{1,0:T(8,128)(2,1)}, bf16[288,512]{1,0:T(8,128)(2,1)}, u32[]{:S(2)}, u32[]{:S(2)}) collective-permute-start(bf16[288,512]{1,0:T(8,128)(2,1)} %shard_map.77.items_ref), channel_id=1, source_target_pairs={{0,128},{1,905},{64,192},{65,969},{128,256},{129,1},{192,320},{193... | collective-permute-start | bytes 884744 | tf_op jit(solution)/shard_map/ppermute | solution.py:234
  57.8 14.6 %collective-permute-start.7 = (bf16[288,512]{1,0:T(8,128)(2,1)}, bf16[288,512]{1,0:T(8,128)(2,1)S(1)}, u32[]{:S(2)}, u32[]{:S(2)}) collective-permute-start(bf16[288,512]{1,0:T(8,128)(2,1)} %shard_map.77.items_ref), channel_id=1, source_target_pairs={{0,192},{1,841},{64,256},{65,905},{128,320},{129,969},{192,384},{1... | collective-permute-start | bytes 884744 | tf_op jit(solution)/shard_map/ppermute | solution.py:234
  63.6 1.0 copy-start.1
  74.5 0.7 copy-start.2
  75.1 15.7 %all-to-all-start = ((f32[32,8,128]{2,1,0:T(8,128)}), f32[32,8,128]{2,1,0:T(8,128)S(1)}, u32[]{:S(2)}, u32[]{:S(2)}) async-start(f32[32,8,128]{2,1,0:T(8,128)} %bitcast.51), calls=%async_computation | async-start | bytes 262144 | tf_op jit(solution)/shard_map/all_to_all | solution.py:259
  83.2 11.6 %collective-permute-start.8 = (f32[4,128]{1,0:T(4,128)S(1)}, f32[4,128]{1,0:T(4,128)S(1)}, u32[]{:S(2)}, u32[]{:S(2)}) collective-permute-start(f32[4,128]{1,0:T(4,128)S(1)} %slice.72), channel_id=1, source_target_pairs={{0,776},{1,257},{64,840},{65,321},{128,904},{129,385},{192,968},{1... | collective-permute-start | bytes 6152 | tf_op jit(solution)/shard_map/ppermute | solution.py:260
  94.8 17.0 %collective-permute-start.9 = (f32[2,128]{1,0:T(2,128)S(1)}, f32[2,128]{1,0:T(2,128)S(1)}, u32[]{:S(2)}, u32[]{:S(2)}) collective-permute-start(f32[2,128]{1,0:T(2,128)S(1)} %slice.59), channel_id=1, source_target_pairs={{0,904},{1,129},{64,968},{65,193},{128,0},{129,257},{192,64},{193,... | collective-permute-start | bytes 3080 | tf_op jit(solution)/shard_map/ppermute | solution.py:269
  96.7 26.4 %collective-permute-start.11 = (f32[8,128]{1,0:T(8,128)S(1)}, f32[8,128]{1,0:T(8,128)S(1)}, u32[]{:S(2)}, u32[]{:S(2)}) collective-permute-start(f32[8,128]{1,0:T(8,128)S(1)} %pad_maximum_fusion.2), channel_id=1, source_target_pairs={{0,8},{8,0},{1,9},{9,1},{2,10},{10,2},{3,11},{11,3},{4,12},{12,4},... | collective-permute-start | bytes 12296 | tf_op jit(solution)/shard_map/ppermute | solution.py:268
  111.9 11.8 %collective-permute-start.10 = (f32[64]{0:T(128)S(1)}, f32[64]{0:T(128)S(1)}, u32[]{:S(2)}, u32[]{:S(2)}) collective-permute-start(f32[64]{0:T(128)S(1)} %get-tuple-element.38), channel_id=1, source_target_pairs={{0,968},{1,65},{64,0},{65,129},{128,64},{129,193},{192,128},{193,2... | collective-permute-start | bytes 776 | tf_op jit(solution)/shard_map/ppermute | solution.py:271
  115.1 8.6 %collective-permute-start.12 = (f32[64]{0:T(128)S(1)}, f32[64]{0:T(128)S(1)}, u32[]{:S(2)}, u32[]{:S(2)}) collective-permute-start(f32[64]{0:T(128)S(1)} %get-tuple-element.36), channel_id=1, source_target_pairs={{0,969},{1,64},{64,1},{65,128},{128,65},{129,192},{192,129},{193,2... | collective-permute-start | bytes 776 | tf_op jit(solution)/shard_map/ppermute | solution.py:272
  117.3 7.0 %collective-permute-start.13 = (f32[64]{0:T(128)S(1)}, f32[64]{0:T(128)S(1)}, u32[]{:S(2)}, u32[]{:S(2)}) collective-permute-start(f32[64]{0:T(128)S(1)} %get-tuple-element.37), channel_id=1, source_target_pairs={{0,905},{1,128},{64,969},{65,192},{128,1},{129,256},{192,65},{193,... | collective-permute-start | bytes 776 | tf_op jit(solution)/shard_map/ppermute | solution.py:273

commit v3 on v2

--- a/solution.py
+++ b/solution.py
@@ -19,8 +19,10 @@
 USERS = 512
 Y = 4
 DEPTH = 512
-ITEMS = 256
+PARTS = 4
+ITEMS = PARTS * BLOCK
 HALF = ITEMS // 2
+SEGMENT = 256
 EXTRA = 16
 TEMP = 4.0 / math.sqrt(DEPTH)
 LOG2E = 1.0 / math.log(2.0)
@@ -54,42 +56,42 @@
 
 
 def score_kernel(first, last, base_ref, items_ref, *refs):
-    users_refs, refs = refs[:Y], refs[Y:]
-    if first:
-        item_ref, row_ref, scores, weight, ids, top_item, sum_item = refs
-    else:
-        past_ref, item_ref, row_ref, scores, weight, ids, top_item, sum_item = refs
+    mine_ref, other_ref, *refs = refs
+    rows = SEGMENT + EXTRA
+    segments = [(ref, y * rows) for y in range(Y) for ref in (mine_ref, other_ref)]
+    past_ref = None if first else refs.pop(0)
+    item_ref, row_ref, scores, weight, ids, top_item, sum_item = refs
     for half in range(2):
         start = half * (HALF + EXTRA) + HALF
         extra = items_ref[start : start + EXTRA, 0:256].astype(F32)
         row = (extra[0:1, 0:128] + extra[0:1, 128:256]) * (1.0 / TEMP)
         weight[HALF * half : HALF * (half + 1), :] = jnp.broadcast_to(row, (HALF, 128)).T
     spot = lax.broadcasted_iota(jnp.int32, (BLOCK, 128), 0)
-    for part in range(ITEMS // BLOCK):
+    for part in range(PARTS):
         ids[part * BLOCK : (part + 1) * BLOCK, :] = (spot + base_ref[part]).astype(F32)
 
     chunks = [slice(g, g + CHUNK) for g in range(0, ITEMS, CHUNK)]
-    tiles = [slice(k, k + 128) for k in range(0, USERS, 128)]
+    tiles = [slice(k, k + 128) for k in range(0, SEGMENT, 128)]
     items = jnp.concatenate(
         [items_ref[0:HALF, :], items_ref[HALF + EXTRA : 2 * HALF + EXTRA, :]], axis=0
     )
     tops, positives = [], []
-    for y in range(Y):
+    for s, (users_ref, start) in enumerate(segments):
         raw = lax.dot_general(
             items,
-            users_refs[y][0:USERS, :],
+            users_ref[start : start + SEGMENT, :],
             (((1,), (1,)), ((), ())),
             preferred_element_type=F32,
         )
-        index_rows = users_refs[y][USERS : USERS + EXTRA, :].astype(F32)
+        index_rows = users_ref[start + SEGMENT : start + rows, 0:SEGMENT].astype(F32)
         wanted = index_rows[0:1, :] * 256.0 + index_rows[1:2, :]
-        top_y, positive_y = [], []
+        top_s, positive_s = [], []
         for k in tiles:
             top, positive = None, None
             for g in chunks:
                 piece = raw[g, k]
-                scores[g, y * USERS + k.start : y * USERS + k.stop] = piece
-                if y == 0 and k.start == 0:
+                scores[g, s * SEGMENT + k.start : s * SEGMENT + k.stop] = piece
+                if s == 0 and k.start == 0:
                     top_item[g, :] = piece
                 else:
                     top_item[g, :] = jnp.maximum(top_item[g, :], piece)
@@ -100,20 +102,20 @@
                 part_positive = jnp.sum(found.reshape(shape), axis=0)
                 top = part_top if top is None else jnp.maximum(top, part_top)
                 positive = part_positive if positive is None else positive + part_positive
-            top_y.append(jnp.max(top, axis=0, keepdims=True))
-            positive_y.append(jnp.sum(positive, axis=0, keepdims=True))
-        tops.append(top_y)
-        positives.append(positive_y)
+            top_s.append(jnp.max(top, axis=0, keepdims=True))
+            positive_s.append(jnp.sum(positive, axis=0, keepdims=True))
+        tops.append(top_s)
+        positives.append(positive_s)
 
     for g in chunks:
         top_item[g, :] = jnp.broadcast_to(
             jnp.max(top_item[g, :], axis=1, keepdims=True), (CHUNK, 128)
         )
-    for y in range(Y):
-        ready = []
+    ready = []
+    for s in range(len(segments)):
         for t, k in enumerate(tiles):
-            place = slice(y * USERS + k.start, y * USERS + k.stop)
-            top, positive = tops[y][t], positives[y][t]
+            place = slice(s * SEGMENT + k.start, s * SEGMENT + k.stop)
+            top, positive = tops[s][t], positives[s][t]
             if not first:
                 old_top = past_ref[0:1, place]
                 top = jnp.maximum(old_top, top)
@@ -122,7 +124,7 @@
             for g in chunks:
                 piece = scores[g, place]
                 by_item = jnp.exp2((piece - top_item[g, :]) * (TEMP * LOG2E))
-                if y == 0 and t == 0:
+                if s == 0 and t == 0:
                     sum_item[g, :] = by_item
                 else:
                     sum_item[g, :] = sum_item[g, :] + by_item
@@ -139,11 +141,20 @@
                 row_ref[0:1, place] = top
                 row_ref[1:2, place] = total
                 row_ref[2:3, place] = positive
-        if last:
-            tile = jnp.concatenate([lse for lse, _ in ready] + [pos for _, pos in ready], axis=0)
-            block = (base_ref[4] + y) % Y
+    if last:
+        for y in range(Y):
+            straight = ready[4 * y : 4 * y + 4]
+            turned = straight[2:] + straight[:2]
+            tile = jnp.concatenate(
+                [
+                    jnp.where(base_ref[PARTS] == 0, straight[t][kind], turned[t][kind])
+                    for kind in range(2)
+                    for t in range(4)
+                ],
+                axis=0,
+            )
             for peer in range(8):
-                row_ref[pl.ds(pl.multiple_of((block * 8 + peer) * 8, 8), 8), :] = tile
+                row_ref[(y * 8 + peer) * 8 : (y * 8 + peer + 1) * 8, :] = tile
     for half in range(2):
         g = slice(128 * half, 128 * half + 128)
         total = jnp.broadcast_to(jnp.sum(sum_item[g, :], axis=1, keepdims=True), (128, 128))
@@ -170,7 +181,7 @@
             pltpu.VMEM((ITEMS, 128), F32),
             pltpu.VMEM((ITEMS, 128), F32),
         ],
-        compiler_params=pltpu.CompilerParams(vmem_limit_bytes=24 * 1024 * 1024),
+        compiler_params=pltpu.CompilerParams(vmem_limit_bytes=12 * 1024 * 1024),
         cost_estimate=pl.CostEstimate(
             flops=2 * ITEMS * Y * USERS * DEPTH,
             bytes_accessed=4 * 1024 * 1024,
@@ -191,6 +202,7 @@
         out_shape=jax.ShapeDtypeStruct((2 * (HALF + EXTRA), DEPTH), BF16),
         in_specs=[vmem, vmem],
         out_specs=vmem,
+        compiler_params=pltpu.CompilerParams(vmem_limit_bytes=4 * 1024 * 1024),
         cost_estimate=pl.CostEstimate(flops=60 * 10**9, bytes_accessed=600_000, transcendentals=0),
     )(near, far)
 
@@ -207,6 +219,7 @@
     embedded = jnp.dot(hidden, layer_two, preferred_element_type=F32).astype(BF16)
     weight_high, weight_low = high_low(log_weight)
 
+    zl, y, zh, x, c = (lax.axis_index(name) for name in AXES)
     def rows(values, count):
         return jnp.pad(values[None, :], ((0, count - 1), (0, DEPTH - values.shape[0])))
 
@@ -219,21 +232,25 @@
     )
     near = jnp.concatenate([embedded, came[0:BLOCK], rows(weights, EXTRA)], axis=0)
 
-    high = (positive_index // 256).astype(BF16)
-    low = (positive_index % 256).astype(BF16)
-    index_rows = jnp.pad(jnp.stack([high, low]), ((0, EXTRA - 2), (0, 0)))
-    own = jnp.concatenate([user_vectors, index_rows], axis=0)
+    high = (positive_index // 256).astype(BF16).reshape(2, 1, SEGMENT)
+    low = (positive_index % 256).astype(BF16).reshape(2, 1, SEGMENT)
+    index_rows = jnp.pad(
+        jnp.concatenate([high, low], axis=1), ((0, 0), (0, EXTRA - 2), (0, DEPTH - SEGMENT))
+    )
+    own = jnp.concatenate([user_vectors.reshape(2, SEGMENT, DEPTH), index_rows], axis=1)
+    half = lax.dynamic_index_in_dim(own, c, 0, keepdims=False)
 
     far = lax.ppermute(near, ZC, along(4))
-    own, near = lax.optimization_barrier((own, near))
-    users = [own] + [
-        lax.ppermute(own, "y", [(k, (k - r) % Y) for k in range(Y)]) for r in (1, 3, 2)
-    ]
-    users = [users[0], users[1], users[3], users[2]]
+    half, near = lax.optimization_barrier((half, near))
+    mine = lax.all_to_all(jnp.tile(half, (Y, 1)), "y", 0, 0, tiled=True)
     pair = stack_call(near, far)
-    pairs = [pair] + [lax.ppermute(pair, ZC, along(step)) for step in (1, 2, 3)]
-
-    zl, y, zh, x, c = (lax.axis_index(name) for name in AXES)
+    two_on = lax.ppermute(pair, ZC, along(2))
+    one_on = lax.ppermute(pair, ZC, along(1))
+    three_on = lax.ppermute(two_on, ZC, along(1))
+    mine, two_here = lax.optimization_barrier((mine, two_on))
+    users = [mine, lax.ppermute(mine, "c", [(0, 1), (1, 0)])]
+    groups = [pair, one_on, two_here, three_on]
+
     z = zh * 16 + zl
 
     def base(place, core):
@@ -241,18 +258,18 @@
         item = ((place // 16) * 4 + x) * 2 + core
         return (item * 64 + (place % 16) * 4 + y) * BLOCK
 
-    side = jnp.where(c == 0, -1, 1)
+    way = jnp.where(c == 0, -1, 1)
     columns, past = [], None
     for step in range(4):
         bases = jnp.stack(
             [
-                base(z + side * (step + more + cross), jnp.where(cross == 0, c, 1 - c))
+                base(z + way * (step + more + cross), jnp.where(cross == 0, c, 1 - c))
                 for more in (0, 4)
                 for cross in (0, 1)
             ]
-            + [y]
+            + [c]
         ).astype(jnp.int32)
-        column, past = score_call(step == 0, step == 3, bases, pairs[step], users, past)
+        column, past = score_call(step == 0, step == 3, bases, groups[step], users, past)
         columns.append(column)
 
     stacked = jnp.concatenate(columns, axis=0)
@@ -263,10 +280,10 @@
     top = jnp.max(lse, axis=0)
     lse = top + jnp.log(jnp.sum(jnp.exp(lse - top), axis=0))
     mine = jnp.concatenate([lse, jnp.sum(positive, axis=0)], axis=0)
-    came4, mine = lax.optimization_barrier((came4, mine))
     four = join(stacked[:, :HALF], came4)
+    came2 = lax.ppermute(four[2:], ZC, along(-2))
     other = lax.ppermute(mine, "zh", [(0, 1), (1, 0)])
-    came2 = lax.ppermute(four[2:], ZC, along(-2))
+    came2, _ = lax.optimization_barrier((came2, mine))
     two = join(four[:2], came2)
     one_away = lax.ppermute(two[1, :BLOCK], ZC, along(-1))
     cross_one = lax.ppermute(two[0, BLOCK:], ZC, across(1))

time: 126 us -> 121 us (0.960)
  starting transfers between devices: 83.8 us -> 80.8 us
    ppermute x6 -> x4, starting transfers between devices: 21.5 us -> 16.1 us  [the longest x1 5.99 us: on_device(): three_on = lax.ppermute(two_on, ZC, along(1))]
    ppermute x1, starting transfers between devices: 15.1 us -> 10.9 us  [on_device(): other = lax.ppermute(mine, 'zh', [(0, 1), (1, 0)])]
    all_to_all x0 -> x1, starting transfers between devices: none -> 4.18 us  [on_device(): mine = lax.all_to_all(jnp.tile(half, (Y, 1)), 'y', 0, 0, tiled=True)]
    all_to_all x1, starting transfers between devices: 8.02 us -> 11.9 us  [on_device(): plane = lax.all_to_all(past, PLANE, 0, 0, tiled=True).reshape(32, 8, 128)]
    ppermute x1, waiting for transfers between devices: 3.84 us -> 0.01 us  [on_device(): came4 = lax.ppermute(stacked[:, HALF:], ZC, along(-4))]
    ppermute x1, starting transfers between devices: 5.77 us -> 3.54 us  [on_device(): cross_two = lax.ppermute(two[1, BLOCK:], ZC, across(2))]
    ppermute x1, waiting for transfers between devices: 0.01 us -> 2.02 us  [on_device(): other = lax.ppermute(mine, 'zh', [(0, 1), (1, 0)])]
    ppermute x6 -> x4, waiting for transfers between devices: 8.85 us -> 6.98 us  [the longest x1 6.97 us: on_device(): two_on = lax.ppermute(pair, ZC, along(2))]
  transfers between devices with their start and end apart: 15 -> 14, of which waited for: 7 -> 6; matrix products, arithmetic and copies ran while one was open for 1% -> 2% of each run, Pallas kernels for 7% -> 6%
where the time goes in v3:
time: 121 us
  starting transfers between devices  80.8 us (67%)
  waiting for transfers between devices  19.8 us (16%)
  Pallas kernels  9.82 us (8%)
  matrix products  3.3 us (3%)
  local copies, waits for them, and re-layouts  2.99 us (2%)
  other arithmetic  2.31 us (2%)
  between operations  1.52 us (1%)
    ppermute x1, starting transfers between devices, on_device(): far = lax.ppermute(near, ZC, along(4))  19.3 us
    all_to_all x1, starting transfers between devices, on_device(): plane = lax.all_to_all(past, PLANE, 0, 0, tiled=True).reshape(32, 8, 128)  11.9 us
    ppermute x1, starting transfers between devices, on_device(): other = lax.ppermute(mine, 'zh', [(0, 1), (1, 0)])  10.9 us
    pallas_call x4, Pallas kernels, score_call(): pl.pallas_call(functools.partial(score_kernel, first, last), out_shape=(j...  9.8 us
    ppermute x1, waiting for transfers between devices, on_device(): two_on = lax.ppermute(pair, ZC, along(2))  6.97 us
    ppermute x1, starting transfers between devices, on_device(): three_on = lax.ppermute(two_on, ZC, along(1))  5.99 us
    all_to_all x1, waiting for transfers between devices, on_device(): plane = lax.all_to_all(past, PLANE, 0, 0, tiled=True).reshape(32, 8, 128)  5.66 us
    ppermute x1, starting transfers between devices, on_device(): came = lax.ppermute(sent, ZC, across(1))  4.94 us
  transfers between devices with their start and end apart: 14, of which 6 were waited for; matrix products, arithmetic and copies ran while one was open for 2% of the time, Pallas kernels for 6%

profile of v3, /device:TPU:1, one launch (start us, length us, event | category | flops | bytes accessed | tf_op | source)
XLA Modules:
  0.0 120.6 jit_solution(13512401152942743789)
XLA Ops:
  0.7 0.8 fusion.23
  1.5 0.4 copy-done
  1.9 3.3 %fusion.2 = bf16[64,512]{1,0:T(8,128)(2,1)S(1)} fusion(bf16[1024,512]{1,0:T(8,128)(2,1)S(1)} %copy-done, bf16[64,2048]{1,0:T(8,128)(2,1)} %param.6, bf16[2048,1024]{1,0:T(8,128)(2,1)} %param.7), kind=kOutput, calls=%fused_computation.3 | convolution fusion | flops 335708160 | bytes 5570560 | tf_op jit(solution)/shard_map/dot_general | solution.py:219
  5.2 4.9 %collective-permute-start = (bf16[72,512]{1,0:T(8,128)(2,1)S(1)}, bf16[72,512]{1,0:T(8,128)(2,1)S(1)}, u32[]{:S(2)}, u32[]{:S(2)}) collective-permute-start(bf16[72,512]{1,0:T(8,128)(2,1)S(1)} %fusion.10), channel_id=1, source_target_pairs={{0,969},{1,64},{64,1},{65,128},{128,65},{129,192},{192,129},{193,2... | collective-permute-start | bytes 221192 | tf_op jit(solution)/shard_map/ppermute | solution.py:229
  10.2 2.0 %collective-permute-done = bf16[72,512]{1,0:T(8,128)(2,1)S(1)} collective-permute-done((bf16[72,512]{1,0:T(8,128)(2,1)S(1)}, bf16[72,512]{1,0:T(8,128)(2,1)S(1)}, u32[]{:S(2)}, u32[]{:S(2)}) %collective-permute-start) | collective-permute-done | bytes 73760 | tf_op jit(solution)/shard_map/ppermute | solution.py:229
  12.4 19.3 %collective-permute-start.1 = (bf16[144,512]{1,0:T(8,128)(2,1)S(1)}, bf16[144,512]{1,0:T(8,128)(2,1)S(1)}, u32[]{:S(2)}, u32[]{:S(2)}) collective-permute-start(bf16[144,512]{1,0:T(8,128)(2,1)S(1)} %fusion.7.near_ref), channel_id=1, source_target_pairs={{0,256},{1,777},{64,320},{65,841},{128,384},{129,905},{192,448},{1... | collective-permute-start | bytes 442376 | tf_op jit(solution)/shard_map/ppermute | solution.py:243
  31.7 1.1 tile.2
  32.8 4.2 %all-to-all-start = ((bf16[4,272,512]{2,1,0:T(8,128)(2,1)}), bf16[4,272,512]{2,1,0:T(8,128)(2,1)S(1)}, u32[]{:S(2)}, u32[]{:S(2)}) async-start(bf16[4,272,512]{2,1,0:T(8,128)(2,1)} %tile.2), calls=%async_computation | async-start | bytes 2228224 | tf_op jit(solution)/shard_map/all_to_all | solution.py:245
  37.0 1.4 %collective-permute-done.1.far_ref = bf16[144,512]{1,0:T(8,128)(2,1)S(1)} collective-permute-done((bf16[144,512]{1,0:T(8,128)(2,1)S(1)}, bf16[144,512]{1,0:T(8,128)(2,1)S(1)}, u32[]{:S(2)}, u32[]{:S(2)}) %collective-permute-start.1) | collective-permute-done | bytes 147488 | tf_op jit(solution)/shard_map/ppermute | solution.py:243
  38.5 4.3 %collective-permute-start.2 = (bf16[288,512]{1,0:T(8,128)(2,1)S(1)}, bf16[288,512]{1,0:T(8,128)(2,1)}, u32[]{:S(2)}, u32[]{:S(2)}) collective-permute-start(bf16[288,512]{1,0:T(8,128)(2,1)S(1)} %shard_map.77.items_ref), channel_id=1, source_target_pairs={{0,128},{1,905},{64,192},{65,969},{128,256},{129,1},{192,320},{193... | collective-permute-start | bytes 884744 | tf_op jit(solution)/shard_map/ppermute | solution.py:247
  42.8 7.0 %collective-permute-done.2.items_ref = bf16[288,512]{1,0:T(8,128)(2,1)} collective-permute-done((bf16[288,512]{1,0:T(8,128)(2,1)S(1)}, bf16[288,512]{1,0:T(8,128)(2,1)}, u32[]{:S(2)}, u32[]{:S(2)}) %collective-permute-start.2) | collective-permute-done | bytes 294944 | tf_op jit(solution)/shard_map/ppermute | solution.py:247
  49.8 1.8 %all-to-all-done = bf16[4,272,512]{2,1,0:T(8,128)(2,1)S(1)} async-done(((bf16[4,272,512]{2,1,0:T(8,128)(2,1)}), bf16[4,272,512]{2,1,0:T(8,128)(2,1)S(1)}, u32[]{:S(2)}, u32[]{:S(2)}) %all-to-all-start) | async-done | bytes 1114144 | tf_op jit(solution)/shard_map/all_to_all | solution.py:245
  51.6 3.7 %collective-permute-start.3 = (bf16[1088,512]{1,0:T(8,128)(2,1)S(1)}, bf16[1088,512]{1,0:T(8,128)(2,1)S(1)}, u32[]{:S(2)}, u32[]{:S(2)}) collective-permute-start(bf16[1088,512]{1,0:T(8,128)(2,1)S(1)} %bitcast.55), channel_id=1, source_target_pairs={{0,1},{1,0},{2,3},{3,2},{4,5},{5,4},{6,7},{7,6},{8,9},{9,8},{10,11... | collective-permute-start | bytes 3342344 | tf_op jit(solution)/shard_map/ppermute | solution.py:251
  55.3 2.0 %collective-permute-start.4 = (bf16[288,512]{1,0:T(8,128)(2,1)}, bf16[288,512]{1,0:T(8,128)(2,1)}, u32[]{:S(2)}, u32[]{:S(2)}) collective-permute-start(bf16[288,512]{1,0:T(8,128)(2,1)} %copy-done.1), channel_id=1, source_target_pairs={{0,64},{1,969},{64,128},{65,1},{128,192},{129,65},{192,256},{193,1... | collective-permute-start | bytes 884744 | tf_op jit(solution)/shard_map/ppermute | solution.py:248
  57.4 6.0 %collective-permute-start.5 = (bf16[288,512]{1,0:T(8,128)(2,1)}, bf16[288,512]{1,0:T(8,128)(2,1)}, u32[]{:S(2)}, u32[]{:S(2)}) collective-permute-start(bf16[288,512]{1,0:T(8,128)(2,1)} %collective-permute-done.2.items_ref), channel_id=1, source_target_pairs={{0,64},{1,969},{64,128},{65,1},{128,192},{129,65},{192,256},{193,1... | collective-permute-start | bytes 884744 | tf_op jit(solution)/shard_map/ppermute | solution.py:249
  63.9 0.1 stack.71.base_ref
  64.3 1.0 copy-done.2
  65.2 2.0 %shard_map.78 = (f32[1,256]{1,0:T(1,128)S(1)}, f32[8,2048]{1,0:T(8,128)S(1)}) custom-call(s32[5]{0:T(128)S(1)} %stack.71.base_ref, bf16[288,512]{1,0:T(8,128)(2,1)S(1)} %copy-done.2, bf16[1088,512]{1,0:T(8,128)(2,1)S(1)} %bitcast.56, bf16[1088,512]{1,0:T(8,128)(2,1)S(1)} %collective-permute-done.3.refs_1_), custom_call_target="tpu_custom_call" | custom-call | flops 536870912 | bytes 4194304 | tf_op jit(solution)/shard_map/pallas_call | solution.py:169
  67.2 2.4 %shard_map.79 = (f32[1,256]{1,0:T(1,128)S(1)}, f32[8,2048]{1,0:T(8,128)S(1)}) custom-call(s32[5]{0:T(128)S(1)} %stack.76.base_ref, bf16[288,512]{1,0:T(8,128)(2,1)} %collective-permute-done.4.items_ref, bf16[1088,512]{1,0:T(8,128)(2,1)S(1)} %bitcast.57, bf16[1088,512]{1,0:T(8,128)(2,1)S(1)} %collective-permute-done.3.refs_1_, ...), custom_call_target="tpu_custom_call" | custom-call | flops 536870912 | bytes 4194304 | tf_op jit(solution)/shard_map/pallas_call | solution.py:169
  69.6 2.4 %shard_map.80 = (f32[1,256]{1,0:T(1,128)S(1)}, f32[8,2048]{1,0:T(8,128)S(1)}) custom-call(s32[5]{0:T(128)S(1)} %stack.81.base_ref, bf16[288,512]{1,0:T(8,128)(2,1)} %collective-permute-done.2.items_ref, bf16[1088,512]{1,0:T(8,128)(2,1)S(1)} %bitcast.58, bf16[1088,512]{1,0:T(8,128)(2,1)S(1)} %collective-permute-done.3.refs_1_, ...), custom_call_target="tpu_custom_call" | custom-call | flops 536870912 | bytes 4194304 | tf_op jit(solution)/shard_map/pallas_call | solution.py:169
  72.0 3.1 %shard_map.81 = (f32[1,256]{1,0:T(1,128)S(1)}, f32[256,128]{1,0:T(8,128)}) custom-call(s32[5]{0:T(128)S(1)} %stack.86.base_ref, bf16[288,512]{1,0:T(8,128)(2,1)} %collective-permute-done.5.items_ref, bf16[1088,512]{1,0:T(8,128)(2,1)S(1)} %bitcast.59, bf16[1088,512]{1,0:T(8,128)(2,1)S(1)} %collective-permute-done.3.refs_1_, ...), custom_call_target="tpu_custom_call" | custom-call | flops 536870912 | bytes 4194304 | tf_op jit(solution)/shard_map/pallas_call | solution.py:169
  75.1 1.9 %collective-permute-start.6 = (f32[4,128]{1,0:T(4,128)S(1)}, f32[4,128]{1,0:T(4,128)S(1)}, u32[]{:S(2)}, u32[]{:S(2)}) collective-permute-start(f32[4,128]{1,0:T(4,128)S(1)} %slice.64), channel_id=1, source_target_pairs={{0,776},{1,257},{64,840},{65,321},{128,904},{129,385},{192,968},{1... | collective-permute-start | bytes 6152 | tf_op jit(solution)/shard_map/ppermute | solution.py:277
  77.0 11.9 %all-to-all-start.1 = ((f32[32,8,128]{2,1,0:T(8,128)}), f32[32,8,128]{2,1,0:T(8,128)S(1)}, u32[]{:S(2)}, u32[]{:S(2)}) async-start(f32[32,8,128]{2,1,0:T(8,128)} %bitcast.23), calls=%async_computation.1 | async-start | bytes 262144 | tf_op jit(solution)/shard_map/all_to_all | solution.py:276
  89.0 1.9 %collective-permute-start.7 = (f32[2,128]{1,0:T(2,128)S(1)}, f32[2,128]{1,0:T(2,128)S(1)}, u32[]{:S(2)}, u32[]{:S(2)}) collective-permute-start(f32[2,128]{1,0:T(2,128)S(1)} %slice.51), channel_id=1, source_target_pairs={{0,904},{1,129},{64,968},{65,193},{128,0},{129,257},{192,64},{193,... | collective-permute-start | bytes 3080 | tf_op jit(solution)/shard_map/ppermute | solution.py:284
  90.9 5.7 %all-to-all-done.1 = f32[32,8,128]{2,1,0:T(8,128)S(1)} async-done(((f32[32,8,128]{2,1,0:T(8,128)}), f32[32,8,128]{2,1,0:T(8,128)S(1)}, u32[]{:S(2)}, u32[]{:S(2)}) %all-to-all-start.1) | async-done | bytes 131104 | tf_op jit(solution)/shard_map/all_to_all | solution.py:276
  96.7 10.9 %collective-permute-start.9 = (f32[8,128]{1,0:T(8,128)S(1)}, f32[8,128]{1,0:T(8,128)S(1)}, u32[]{:S(2)}, u32[]{:S(2)}) collective-permute-start(f32[8,128]{1,0:T(8,128)S(1)} %pad_maximum_fusion.1), channel_id=1, source_target_pairs={{0,8},{8,0},{1,9},{9,1},{2,10},{10,2},{3,11},{11,3},{4,12},{12,4},... | collective-permute-start | bytes 12296 | tf_op jit(solution)/shard_map/ppermute | solution.py:285
  107.7 3.3 %collective-permute-start.8 = (f32[64]{0:T(128)S(1)}, f32[64]{0:T(128)S(1)}, u32[]{:S(2)}, u32[]{:S(2)}) collective-permute-start(f32[64]{0:T(128)S(1)} %get-tuple-element.40), channel_id=1, source_target_pairs={{0,968},{1,65},{64,0},{65,129},{128,64},{129,193},{192,128},{193,2... | collective-permute-start | bytes 776 | tf_op jit(solution)/shard_map/ppermute | solution.py:288
  111.0 2.8 %collective-permute-start.10 = (f32[64]{0:T(128)S(1)}, f32[64]{0:T(128)S(1)}, u32[]{:S(2)}, u32[]{:S(2)}) collective-permute-start(f32[64]{0:T(128)S(1)} %get-tuple-element.38), channel_id=1, source_target_pairs={{0,969},{1,64},{64,1},{65,128},{128,65},{129,192},{192,129},{193,2... | collective-permute-start | bytes 776 | tf_op jit(solution)/shard_map/ppermute | solution.py:289
  113.8 3.5 %collective-permute-start.11 = (f32[64]{0:T(128)S(1)}, f32[64]{0:T(128)S(1)}, u32[]{:S(2)}, u32[]{:S(2)}) collective-permute-start(f32[64]{0:T(128)S(1)} %get-tuple-element.39), channel_id=1, source_target_pairs={{0,905},{1,128},{64,969},{65,192},{128,1},{129,256},{192,65},{193,... | collective-permute-start | bytes 776 | tf_op jit(solution)/shard_map/ppermute | solution.py:290
  117.4 2.0 %collective-permute-done.9 = f32[8,128]{1,0:T(8,128)S(1)} collective-permute-done((f32[8,128]{1,0:T(8,128)S(1)}, f32[8,128]{1,0:T(8,128)S(1)}, u32[]{:S(2)}, u32[]{:S(2)}) %collective-permute-start.9) | collective-permute-done | bytes 4128 | tf_op jit(solution)/shard_map/ppermute | solution.py:285
  119.4 0.6 add_subtract_fusion
  120.0 0.5 log_add_fusion.3
  (43 shorter events, 0.9 us)
Async XLA Ops:
  0.6 1.3 %copy-start = (bf16[1024,512]{1,0:T(8,128)(2,1)S(1)}, bf16[1024,512]{1,0:T(8,128)(2,1)}, u32[]{:S(2)}) copy-start(bf16[1024,512]{1,0:T(8,128)(2,1)} %param.8) | copy-start | bytes 3145732
  0.6 9.5 %copy-start.4 = (s32[512]{0:T(512)S(1)}, s32[512]{0:T(512)}, u32[]{:S(2)}) copy-start(s32[512]{0:T(512)} %param.11) | copy-start | bytes 6148
  0.7 31.0 %copy-start.3 = (bf16[512,512]{1,0:T(8,128)(2,1)S(1)}, bf16[512,512]{1,0:T(8,128)(2,1)}, u32[]{:S(2)}) copy-start(bf16[512,512]{1,0:T(8,128)(2,1)} %param.10) | copy-start | bytes 1572868
  5.2 7.0 %collective-permute-start = (bf16[72,512]{1,0:T(8,128)(2,1)S(1)}, bf16[72,512]{1,0:T(8,128)(2,1)S(1)}, u32[]{:S(2)}, u32[]{:S(2)}) collective-permute-start(bf16[72,512]{1,0:T(8,128)(2,1)S(1)} %fusion.10), channel_id=1, source_target_pairs={{0,969},{1,64},{64,1},{65,128},{128,65},{129,192},{192,129},{193,2... | collective-permute-start | bytes 221192 | tf_op jit(solution)/shard_map/ppermute | solution.py:229
  12.4 26.1 %collective-permute-start.1 = (bf16[144,512]{1,0:T(8,128)(2,1)S(1)}, bf16[144,512]{1,0:T(8,128)(2,1)S(1)}, u32[]{:S(2)}, u32[]{:S(2)}) collective-permute-start(bf16[144,512]{1,0:T(8,128)(2,1)S(1)} %fusion.7.near_ref), channel_id=1, source_target_pairs={{0,256},{1,777},{64,320},{65,841},{128,384},{129,905},{192,448},{1... | collective-permute-start | bytes 442376 | tf_op jit(solution)/shard_map/ppermute | solution.py:243
  32.8 18.7 %all-to-all-start = ((bf16[4,272,512]{2,1,0:T(8,128)(2,1)}), bf16[4,272,512]{2,1,0:T(8,128)(2,1)S(1)}, u32[]{:S(2)}, u32[]{:S(2)}) async-start(bf16[4,272,512]{2,1,0:T(8,128)(2,1)} %tile.2), calls=%async_computation | async-start | bytes 2228224 | tf_op jit(solution)/shard_map/all_to_all | solution.py:245
  38.5 13.1 %copy-start.1 = (bf16[288,512]{1,0:T(8,128)(2,1)}, bf16[288,512]{1,0:T(8,128)(2,1)S(1)}, u32[]{:S(2)}) copy-start(bf16[288,512]{1,0:T(8,128)(2,1)S(1)} %shard_map.77.items_ref) | copy-start | bytes 884740
  38.5 11.3 %collective-permute-start.2 = (bf16[288,512]{1,0:T(8,128)(2,1)S(1)}, bf16[288,512]{1,0:T(8,128)(2,1)}, u32[]{:S(2)}, u32[]{:S(2)}) collective-permute-start(bf16[288,512]{1,0:T(8,128)(2,1)S(1)} %shard_map.77.items_ref), channel_id=1, source_target_pairs={{0,128},{1,905},{64,192},{65,969},{128,256},{129,1},{192,320},{193... | collective-permute-start | bytes 884744 | tf_op jit(solution)/shard_map/ppermute | solution.py:247
  51.6 12.7 %collective-permute-start.3 = (bf16[1088,512]{1,0:T(8,128)(2,1)S(1)}, bf16[1088,512]{1,0:T(8,128)(2,1)S(1)}, u32[]{:S(2)}, u32[]{:S(2)}) collective-permute-start(bf16[1088,512]{1,0:T(8,128)(2,1)S(1)} %bitcast.55), channel_id=1, source_target_pairs={{0,1},{1,0},{2,3},{3,2},{4,5},{5,4},{6,7},{7,6},{8,9},{9,8},{10,11... | collective-permute-start | bytes 3342344 | tf_op jit(solution)/shard_map/ppermute | solution.py:251
  55.3 11.9 %collective-permute-start.4 = (bf16[288,512]{1,0:T(8,128)(2,1)}, bf16[288,512]{1,0:T(8,128)(2,1)}, u32[]{:S(2)}, u32[]{:S(2)}) collective-permute-start(bf16[288,512]{1,0:T(8,128)(2,1)} %copy-done.1), channel_id=1, source_target_pairs={{0,64},{1,969},{64,128},{65,1},{128,192},{129,65},{192,256},{193,1... | collective-permute-start | bytes 884744 | tf_op jit(solution)/shard_map/ppermute | solution.py:248
  57.4 14.6 %collective-permute-start.5 = (bf16[288,512]{1,0:T(8,128)(2,1)}, bf16[288,512]{1,0:T(8,128)(2,1)}, u32[]{:S(2)}, u32[]{:S(2)}) collective-permute-start(bf16[288,512]{1,0:T(8,128)(2,1)} %collective-permute-done.2.items_ref), channel_id=1, source_target_pairs={{0,64},{1,969},{64,128},{65,1},{128,192},{129,65},{192,256},{193,1... | collective-permute-start | bytes 884744 | tf_op jit(solution)/shard_map/ppermute | solution.py:249
  64.3 1.0 copy-start.2
  75.1 13.9 %collective-permute-start.6 = (f32[4,128]{1,0:T(4,128)S(1)}, f32[4,128]{1,0:T(4,128)S(1)}, u32[]{:S(2)}, u32[]{:S(2)}) collective-permute-start(f32[4,128]{1,0:T(4,128)S(1)} %slice.64), channel_id=1, source_target_pairs={{0,776},{1,257},{64,840},{65,321},{128,904},{129,385},{192,968},{1... | collective-permute-start | bytes 6152 | tf_op jit(solution)/shard_map/ppermute | solution.py:277
  77.0 19.6 %all-to-all-start.1 = ((f32[32,8,128]{2,1,0:T(8,128)}), f32[32,8,128]{2,1,0:T(8,128)S(1)}, u32[]{:S(2)}, u32[]{:S(2)}) async-start(f32[32,8,128]{2,1,0:T(8,128)} %bitcast.23), calls=%async_computation.1 | async-start | bytes 262144 | tf_op jit(solution)/shard_map/all_to_all | solution.py:276
  89.0 18.6 %collective-permute-start.7 = (f32[2,128]{1,0:T(2,128)S(1)}, f32[2,128]{1,0:T(2,128)S(1)}, u32[]{:S(2)}, u32[]{:S(2)}) collective-permute-start(f32[2,128]{1,0:T(2,128)S(1)} %slice.51), channel_id=1, source_target_pairs={{0,904},{1,129},{64,968},{65,193},{128,0},{129,257},{192,64},{193,... | collective-permute-start | bytes 3080 | tf_op jit(solution)/shard_map/ppermute | solution.py:284
  96.7 22.7 %collective-permute-start.9 = (f32[8,128]{1,0:T(8,128)S(1)}, f32[8,128]{1,0:T(8,128)S(1)}, u32[]{:S(2)}, u32[]{:S(2)}) collective-permute-start(f32[8,128]{1,0:T(8,128)S(1)} %pad_maximum_fusion.1), channel_id=1, source_target_pairs={{0,8},{8,0},{1,9},{9,1},{2,10},{10,2},{3,11},{11,3},{4,12},{12,4},... | collective-permute-start | bytes 12296 | tf_op jit(solution)/shard_map/ppermute | solution.py:285
  107.7 12.3 %collective-permute-start.8 = (f32[64]{0:T(128)S(1)}, f32[64]{0:T(128)S(1)}, u32[]{:S(2)}, u32[]{:S(2)}) collective-permute-start(f32[64]{0:T(128)S(1)} %get-tuple-element.40), channel_id=1, source_target_pairs={{0,968},{1,65},{64,0},{65,129},{128,64},{129,193},{192,128},{193,2... | collective-permute-start | bytes 776 | tf_op jit(solution)/shard_map/ppermute | solution.py:288
  111.0 9.0 %collective-permute-start.10 = (f32[64]{0:T(128)S(1)}, f32[64]{0:T(128)S(1)}, u32[]{:S(2)}, u32[]{:S(2)}) collective-permute-start(f32[64]{0:T(128)S(1)} %get-tuple-element.38), channel_id=1, source_target_pairs={{0,969},{1,64},{64,1},{65,128},{128,65},{129,192},{192,129},{193,2... | collective-permute-start | bytes 776 | tf_op jit(solution)/shard_map/ppermute | solution.py:289
  113.8 6.2 %collective-permute-start.11 = (f32[64]{0:T(128)S(1)}, f32[64]{0:T(128)S(1)}, u32[]{:S(2)}, u32[]{:S(2)}) collective-permute-start(f32[64]{0:T(128)S(1)} %get-tuple-element.39), channel_id=1, source_target_pairs={{0,905},{1,128},{64,969},{65,192},{128,1},{129,256},{192,65},{193,... | collective-permute-start | bytes 776 | tf_op jit(solution)/shard_map/ppermute | solution.py:290

commit v4 on v3

--- a/solution.py
+++ b/solution.py
@@ -25,7 +25,10 @@
 SEGMENT = 256
 EXTRA = 16
 TEMP = 4.0 / math.sqrt(DEPTH)
-LOG2E = 1.0 / math.log(2.0)
+LN2 = math.log(2.0)
+LOG2E = 1.0 / LN2
+CALLS = ((0, 1, 2), (3,))
+GROUPS = ((0, 1, 2, 3), (4, 5, 6, 7))
 CHUNK = 32
 
 
@@ -55,99 +58,99 @@
     return high, (values - high.astype(F32)).astype(BF16)
 
 
-def score_kernel(first, last, base_ref, items_ref, *refs):
-    mine_ref, other_ref, *refs = refs
+def score_kernel(first, last, count, base_ref, *refs):
+    items_refs, (mine_ref, other_ref, *refs) = refs[:count], refs[count:]
     rows = SEGMENT + EXTRA
     segments = [(ref, y * rows) for y in range(Y) for ref in (mine_ref, other_ref)]
     past_ref = None if first else refs.pop(0)
     item_ref, row_ref, scores, weight, ids, top_item, sum_item = refs
-    for half in range(2):
-        start = half * (HALF + EXTRA) + HALF
-        extra = items_ref[start : start + EXTRA, 0:256].astype(F32)
-        row = (extra[0:1, 0:128] + extra[0:1, 128:256]) * (1.0 / TEMP)
+    halves = [(ref, half * (HALF + EXTRA)) for ref in items_refs for half in range(2)]
+    for half, (items_ref, start) in enumerate(halves):
+        extra = items_ref[start + HALF : start + HALF + EXTRA, 0:256].astype(F32)
+        row = (extra[0:1, 0:128] + extra[0:1, 128:256]) * LOG2E
         weight[HALF * half : HALF * (half + 1), :] = jnp.broadcast_to(row, (HALF, 128)).T
     spot = lax.broadcasted_iota(jnp.int32, (BLOCK, 128), 0)
-    for part in range(PARTS):
+    for part in range(PARTS * count):
         ids[part * BLOCK : (part + 1) * BLOCK, :] = (spot + base_ref[part]).astype(F32)
 
-    chunks = [slice(g, g + CHUNK) for g in range(0, ITEMS, CHUNK)]
-    tiles = [slice(k, k + 128) for k in range(0, SEGMENT, 128)]
-    items = jnp.concatenate(
-        [items_ref[0:HALF, :], items_ref[HALF + EXTRA : 2 * HALF + EXTRA, :]], axis=0
-    )
-    tops, positives = [], []
-    for s, (users_ref, start) in enumerate(segments):
-        raw = lax.dot_general(
-            items,
-            users_ref[start : start + SEGMENT, :],
-            (((1,), (1,)), ((), ())),
-            preferred_element_type=F32,
-        )
-        index_rows = users_ref[start + SEGMENT : start + rows, 0:SEGMENT].astype(F32)
-        wanted = index_rows[0:1, :] * 256.0 + index_rows[1:2, :]
-        top_s, positive_s = [], []
-        for k in tiles:
-            top, positive = None, None
-            for g in chunks:
-                piece = raw[g, k]
-                scores[g, s * SEGMENT + k.start : s * SEGMENT + k.stop] = piece
-                if s == 0 and k.start == 0:
-                    top_item[g, :] = piece
-                else:
-                    top_item[g, :] = jnp.maximum(top_item[g, :], piece)
-                logits = piece + weight[g, :]
-                found = jnp.where(ids[g, :] == wanted[:, k], logits, 0.0)
-                shape = (CHUNK // 8, 8, 128)
-                part_top = jnp.max(logits.reshape(shape), axis=0)
-                part_positive = jnp.sum(found.reshape(shape), axis=0)
-                top = part_top if top is None else jnp.maximum(top, part_top)
-                positive = part_positive if positive is None else positive + part_positive
-            top_s.append(jnp.max(top, axis=0, keepdims=True))
-            positive_s.append(jnp.sum(positive, axis=0, keepdims=True))
-        tops.append(top_s)
-        positives.append(positive_s)
+    chunks = [slice(g, g + CHUNK) for g in range(0, ITEMS * count, CHUNK)]
+    shape = (CHUNK // 8, 8, 128)
+    items = jnp.concatenate([ref[start : start + HALF, :] for ref, start in halves], axis=0)
+    tops, positives = {}, {}
+    tiles_of = [
+        [s * SEGMENT + k for s in group for k in range(0, SEGMENT, 128)]
+        for group in GROUPS
+    ]
+    for group, tiles in zip(GROUPS, tiles_of):
+        wanted = {}
+        for s in group:
+            users_ref, start = segments[s]
+            scores[:, s * SEGMENT : (s + 1) * SEGMENT] = lax.dot_general(
+                items,
+                users_ref[start : start + SEGMENT, :],
+                (((1,), (1,)), ((), ())),
+                preferred_element_type=F32,
+            ) * (TEMP * LOG2E)
+            index_rows = users_ref[start + SEGMENT : start + rows, 0:SEGMENT].astype(F32)
+            spots = index_rows[0:1, :] * 256.0 + index_rows[1:2, :]
+            for k in range(0, SEGMENT, 128):
+                wanted[s * SEGMENT + k] = jnp.broadcast_to(spots[:, k : k + 128], (8, 128))
+        for g in chunks:
+            best, heavy, known = None, weight[g, :].reshape(shape), ids[g, :].reshape(shape)
+            if group != GROUPS[0]:
+                best = top_item[g, :].reshape(shape)
+            for k in tiles:
+                piece = scores[g, k : k + 128].reshape(shape)
+                best = piece if best is None else jnp.maximum(best, piece)
+                logits = piece + heavy
+                top = jnp.max(logits, axis=0)
+                positive = jnp.sum(jnp.where(known == wanted[k], logits, 0.0), axis=0)
+                tops[k] = jnp.maximum(tops[k], top) if k in tops else top
+                positives[k] = positives[k] + positive if k in positives else positive
+            top_item[g, :] = best.reshape(CHUNK, 128)
 
     for g in chunks:
         top_item[g, :] = jnp.broadcast_to(
             jnp.max(top_item[g, :], axis=1, keepdims=True), (CHUNK, 128)
         )
     ready = []
-    for s in range(len(segments)):
-        for t, k in enumerate(tiles):
-            place = slice(s * SEGMENT + k.start, s * SEGMENT + k.stop)
-            top, positive = tops[s][t], positives[s][t]
+    for group, tiles in zip(GROUPS, tiles_of):
+        level, totals = {}, {}
+        for k in tiles:
+            level[k] = jnp.max(tops[k], axis=0, keepdims=True)
             if not first:
-                old_top = past_ref[0:1, place]
-                top = jnp.maximum(old_top, top)
-                positive = positive + past_ref[2:3, place]
-            total = None
-            for g in chunks:
-                piece = scores[g, place]
-                by_item = jnp.exp2((piece - top_item[g, :]) * (TEMP * LOG2E))
-                if s == 0 and t == 0:
-                    sum_item[g, :] = by_item
-                else:
-                    sum_item[g, :] = sum_item[g, :] + by_item
-                by_user = jnp.exp2((piece + weight[g, :] - top) * (TEMP * LOG2E))
-                part = jnp.sum(by_user.reshape(CHUNK // 8, 8, 128), axis=0)
-                total = part if total is None else total + part
-            total = jnp.sum(total, axis=0, keepdims=True)
+                level[k] = jnp.maximum(past_ref[0:1, k : k + 128], level[k])
+            level[k] = jnp.broadcast_to(level[k], (8, 128))
+        for g in chunks:
+            best, heavy = top_item[g, :].reshape(shape), weight[g, :].reshape(shape)
+            amount = None if group == GROUPS[0] else sum_item[g, :].reshape(shape)
+            for k in tiles:
+                piece = scores[g, k : k + 128].reshape(shape)
+                by_item = jnp.exp2(piece - best)
+                amount = by_item if amount is None else amount + by_item
+                part = jnp.sum(jnp.exp2(piece + heavy - level[k]), axis=0)
+                totals[k] = totals[k] + part if k in totals else part
+            sum_item[g, :] = amount.reshape(CHUNK, 128)
+        for k in tiles:
+            top = level[k][0:1, :]
+            total = jnp.sum(totals[k], axis=0, keepdims=True)
+            positive = jnp.sum(positives[k], axis=0, keepdims=True)
             if not first:
-                total = total + past_ref[1:2, place] * jnp.exp2((old_top - top) * (TEMP * LOG2E))
+                total = total + past_ref[1:2, k : k + 128] * jnp.exp2(past_ref[0:1, k : k + 128] - top)
+                positive = positive + past_ref[2:3, k : k + 128]
             if last:
-                lse = top * TEMP + jnp.log(total)
-                ready.append((lse, positive * TEMP))
+                ready.append((top * LN2 + jnp.log(total), positive * LN2))
             else:
-                row_ref[0:1, place] = top
-                row_ref[1:2, place] = total
-                row_ref[2:3, place] = positive
+                row_ref[0:1, k : k + 128] = top
+                row_ref[1:2, k : k + 128] = total
+                row_ref[2:3, k : k + 128] = positive
     if last:
         for y in range(Y):
             straight = ready[4 * y : 4 * y + 4]
             turned = straight[2:] + straight[:2]
             tile = jnp.concatenate(
                 [
-                    jnp.where(base_ref[PARTS] == 0, straight[t][kind], turned[t][kind])
+                    jnp.where(base_ref[PARTS * count] == 0, straight[t][kind], turned[t][kind])
                     for kind in range(2)
                     for t in range(4)
                 ],
@@ -155,37 +158,38 @@
             )
             for peer in range(8):
                 row_ref[(y * 8 + peer) * 8 : (y * 8 + peer + 1) * 8, :] = tile
-    for half in range(2):
+    for half in range(2 * count):
         g = slice(128 * half, 128 * half + 128)
         total = jnp.broadcast_to(jnp.sum(sum_item[g, :], axis=1, keepdims=True), (128, 128))
-        lse = top_item[g, :] * TEMP + jnp.log(total)
+        lse = top_item[g, :] * LN2 + jnp.log(total)
         item_ref[0:1, g] = lse.T[0:1, :]
 
 
 def score_call(first, last, bases, items, users, past):
     vmem = pl.BlockSpec(memory_space=pltpu.VMEM)
-    operands = (bases, items, *users) + (() if first else (past,))
+    count = len(items)
+    operands = (bases, *items, *users) + (() if first else (past,))
     row_shape = (32 * 8, 128) if last else (8, Y * USERS)
     return pl.pallas_call(
-        functools.partial(score_kernel, first, last),
+        functools.partial(score_kernel, first, last, count),
         out_shape=(
-            jax.ShapeDtypeStruct((1, ITEMS), F32),
+            jax.ShapeDtypeStruct((1, ITEMS * count), F32),
             jax.ShapeDtypeStruct(row_shape, F32),
         ),
         in_specs=[pl.BlockSpec(memory_space=pltpu.SMEM)] + [vmem] * (len(operands) - 1),
         out_specs=(vmem, vmem),
         scratch_shapes=[
-            pltpu.VMEM((ITEMS, Y * USERS), F32),
-            pltpu.VMEM((ITEMS, 128), F32),
-            pltpu.VMEM((ITEMS, 128), F32),
-            pltpu.VMEM((ITEMS, 128), F32),
-            pltpu.VMEM((ITEMS, 128), F32),
+            pltpu.VMEM((ITEMS * count, Y * USERS), F32),
+            pltpu.VMEM((ITEMS * count, 128), F32),
+            pltpu.VMEM((ITEMS * count, 128), F32),
+            pltpu.VMEM((ITEMS * count, 128), F32),
+            pltpu.VMEM((ITEMS * count, 128), F32),
         ],
-        compiler_params=pltpu.CompilerParams(vmem_limit_bytes=12 * 1024 * 1024),
+        compiler_params=pltpu.CompilerParams(vmem_limit_bytes=20 * 1024 * 1024),
         cost_estimate=pl.CostEstimate(
-            flops=2 * ITEMS * Y * USERS * DEPTH,
+            flops=2 * ITEMS * count * Y * USERS * DEPTH,
             bytes_accessed=4 * 1024 * 1024,
-            transcendentals=2 * ITEMS * Y * USERS,
+            transcendentals=2 * ITEMS * count * Y * USERS,
         ),
     )(*operands)
 
@@ -246,6 +250,7 @@
     pair = stack_call(near, far)
     two_on = lax.ppermute(pair, ZC, along(2))
     one_on = lax.ppermute(pair, ZC, along(1))
+    one_on, two_on = lax.optimization_barrier((one_on, two_on))
     three_on = lax.ppermute(two_on, ZC, along(1))
     mine, two_here = lax.optimization_barrier((mine, two_on))
     users = [mine, lax.ppermute(mine, "c", [(0, 1), (1, 0)])]
@@ -260,17 +265,20 @@
 
     way = jnp.where(c == 0, -1, 1)
     columns, past = [], None
-    for step in range(4):
+    for steps in CALLS:
         bases = jnp.stack(
             [
                 base(z + way * (step + more + cross), jnp.where(cross == 0, c, 1 - c))
+                for step in steps
                 for more in (0, 4)
                 for cross in (0, 1)
             ]
             + [c]
         ).astype(jnp.int32)
-        column, past = score_call(step == 0, step == 3, bases, groups[step], users, past)
-        columns.append(column)
+        column, past = score_call(
+            steps[0] == 0, steps[-1] == 3, bases, [groups[step] for step in steps], users, past
+        )
+        columns.append(column.reshape(len(steps), ITEMS))
 
     stacked = jnp.concatenate(columns, axis=0)
     plane = lax.all_to_all(past, PLANE, 0, 0, tiled=True).reshape(32, 8, 128)

time: 121 us -> 122 us (level)
  waiting for transfers between devices: 19.8 us -> 15.8 us
  starting transfers between devices: 80.8 us -> 84.7 us
  local copies, waits for them, and re-layouts: 2.99 us -> 5.22 us
  Pallas kernels: 9.82 us -> 8.47 us
    ppermute x1, starting transfers between devices: 5.99 us -> 2.01 us  [on_device(): three_on = lax.ppermute(two_on, ZC, along(1))]
    ppermute x1, starting transfers between devices: 3.75 us -> 7.15 us  [on_device(): users = [mine, lax.ppermute(mine, 'c', [(0, 1), (1, 0)])]]
    unnamed x11 -> x15, local copies, waits for them, and re-layouts: 1.35 us -> 3.74 us
    ppermute x1, waiting for transfers between devices: 6.97 us -> 4.94 us  [on_device(): two_on = lax.ppermute(pair, ZC, along(2))]
    all_to_all x1, waiting for transfers between devices: 1.75 us -> 0.01 us  [on_device(): mine = lax.all_to_all(jnp.tile(half, (Y, 1)), 'y', 0, 0, tiled=True)]
    ppermute x1, starting transfers between devices: 2.03 us -> 3.62 us  [on_device(): one_on = lax.ppermute(pair, ZC, along(1))]
    pallas_call x4 -> x2, Pallas kernels: 9.8 us -> 8.45 us  [score_call(): pl.pallas_call(functools.partial(score_kernel, first, last, count), out_s...]
  transfers between devices with their start and end apart: 14 -> 14, of which waited for: 6 -> 6; matrix products, arithmetic and copies ran while one was open for 2% -> 2% of each run, Pallas kernels for 6% -> 4%
where the time goes in v4:
time: 122 us; the launch traced here: 121 us
  starting transfers between devices  84.7 us (69%)
  waiting for transfers between devices  15.8 us (13%)
  Pallas kernels  8.47 us (7%)
  local copies, waits for them, and re-layouts  5.22 us (4%)
  matrix products  3.3 us (3%)
  other arithmetic  2.33 us (2%)
  between operations  1.51 us (1%)
    ppermute x1, starting transfers between devices, on_device(): far = lax.ppermute(near, ZC, along(4))  19.3 us
    all_to_all x1, starting transfers between devices, on_device(): plane = lax.all_to_all(past, PLANE, 0, 0, tiled=True).reshape(32, 8, 128)  13.1 us
    ppermute x1, starting transfers between devices, on_device(): other = lax.ppermute(mine, 'zh', [(0, 1), (1, 0)])  11.3 us
    pallas_call x2, Pallas kernels, score_call(): pl.pallas_call(functools.partial(score_kernel, first, last, count), out_s...  8.45 us
    ppermute x1, starting transfers between devices, on_device(): users = [mine, lax.ppermute(mine, 'c', [(0, 1), (1, 0)])]  7.15 us
    all_to_all x1, waiting for transfers between devices, on_device(): plane = lax.all_to_all(past, PLANE, 0, 0, tiled=True).reshape(32, 8, 128)  5.65 us
    ppermute x1, waiting for transfers between devices, on_device(): two_on = lax.ppermute(pair, ZC, along(2))  4.94 us
    ppermute x1, starting transfers between devices, on_device(): came = lax.ppermute(sent, ZC, across(1))  4.94 us
  transfers between devices with their start and end apart: 14, of which 6 were waited for; matrix products, arithmetic and copies ran while one was open for 2% of the time, Pallas kernels for 4%

profile of v4, /device:TPU:1, one launch (start us, length us, event | category | flops | bytes accessed | tf_op | source)
XLA Modules:
  0.0 121.3 jit_solution(17782620699532915111)
XLA Ops:
  0.7 0.8 fusion.24
  1.5 0.4 copy-done
  1.9 3.3 %fusion.2 = bf16[64,512]{1,0:T(8,128)(2,1)S(1)} fusion(bf16[1024,512]{1,0:T(8,128)(2,1)S(1)} %copy-done, bf16[64,2048]{1,0:T(8,128)(2,1)} %param.6, bf16[2048,1024]{1,0:T(8,128)(2,1)} %param.7), kind=kOutput, calls=%fused_computation.3 | convolution fusion | flops 335708160 | bytes 5570560 | tf_op jit(solution)/shard_map/dot_general | solution.py:223
  5.2 4.9 %collective-permute-start = (bf16[72,512]{1,0:T(8,128)(2,1)S(1)}, bf16[72,512]{1,0:T(8,128)(2,1)S(1)}, u32[]{:S(2)}, u32[]{:S(2)}) collective-permute-start(bf16[72,512]{1,0:T(8,128)(2,1)S(1)} %fusion.10), channel_id=1, source_target_pairs={{0,969},{1,64},{64,1},{65,128},{128,65},{129,192},{192,129},{193,2... | collective-permute-start | bytes 221192 | tf_op jit(solution)/shard_map/ppermute | solution.py:233
  10.2 2.0 %collective-permute-done = bf16[72,512]{1,0:T(8,128)(2,1)S(1)} collective-permute-done((bf16[72,512]{1,0:T(8,128)(2,1)S(1)}, bf16[72,512]{1,0:T(8,128)(2,1)S(1)}, u32[]{:S(2)}, u32[]{:S(2)}) %collective-permute-start) | collective-permute-done | bytes 73760 | tf_op jit(solution)/shard_map/ppermute | solution.py:233
  12.4 19.3 %collective-permute-start.1 = (bf16[144,512]{1,0:T(8,128)(2,1)S(1)}, bf16[144,512]{1,0:T(8,128)(2,1)S(1)}, u32[]{:S(2)}, u32[]{:S(2)}) collective-permute-start(bf16[144,512]{1,0:T(8,128)(2,1)S(1)} %fusion.7.near_ref), channel_id=1, source_target_pairs={{0,256},{1,777},{64,320},{65,841},{128,384},{129,905},{192,448},{1... | collective-permute-start | bytes 442376 | tf_op jit(solution)/shard_map/ppermute | solution.py:247
  31.7 1.1 tile.2
  32.8 4.2 %all-to-all-start = ((bf16[4,272,512]{2,1,0:T(8,128)(2,1)}), bf16[4,272,512]{2,1,0:T(8,128)(2,1)S(1)}, u32[]{:S(2)}, u32[]{:S(2)}) async-start(bf16[4,272,512]{2,1,0:T(8,128)(2,1)} %tile.2), calls=%async_computation | async-start | bytes 2228224 | tf_op jit(solution)/shard_map/all_to_all | solution.py:249
  37.0 1.4 %collective-permute-done.1.far_ref = bf16[144,512]{1,0:T(8,128)(2,1)S(1)} collective-permute-done((bf16[144,512]{1,0:T(8,128)(2,1)S(1)}, bf16[144,512]{1,0:T(8,128)(2,1)S(1)}, u32[]{:S(2)}, u32[]{:S(2)}) %collective-permute-start.1) | collective-permute-done | bytes 147488 | tf_op jit(solution)/shard_map/ppermute | solution.py:247
  38.5 3.6 %collective-permute-start.2 = (bf16[288,512]{1,0:T(8,128)(2,1)S(1)}, bf16[288,512]{1,0:T(8,128)(2,1)S(1)}, u32[]{:S(2)}, u32[]{:S(2)}) collective-permute-start(bf16[288,512]{1,0:T(8,128)(2,1)S(1)} %shard_map.77.refs_0_), channel_id=1, source_target_pairs={{0,64},{1,969},{64,128},{65,1},{128,192},{129,65},{192,256},{193,1... | collective-permute-start | bytes 884744 | tf_op jit(solution)/shard_map/ppermute | solution.py:252
  42.1 4.7 %collective-permute-start.3 = (bf16[288,512]{1,0:T(8,128)(2,1)S(1)}, bf16[288,512]{1,0:T(8,128)(2,1)}, u32[]{:S(2)}, u32[]{:S(2)}) collective-permute-start(bf16[288,512]{1,0:T(8,128)(2,1)S(1)} %shard_map.77.refs_0_), channel_id=1, source_target_pairs={{0,128},{1,905},{64,192},{65,969},{128,256},{129,1},{192,320},{193... | collective-permute-start | bytes 884744 | tf_op jit(solution)/shard_map/ppermute | solution.py:251
  46.9 0.7 copy-done.1
  47.6 0.7 copy-done.3
  48.3 4.9 %collective-permute-done.3.refs_2_ = bf16[288,512]{1,0:T(8,128)(2,1)} collective-permute-done((bf16[288,512]{1,0:T(8,128)(2,1)S(1)}, bf16[288,512]{1,0:T(8,128)(2,1)}, u32[]{:S(2)}, u32[]{:S(2)}) %collective-permute-start.3) | collective-permute-done | bytes 294944 | tf_op jit(solution)/shard_map/ppermute | solution.py:251
  53.3 7.2 %collective-permute-start.4 = (bf16[1088,512]{1,0:T(8,128)(2,1)S(1)}, bf16[1088,512]{1,0:T(8,128)(2,1)S(1)}, u32[]{:S(2)}, u32[]{:S(2)}) collective-permute-start(bf16[1088,512]{1,0:T(8,128)(2,1)S(1)} %bitcast.55), channel_id=1, source_target_pairs={{0,1},{1,0},{2,3},{3,2},{4,5},{5,4},{6,7},{7,6},{8,9},{9,8},{10,11... | collective-permute-start | bytes 3342344 | tf_op jit(solution)/shard_map/ppermute | solution.py:256
  60.4 2.0 %collective-permute-start.5 = (bf16[288,512]{1,0:T(8,128)(2,1)}, bf16[288,512]{1,0:T(8,128)(2,1)}, u32[]{:S(2)}, u32[]{:S(2)}) collective-permute-start(bf16[288,512]{1,0:T(8,128)(2,1)} %collective-permute-done.3.refs_2_), channel_id=1, source_target_pairs={{0,64},{1,969},{64,128},{65,1},{128,192},{129,65},{192,256},{193,1... | collective-permute-start | bytes 884744 | tf_op jit(solution)/shard_map/ppermute | solution.py:254
  63.2 1.0 copy-done.2
  64.2 1.0 copy-done.4
  65.1 5.2 %shard_map.78 = (f32[1,768]{1,0:T(1,128)S(1)}, f32[8,2048]{1,0:T(8,128)S(1)}) custom-call(s32[13]{0:T(128)S(1)} %stack.71.base_ref, bf16[288,512]{1,0:T(8,128)(2,1)S(1)} %copy-done.2, bf16[288,512]{1,0:T(8,128)(2,1)S(1)} %copy-done.4, bf16[288,512]{1,0:T(8,128)(2,1)} %collective-permute-done.3.refs_2_, bf16[1088,512]{1,0:T(8,128)(2,1)S(1)} %bitcast.56, ...), custom_call_target="tpu_custom_call" | custom-call | flops 1610612736 | bytes 4194304 | tf_op jit(solution)/shard_map/pallas_call | solution.py:173
  70.4 3.2 %shard_map.79 = (f32[1,256]{1,0:T(1,128)S(1)}, f32[256,128]{1,0:T(8,128)}) custom-call(s32[5]{0:T(128)S(1)} %stack.76.base_ref, bf16[288,512]{1,0:T(8,128)(2,1)} %collective-permute-done.5.refs_0_, bf16[1088,512]{1,0:T(8,128)(2,1)S(1)} %bitcast.57, bf16[1088,512]{1,0:T(8,128)(2,1)S(1)} %collective-permute-done.4.refs_4_.refs_2_, ...), custom_call_target="tpu_custom_call" | custom-call | flops 536870912 | bytes 4194304 | tf_op jit(solution)/shard_map/pallas_call | solution.py:173
  73.6 2.6 %collective-permute-start.6 = (f32[4,128]{1,0:T(4,128)S(1)}, f32[4,128]{1,0:T(4,128)S(1)}, u32[]{:S(2)}, u32[]{:S(2)}) collective-permute-start(f32[4,128]{1,0:T(4,128)S(1)} %pad_maximum_fusion.1), channel_id=1, source_target_pairs={{0,776},{1,257},{64,840},{65,321},{128,904},{129,385},{192,968},{1... | collective-permute-start | bytes 6152 | tf_op jit(solution)/shard_map/ppermute | solution.py:285
  76.3 13.1 %all-to-all-start.1 = ((f32[32,8,128]{2,1,0:T(8,128)}), f32[32,8,128]{2,1,0:T(8,128)S(1)}, u32[]{:S(2)}, u32[]{:S(2)}) async-start(f32[32,8,128]{2,1,0:T(8,128)} %bitcast.23), calls=%async_computation.1 | async-start | bytes 262144 | tf_op jit(solution)/shard_map/all_to_all | solution.py:284
  89.4 1.9 %collective-permute-start.7 = (f32[2,128]{1,0:T(2,128)S(1)}, f32[2,128]{1,0:T(2,128)S(1)}, u32[]{:S(2)}, u32[]{:S(2)}) collective-permute-start(f32[2,128]{1,0:T(2,128)S(1)} %slice.51), channel_id=1, source_target_pairs={{0,904},{1,129},{64,968},{65,193},{128,0},{129,257},{192,64},{193,... | collective-permute-start | bytes 3080 | tf_op jit(solution)/shard_map/ppermute | solution.py:292
  91.3 5.7 %all-to-all-done.1 = f32[32,8,128]{2,1,0:T(8,128)S(1)} async-done(((f32[32,8,128]{2,1,0:T(8,128)}), f32[32,8,128]{2,1,0:T(8,128)S(1)}, u32[]{:S(2)}, u32[]{:S(2)}) %all-to-all-start.1) | async-done | bytes 131104 | tf_op jit(solution)/shard_map/all_to_all | solution.py:284
  97.1 11.3 %collective-permute-start.9 = (f32[8,128]{1,0:T(8,128)S(1)}, f32[8,128]{1,0:T(8,128)S(1)}, u32[]{:S(2)}, u32[]{:S(2)}) collective-permute-start(f32[8,128]{1,0:T(8,128)S(1)} %pad_maximum_fusion), channel_id=1, source_target_pairs={{0,8},{8,0},{1,9},{9,1},{2,10},{10,2},{3,11},{11,3},{4,12},{12,4},... | collective-permute-start | bytes 12296 | tf_op jit(solution)/shard_map/ppermute | solution.py:293
  108.6 3.1 %collective-permute-start.8 = (f32[64]{0:T(128)S(1)}, f32[64]{0:T(128)S(1)}, u32[]{:S(2)}, u32[]{:S(2)}) collective-permute-start(f32[64]{0:T(128)S(1)} %get-tuple-element.36), channel_id=1, source_target_pairs={{0,968},{1,65},{64,0},{65,129},{128,64},{129,193},{192,128},{193,2... | collective-permute-start | bytes 776 | tf_op jit(solution)/shard_map/ppermute | solution.py:296
  111.7 3.0 %collective-permute-start.10 = (f32[64]{0:T(128)S(1)}, f32[64]{0:T(128)S(1)}, u32[]{:S(2)}, u32[]{:S(2)}) collective-permute-start(f32[64]{0:T(128)S(1)} %get-tuple-element.34), channel_id=1, source_target_pairs={{0,969},{1,64},{64,1},{65,128},{128,65},{129,192},{192,129},{193,2... | collective-permute-start | bytes 776 | tf_op jit(solution)/shard_map/ppermute | solution.py:297
  114.7 3.7 %collective-permute-start.11 = (f32[64]{0:T(128)S(1)}, f32[64]{0:T(128)S(1)}, u32[]{:S(2)}, u32[]{:S(2)}) collective-permute-start(f32[64]{0:T(128)S(1)} %get-tuple-element.35), channel_id=1, source_target_pairs={{0,905},{1,128},{64,969},{65,192},{128,1},{129,256},{192,65},{193,... | collective-permute-start | bytes 776 | tf_op jit(solution)/shard_map/ppermute | solution.py:298
  118.4 1.4 %collective-permute-done.9 = f32[8,128]{1,0:T(8,128)S(1)} collective-permute-done((f32[8,128]{1,0:T(8,128)S(1)}, f32[8,128]{1,0:T(8,128)S(1)}, u32[]{:S(2)}, u32[]{:S(2)}) %collective-permute-start.9) | collective-permute-done | bytes 4128 | tf_op jit(solution)/shard_map/ppermute | solution.py:293
  119.8 0.6 add_subtract_fusion
  120.4 0.4 collective-permute-done.11
  120.8 0.5 log_add_fusion.3
  (44 shorter events, 0.9 us)
Async XLA Ops:
  0.6 1.3 %copy-start = (bf16[1024,512]{1,0:T(8,128)(2,1)S(1)}, bf16[1024,512]{1,0:T(8,128)(2,1)}, u32[]{:S(2)}) copy-start(bf16[1024,512]{1,0:T(8,128)(2,1)} %param.8) | copy-start | bytes 3145732
  0.6 9.5 %copy-start.6 = (s32[512]{0:T(512)S(1)}, s32[512]{0:T(512)}, u32[]{:S(2)}) copy-start(s32[512]{0:T(512)} %param.11) | copy-start | bytes 6148
  0.7 31.0 %copy-start.5 = (bf16[512,512]{1,0:T(8,128)(2,1)S(1)}, bf16[512,512]{1,0:T(8,128)(2,1)}, u32[]{:S(2)}) copy-start(bf16[512,512]{1,0:T(8,128)(2,1)} %param.10) | copy-start | bytes 1572868
  5.2 7.0 %collective-permute-start = (bf16[72,512]{1,0:T(8,128)(2,1)S(1)}, bf16[72,512]{1,0:T(8,128)(2,1)S(1)}, u32[]{:S(2)}, u32[]{:S(2)}) collective-permute-start(bf16[72,512]{1,0:T(8,128)(2,1)S(1)} %fusion.10), channel_id=1, source_target_pairs={{0,969},{1,64},{64,1},{65,128},{128,65},{129,192},{192,129},{193,2... | collective-permute-start | bytes 221192 | tf_op jit(solution)/shard_map/ppermute | solution.py:233
  12.4 26.1 %collective-permute-start.1 = (bf16[144,512]{1,0:T(8,128)(2,1)S(1)}, bf16[144,512]{1,0:T(8,128)(2,1)S(1)}, u32[]{:S(2)}, u32[]{:S(2)}) collective-permute-start(bf16[144,512]{1,0:T(8,128)(2,1)S(1)} %fusion.7.near_ref), channel_id=1, source_target_pairs={{0,256},{1,777},{64,320},{65,841},{128,384},{129,905},{192,448},{1... | collective-permute-start | bytes 442376 | tf_op jit(solution)/shard_map/ppermute | solution.py:247
  32.8 20.4 %all-to-all-start = ((bf16[4,272,512]{2,1,0:T(8,128)(2,1)}), bf16[4,272,512]{2,1,0:T(8,128)(2,1)S(1)}, u32[]{:S(2)}, u32[]{:S(2)}) async-start(bf16[4,272,512]{2,1,0:T(8,128)(2,1)} %tile.2), calls=%async_computation | async-start | bytes 2228224 | tf_op jit(solution)/shard_map/all_to_all | solution.py:249
  38.5 9.1 %collective-permute-start.2 = (bf16[288,512]{1,0:T(8,128)(2,1)S(1)}, bf16[288,512]{1,0:T(8,128)(2,1)S(1)}, u32[]{:S(2)}, u32[]{:S(2)}) collective-permute-start(bf16[288,512]{1,0:T(8,128)(2,1)S(1)} %shard_map.77.refs_0_), channel_id=1, source_target_pairs={{0,64},{1,969},{64,128},{65,1},{128,192},{129,65},{192,256},{193,1... | collective-permute-start | bytes 884744 | tf_op jit(solution)/shard_map/ppermute | solution.py:252
  42.1 11.1 %collective-permute-start.3 = (bf16[288,512]{1,0:T(8,128)(2,1)S(1)}, bf16[288,512]{1,0:T(8,128)(2,1)}, u32[]{:S(2)}, u32[]{:S(2)}) collective-permute-start(bf16[288,512]{1,0:T(8,128)(2,1)S(1)} %shard_map.77.refs_0_), channel_id=1, source_target_pairs={{0,128},{1,905},{64,192},{65,969},{128,256},{129,1},{192,320},{193... | collective-permute-start | bytes 884744 | tf_op jit(solution)/shard_map/ppermute | solution.py:251
  46.9 0.7 copy-start.1
  47.6 0.7 copy-start.3
  53.3 9.9 %collective-permute-start.4 = (bf16[1088,512]{1,0:T(8,128)(2,1)S(1)}, bf16[1088,512]{1,0:T(8,128)(2,1)S(1)}, u32[]{:S(2)}, u32[]{:S(2)}) collective-permute-start(bf16[1088,512]{1,0:T(8,128)(2,1)S(1)} %bitcast.55), channel_id=1, source_target_pairs={{0,1},{1,0},{2,3},{3,2},{4,5},{5,4},{6,7},{7,6},{8,9},{9,8},{10,11... | collective-permute-start | bytes 3342344 | tf_op jit(solution)/shard_map/ppermute | solution.py:256
  60.4 10.0 %collective-permute-start.5 = (bf16[288,512]{1,0:T(8,128)(2,1)}, bf16[288,512]{1,0:T(8,128)(2,1)}, u32[]{:S(2)}, u32[]{:S(2)}) collective-permute-start(bf16[288,512]{1,0:T(8,128)(2,1)} %collective-permute-done.3.refs_2_), channel_id=1, source_target_pairs={{0,64},{1,969},{64,128},{65,1},{128,192},{129,65},{192,256},{193,1... | collective-permute-start | bytes 884744 | tf_op jit(solution)/shard_map/ppermute | solution.py:254
  63.2 1.0 copy-start.2
  64.2 1.0 copy-start.4
  73.6 15.7 %collective-permute-start.6 = (f32[4,128]{1,0:T(4,128)S(1)}, f32[4,128]{1,0:T(4,128)S(1)}, u32[]{:S(2)}, u32[]{:S(2)}) collective-permute-start(f32[4,128]{1,0:T(4,128)S(1)} %pad_maximum_fusion.1), channel_id=1, source_target_pairs={{0,776},{1,257},{64,840},{65,321},{128,904},{129,385},{192,968},{1... | collective-permute-start | bytes 6152 | tf_op jit(solution)/shard_map/ppermute | solution.py:285
  76.3 20.7 %all-to-all-start.1 = ((f32[32,8,128]{2,1,0:T(8,128)}), f32[32,8,128]{2,1,0:T(8,128)S(1)}, u32[]{:S(2)}, u32[]{:S(2)}) async-start(f32[32,8,128]{2,1,0:T(8,128)} %bitcast.23), calls=%async_computation.1 | async-start | bytes 262144 | tf_op jit(solution)/shard_map/all_to_all | solution.py:284
  89.4 19.1 %collective-permute-start.7 = (f32[2,128]{1,0:T(2,128)S(1)}, f32[2,128]{1,0:T(2,128)S(1)}, u32[]{:S(2)}, u32[]{:S(2)}) collective-permute-start(f32[2,128]{1,0:T(2,128)S(1)} %slice.51), channel_id=1, source_target_pairs={{0,904},{1,129},{64,968},{65,193},{128,0},{129,257},{192,64},{193,... | collective-permute-start | bytes 3080 | tf_op jit(solution)/shard_map/ppermute | solution.py:292
  97.1 22.7 %collective-permute-start.9 = (f32[8,128]{1,0:T(8,128)S(1)}, f32[8,128]{1,0:T(8,128)S(1)}, u32[]{:S(2)}, u32[]{:S(2)}) collective-permute-start(f32[8,128]{1,0:T(8,128)S(1)} %pad_maximum_fusion), channel_id=1, source_target_pairs={{0,8},{8,0},{1,9},{9,1},{2,10},{10,2},{3,11},{11,3},{4,12},{12,4},... | collective-permute-start | bytes 12296 | tf_op jit(solution)/shard_map/ppermute | solution.py:293
  108.6 11.8 %collective-permute-start.8 = (f32[64]{0:T(128)S(1)}, f32[64]{0:T(128)S(1)}, u32[]{:S(2)}, u32[]{:S(2)}) collective-permute-start(f32[64]{0:T(128)S(1)} %get-tuple-element.36), channel_id=1, source_target_pairs={{0,968},{1,65},{64,0},{65,129},{128,64},{129,193},{192,128},{193,2... | collective-permute-start | bytes 776 | tf_op jit(solution)/shard_map/ppermute | solution.py:296
  111.7 8.7 %collective-permute-start.10 = (f32[64]{0:T(128)S(1)}, f32[64]{0:T(128)S(1)}, u32[]{:S(2)}, u32[]{:S(2)}) collective-permute-start(f32[64]{0:T(128)S(1)} %get-tuple-element.34), channel_id=1, source_target_pairs={{0,969},{1,64},{64,1},{65,128},{128,65},{129,192},{192,129},{193,2... | collective-permute-start | bytes 776 | tf_op jit(solution)/shard_map/ppermute | solution.py:297
  114.7 6.1 %collective-permute-start.11 = (f32[64]{0:T(128)S(1)}, f32[64]{0:T(128)S(1)}, u32[]{:S(2)}, u32[]{:S(2)}) collective-permute-start(f32[64]{0:T(128)S(1)} %get-tuple-element.35), channel_id=1, source_target_pairs={{0,905},{1,128},{64,969},{65,192},{128,1},{129,256},{192,65},{193,... | collective-permute-start | bytes 776 | tf_op jit(solution)/shard_map/ppermute | solution.py:298

commit v5 on v4

--- a/solution.py
+++ b/solution.py
@@ -27,7 +27,6 @@
 TEMP = 4.0 / math.sqrt(DEPTH)
 LN2 = math.log(2.0)
 LOG2E = 1.0 / LN2
-CALLS = ((0, 1, 2), (3,))
 GROUPS = ((0, 1, 2, 3), (4, 5, 6, 7))
 CHUNK = 32
 
@@ -59,13 +58,12 @@
 
 
 def score_kernel(first, last, count, base_ref, *refs):
-    items_refs, (mine_ref, other_ref, *refs) = refs[:count], refs[count:]
-    rows = SEGMENT + EXTRA
-    segments = [(ref, y * rows) for y in range(Y) for ref in (mine_ref, other_ref)]
+    items_ref, users_ref, *refs = refs
+    segments = [(y * (USERS + EXTRA), k) for y in range(Y) for k in (0, SEGMENT)]
     past_ref = None if first else refs.pop(0)
     item_ref, row_ref, scores, weight, ids, top_item, sum_item = refs
-    halves = [(ref, half * (HALF + EXTRA)) for ref in items_refs for half in range(2)]
-    for half, (items_ref, start) in enumerate(halves):
+    halves = [half * (HALF + EXTRA) for half in range(2 * count)]
+    for half, start in enumerate(halves):
         extra = items_ref[start + HALF : start + HALF + EXTRA, 0:256].astype(F32)
         row = (extra[0:1, 0:128] + extra[0:1, 128:256]) * LOG2E
         weight[HALF * half : HALF * (half + 1), :] = jnp.broadcast_to(row, (HALF, 128)).T
@@ -75,7 +73,7 @@
 
     chunks = [slice(g, g + CHUNK) for g in range(0, ITEMS * count, CHUNK)]
     shape = (CHUNK // 8, 8, 128)
-    items = jnp.concatenate([ref[start : start + HALF, :] for ref, start in halves], axis=0)
+    items = jnp.concatenate([items_ref[start : start + HALF, :] for start in halves], axis=0)
     tops, positives = {}, {}
     tiles_of = [
         [s * SEGMENT + k for s in group for k in range(0, SEGMENT, 128)]
@@ -84,14 +82,14 @@
     for group, tiles in zip(GROUPS, tiles_of):
         wanted = {}
         for s in group:
-            users_ref, start = segments[s]
+            start, part = segments[s]
             scores[:, s * SEGMENT : (s + 1) * SEGMENT] = lax.dot_general(
                 items,
-                users_ref[start : start + SEGMENT, :],
+                users_ref[start + part : start + part + SEGMENT, :],
                 (((1,), (1,)), ((), ())),
                 preferred_element_type=F32,
             ) * (TEMP * LOG2E)
-            index_rows = users_ref[start + SEGMENT : start + rows, 0:SEGMENT].astype(F32)
+            index_rows = users_ref[start + USERS : start + USERS + EXTRA, part : part + SEGMENT].astype(F32)
             spots = index_rows[0:1, :] * 256.0 + index_rows[1:2, :]
             for k in range(0, SEGMENT, 128):
                 wanted[s * SEGMENT + k] = jnp.broadcast_to(spots[:, k : k + 128], (8, 128))
@@ -146,16 +144,8 @@
                 row_ref[2:3, k : k + 128] = positive
     if last:
         for y in range(Y):
-            straight = ready[4 * y : 4 * y + 4]
-            turned = straight[2:] + straight[:2]
-            tile = jnp.concatenate(
-                [
-                    jnp.where(base_ref[PARTS * count] == 0, straight[t][kind], turned[t][kind])
-                    for kind in range(2)
-                    for t in range(4)
-                ],
-                axis=0,
-            )
+            quarters = ready[4 * y : 4 * y + 4]
+            tile = jnp.concatenate([lse for lse, _ in quarters] + [pos for _, pos in quarters], axis=0)
             for peer in range(8):
                 row_ref[(y * 8 + peer) * 8 : (y * 8 + peer + 1) * 8, :] = tile
     for half in range(2 * count):
@@ -165,10 +155,9 @@
         item_ref[0:1, g] = lse.T[0:1, :]
 
 
-def score_call(first, last, bases, items, users, past):
+def score_call(first, last, count, bases, items, users, past):
     vmem = pl.BlockSpec(memory_space=pltpu.VMEM)
-    count = len(items)
-    operands = (bases, *items, *users) + (() if first else (past,))
+    operands = (bases, items, users) + (() if first else (past,))
     row_shape = (32 * 8, 128) if last else (8, Y * USERS)
     return pl.pallas_call(
         functools.partial(score_kernel, first, last, count),
@@ -194,21 +183,22 @@
     )(*operands)
 
 
-def stack_kernel(near_ref, far_ref, pair_ref):
-    pair_ref[0 : HALF + EXTRA, :] = near_ref[...]
-    pair_ref[HALF + EXTRA :, :] = far_ref[...]
-
-
-def stack_call(near, far):
+def stack_kernel(first_ref, second_ref, both_ref):
+    rows = first_ref.shape[0]
+    both_ref[0:rows, :] = first_ref[...]
+    both_ref[rows:, :] = second_ref[...]
+
+
+def stack_call(first, second, flops):
     vmem = pl.BlockSpec(memory_space=pltpu.VMEM)
     return pl.pallas_call(
         stack_kernel,
-        out_shape=jax.ShapeDtypeStruct((2 * (HALF + EXTRA), DEPTH), BF16),
+        out_shape=jax.ShapeDtypeStruct((2 * first.shape[0], DEPTH), BF16),
         in_specs=[vmem, vmem],
         out_specs=vmem,
         compiler_params=pltpu.CompilerParams(vmem_limit_bytes=4 * 1024 * 1024),
-        cost_estimate=pl.CostEstimate(flops=60 * 10**9, bytes_accessed=600_000, transcendentals=0),
-    )(near, far)
+        cost_estimate=pl.CostEstimate(flops=flops, bytes_accessed=600_000, transcendentals=0),
+    )(first, second)
 
 
 def join(*parts):
@@ -236,25 +226,17 @@
     )
     near = jnp.concatenate([embedded, came[0:BLOCK], rows(weights, EXTRA)], axis=0)
 
-    high = (positive_index // 256).astype(BF16).reshape(2, 1, SEGMENT)
-    low = (positive_index % 256).astype(BF16).reshape(2, 1, SEGMENT)
-    index_rows = jnp.pad(
-        jnp.concatenate([high, low], axis=1), ((0, 0), (0, EXTRA - 2), (0, DEPTH - SEGMENT))
-    )
-    own = jnp.concatenate([user_vectors.reshape(2, SEGMENT, DEPTH), index_rows], axis=1)
-    half = lax.dynamic_index_in_dim(own, c, 0, keepdims=False)
+    high = (positive_index // 256).astype(BF16)
+    low = (positive_index % 256).astype(BF16)
+    index_rows = jnp.pad(jnp.stack([high, low]), ((0, EXTRA - 2), (0, 0)))
+    own = jnp.concatenate([user_vectors, index_rows], axis=0)
 
     far = lax.ppermute(near, ZC, along(4))
-    half, near = lax.optimization_barrier((half, near))
-    mine = lax.all_to_all(jnp.tile(half, (Y, 1)), "y", 0, 0, tiled=True)
-    pair = stack_call(near, far)
-    two_on = lax.ppermute(pair, ZC, along(2))
-    one_on = lax.ppermute(pair, ZC, along(1))
-    one_on, two_on = lax.optimization_barrier((one_on, two_on))
-    three_on = lax.ppermute(two_on, ZC, along(1))
-    mine, two_here = lax.optimization_barrier((mine, two_on))
-    users = [mine, lax.ppermute(mine, "c", [(0, 1), (1, 0)])]
-    groups = [pair, one_on, two_here, three_on]
+    own, near = lax.optimization_barrier((own, near))
+    users = lax.all_to_all(jnp.tile(own, (Y, 1)), "y", 0, 0, tiled=True)
+    pair = stack_call(near, far, 60 * 10**9)
+    evens = stack_call(pair, lax.ppermute(pair, ZC, along(2)), 10**6)
+    odds = lax.ppermute(evens, ZC, along(1))
 
     z = zh * 16 + zl
 
@@ -265,7 +247,7 @@
 
     way = jnp.where(c == 0, -1, 1)
     columns, past = [], None
-    for steps in CALLS:
+    for steps, items in (((0, 2), evens), ((1, 3), odds)):
         bases = jnp.stack(
             [
                 base(z + way * (step + more + cross), jnp.where(cross == 0, c, 1 - c))
@@ -273,14 +255,11 @@
                 for more in (0, 4)
                 for cross in (0, 1)
             ]
-            + [c]
         ).astype(jnp.int32)
-        column, past = score_call(
-            steps[0] == 0, steps[-1] == 3, bases, [groups[step] for step in steps], users, past
-        )
-        columns.append(column.reshape(len(steps), ITEMS))
-
-    stacked = jnp.concatenate(columns, axis=0)
+        column, past = score_call(steps[0] == 0, steps[-1] == 3, 2, bases, items, users, past)
+        columns.append(column)
+
+    stacked = jnp.stack([column[0, k : k + ITEMS] for k in (0, ITEMS) for column in columns])
     plane = lax.all_to_all(past, PLANE, 0, 0, tiled=True).reshape(32, 8, 128)
     came4 = lax.ppermute(stacked[:, HALF:], ZC, along(-4))
 

time: 122 us -> 120 us (0.984)
  starting transfers between devices: 84.7 us -> 74.3 us
  waiting for transfers between devices: 15.8 us -> 26.1 us
  local copies, waits for them, and re-layouts: 5.22 us -> 2.24 us
  Pallas kernels: 8.47 us -> 9.71 us
    ppermute x4 -> x2, starting transfers between devices: 17.5 us -> 9.72 us  [the longest x1 5.38 us: on_device(): odds = lax.ppermute(evens, ZC, along(1))]
    all_to_all x1, waiting for transfers between devices: 0.01 us -> 5.68 us  [on_device(): users = lax.all_to_all(jnp.tile(own, (Y, 1)), 'y', 0, 0, tiled=True)]
    unnamed x15 -> x6, local copies, waits for them, and re-layouts: 3.74 us -> 0.37 us
    ppermute x1, waiting for transfers between devices: 1.38 us -> 4.42 us  [on_device(): other = lax.ppermute(mine, 'zh', [(0, 1), (1, 0)])]
    ppermute x4 -> x2, waiting for transfers between devices: 4.94 us -> 7.28 us  [the longest x1 7.28 us: on_device(): evens = stack_call(pair, lax.ppermute(pair, ZC, along(2)), 10 ** 6)]
    ppermute x1, starting transfers between devices: 11.3 us -> 9.72 us  [on_device(): other = lax.ppermute(mine, 'zh', [(0, 1), (1, 0)])]
    ppermute x1, starting transfers between devices: 3.7 us -> 2.27 us  [on_device(): cross_two = lax.ppermute(two[1, BLOCK:], ZC, across(2))]
  transfers between devices with their start and end apart: 14 -> 12, of which waited for: 6 -> 6; matrix products, arithmetic and copies ran while one was open for 2% -> 2% of each run, Pallas kernels for 4% -> 4%
where the time goes in v5:
time: 120 us; the launch traced here: 119 us
  starting transfers between devices  74.3 us (62%)
  waiting for transfers between devices  26.1 us (22%)
  Pallas kernels  9.71 us (8%)
  matrix products  3.3 us (3%)
  other arithmetic  2.32 us (2%)
  local copies, waits for them, and re-layouts  2.24 us (2%)
  between operations  1.5 us (1%)
    ppermute x1, starting transfers between devices, on_device(): far = lax.ppermute(near, ZC, along(4))  19.3 us
    all_to_all x1, starting transfers between devices, on_device(): plane = lax.all_to_all(past, PLANE, 0, 0, tiled=True).reshape(32, 8, 128)  14.2 us
    ppermute x1, starting transfers between devices, on_device(): other = lax.ppermute(mine, 'zh', [(0, 1), (1, 0)])  9.72 us
    pallas_call x2, Pallas kernels, score_call(): pl.pallas_call(functools.partial(score_kernel, first, last, count), out_s...  8.83 us
    ppermute x1, waiting for transfers between devices, on_device(): evens = stack_call(pair, lax.ppermute(pair, ZC, along(2)), 10 ** 6)  7.28 us
    all_to_all x1, waiting for transfers between devices, on_device(): users = lax.all_to_all(jnp.tile(own, (Y, 1)), 'y', 0, 0, tiled=True)  5.68 us
    all_to_all x1, waiting for transfers between devices, on_device(): plane = lax.all_to_all(past, PLANE, 0, 0, tiled=True).reshape(32, 8, 128)  5.66 us
    ppermute x1, starting transfers between devices, on_device(): odds = lax.ppermute(evens, ZC, along(1))  5.38 us
  transfers between devices with their start and end apart: 12, of which 6 were waited for; matrix products, arithmetic and copies ran while one was open for 2% of the time, Pallas kernels for 4%

profile of v5, /device:TPU:1, one launch (start us, length us, event | category | flops | bytes accessed | tf_op | source)
XLA Modules:
  0.0 119.4 jit_solution(14574382287233022977)
XLA Ops:
  0.7 0.8 fusion.25
  1.5 0.1 maximum_bitcast_fusion
  1.5 0.4 copy-done
  1.9 3.3 %fusion.2 = bf16[64,512]{1,0:T(8,128)(2,1)S(1)} fusion(bf16[1024,512]{1,0:T(8,128)(2,1)S(1)} %copy-done, bf16[64,2048]{1,0:T(8,128)(2,1)} %param.6, bf16[2048,1024]{1,0:T(8,128)(2,1)} %param.7), kind=kOutput, calls=%fused_computation.3 | convolution fusion | flops 335708160 | bytes 5570560 | tf_op jit(solution)/shard_map/dot_general | solution.py:213
  5.2 4.9 %collective-permute-start = (bf16[72,512]{1,0:T(8,128)(2,1)S(1)}, bf16[72,512]{1,0:T(8,128)(2,1)S(1)}, u32[]{:S(2)}, u32[]{:S(2)}) collective-permute-start(bf16[72,512]{1,0:T(8,128)(2,1)S(1)} %fusion.7), channel_id=1, source_target_pairs={{0,969},{1,64},{64,1},{65,128},{128,65},{129,192},{192,129},{193,2... | collective-permute-start | bytes 221192 | tf_op jit(solution)/shard_map/ppermute | solution.py:223
  10.2 2.0 %collective-permute-done = bf16[72,512]{1,0:T(8,128)(2,1)S(1)} collective-permute-done((bf16[72,512]{1,0:T(8,128)(2,1)S(1)}, bf16[72,512]{1,0:T(8,128)(2,1)S(1)}, u32[]{:S(2)}, u32[]{:S(2)}) %collective-permute-start) | collective-permute-done | bytes 73760 | tf_op jit(solution)/shard_map/ppermute | solution.py:223
  12.3 0.1 pad_maximum_fusion.3
  12.4 19.3 %collective-permute-start.1 = (bf16[144,512]{1,0:T(8,128)(2,1)S(1)}, bf16[144,512]{1,0:T(8,128)(2,1)S(1)}, u32[]{:S(2)}, u32[]{:S(2)}) collective-permute-start(bf16[144,512]{1,0:T(8,128)(2,1)S(1)} %fusion.4.first_ref), channel_id=1, source_target_pairs={{0,256},{1,777},{64,320},{65,841},{128,384},{129,905},{192,448},{1... | collective-permute-start | bytes 442376 | tf_op jit(solution)/shard_map/ppermute | solution.py:234
  31.7 1.5 %tile.2 = bf16[4,528,512]{2,1,0:T(8,128)(2,1)} broadcast(bf16[528,512]{1,0:T(8,128)(2,1)S(1)} %pad_maximum_fusion), dimensions={1,2} | broadcast | bytes 2703360 | tf_op jit(solution)/shard_map/tile | solution.py:236
  33.2 4.2 %all-to-all-start = ((bf16[4,528,512]{2,1,0:T(8,128)(2,1)}), bf16[4,528,512]{2,1,0:T(8,128)(2,1)S(1)}, u32[]{:S(2)}, u32[]{:S(2)}) async-start(bf16[4,528,512]{2,1,0:T(8,128)(2,1)} %tile.2), calls=%async_computation | async-start | bytes 4325376 | tf_op jit(solution)/shard_map/all_to_all | solution.py:236
  37.4 1.0 collective-permute-done.1.second_ref
  38.5 4.3 %collective-permute-start.2 = (bf16[288,512]{1,0:T(8,128)(2,1)S(1)}, bf16[288,512]{1,0:T(8,128)(2,1)S(1)}, u32[]{:S(2)}, u32[]{:S(2)}) collective-permute-start(bf16[288,512]{1,0:T(8,128)(2,1)S(1)} %shard_map.77.first_ref), channel_id=1, source_target_pairs={{0,128},{1,905},{64,192},{65,969},{128,256},{129,1},{192,320},{193... | collective-permute-start | bytes 884744 | tf_op jit(solution)/shard_map/ppermute | solution.py:238
  42.8 7.3 %collective-permute-done.2.second_ref = bf16[288,512]{1,0:T(8,128)(2,1)S(1)} collective-permute-done((bf16[288,512]{1,0:T(8,128)(2,1)S(1)}, bf16[288,512]{1,0:T(8,128)(2,1)S(1)}, u32[]{:S(2)}, u32[]{:S(2)}) %collective-permute-start.2) | collective-permute-done | bytes 294944 | tf_op jit(solution)/shard_map/ppermute | solution.py:238
  50.1 0.9 shard_map.78.refs_0_
  51.0 5.4 %collective-permute-start.3 = (bf16[576,512]{1,0:T(8,128)(2,1)}, bf16[576,512]{1,0:T(8,128)(2,1)}, u32[]{:S(2)}, u32[]{:S(2)}) collective-permute-start(bf16[576,512]{1,0:T(8,128)(2,1)} %shard_map.78.refs_0_), channel_id=1, source_target_pairs={{0,64},{1,969},{64,128},{65,1},{128,192},{129,65},{192,256},{193,1... | collective-permute-start | bytes 1769480 | tf_op jit(solution)/shard_map/ppermute | solution.py:239
  57.0 0.1 stack.74.base_ref
  57.0 0.1 stack.86.base_ref
  57.1 5.7 %all-to-all-done = bf16[4,528,512]{2,1,0:T(8,128)(2,1)S(1)} async-done(((bf16[4,528,512]{2,1,0:T(8,128)(2,1)}), bf16[4,528,512]{2,1,0:T(8,128)(2,1)S(1)}, u32[]{:S(2)}, u32[]{:S(2)}) %all-to-all-start) | async-done | bytes 2162720 | tf_op jit(solution)/shard_map/all_to_all | solution.py:236
  62.8 4.1 %shard_map.79 = (f32[1,512]{1,0:T(1,128)S(1)}, f32[8,2048]{1,0:T(8,128)S(1)}) custom-call(s32[8]{0:T(128)S(1)} %stack.74.base_ref, bf16[576,512]{1,0:T(8,128)(2,1)} %shard_map.78.refs_0_, bf16[2112,512]{1,0:T(8,128)(2,1)S(1)} %bitcast.51), custom_call_target="tpu_custom_call" | custom-call | flops 1073741824 | bytes 4194304 | tf_op jit(solution)/shard_map/pallas_call | solution.py:162
  66.9 4.7 %shard_map.80 = (f32[1,512]{1,0:T(1,128)S(1)}, f32[256,128]{1,0:T(8,128)}) custom-call(s32[8]{0:T(128)S(1)} %stack.86.base_ref, bf16[576,512]{1,0:T(8,128)(2,1)} %collective-permute-done.3.refs_0_, bf16[2112,512]{1,0:T(8,128)(2,1)S(1)} %bitcast.52, f32[8,2048]{1,0:T(8,128)S(1)} %get-tuple-element.14.refs_2_), custom_call_target="tpu_custom_call" | custom-call | flops 1073741824 | bytes 4194304 | tf_op jit(solution)/shard_map/pallas_call | solution.py:162
  71.7 1.9 %collective-permute-start.4 = (f32[4,128]{1,0:T(4,128)S(1)}, f32[4,128]{1,0:T(4,128)S(1)}, u32[]{:S(2)}, u32[]{:S(2)}) collective-permute-start(f32[4,128]{1,0:T(4,128)S(1)} %slice.80), channel_id=1, source_target_pairs={{0,776},{1,257},{64,840},{65,321},{128,904},{129,385},{192,968},{1... | collective-permute-start | bytes 6152 | tf_op jit(solution)/shard_map/ppermute | solution.py:264
  73.6 14.2 %all-to-all-start.1 = ((f32[32,8,128]{2,1,0:T(8,128)}), f32[32,8,128]{2,1,0:T(8,128)S(1)}, u32[]{:S(2)}, u32[]{:S(2)}) async-start(f32[32,8,128]{2,1,0:T(8,128)} %bitcast.20), calls=%async_computation.1 | async-start | bytes 262144 | tf_op jit(solution)/shard_map/all_to_all | solution.py:263
  87.9 1.9 %collective-permute-start.5 = (f32[2,128]{1,0:T(2,128)S(1)}, f32[2,128]{1,0:T(2,128)S(1)}, u32[]{:S(2)}, u32[]{:S(2)}) collective-permute-start(f32[2,128]{1,0:T(2,128)S(1)} %slice.67), channel_id=1, source_target_pairs={{0,904},{1,129},{64,968},{65,193},{128,0},{129,257},{192,64},{193,... | collective-permute-start | bytes 3080 | tf_op jit(solution)/shard_map/ppermute | solution.py:271
  89.8 5.7 %all-to-all-done.1 = f32[32,8,128]{2,1,0:T(8,128)S(1)} async-done(((f32[32,8,128]{2,1,0:T(8,128)}), f32[32,8,128]{2,1,0:T(8,128)S(1)}, u32[]{:S(2)}, u32[]{:S(2)}) %all-to-all-start.1) | async-done | bytes 131104 | tf_op jit(solution)/shard_map/all_to_all | solution.py:263
  95.6 9.7 %collective-permute-start.7 = (f32[8,128]{1,0:T(8,128)S(1)}, f32[8,128]{1,0:T(8,128)S(1)}, u32[]{:S(2)}, u32[]{:S(2)}) collective-permute-start(f32[8,128]{1,0:T(8,128)S(1)} %pad_maximum_fusion.2), channel_id=1, source_target_pairs={{0,8},{8,0},{1,9},{9,1},{2,10},{10,2},{3,11},{11,3},{4,12},{12,4},... | collective-permute-start | bytes 12296 | tf_op jit(solution)/shard_map/ppermute | solution.py:272
  105.3 0.1 slice_bitcast_fusion.3
  105.4 2.4 %collective-permute-start.6 = (f32[64]{0:T(128)S(1)}, f32[64]{0:T(128)S(1)}, u32[]{:S(2)}, u32[]{:S(2)}) collective-permute-start(f32[64]{0:T(128)S(1)} %get-tuple-element.32), channel_id=1, source_target_pairs={{0,968},{1,65},{64,0},{65,129},{128,64},{129,193},{192,128},{193,2... | collective-permute-start | bytes 776 | tf_op jit(solution)/shard_map/ppermute | solution.py:275
  107.8 3.8 %collective-permute-start.8 = (f32[64]{0:T(128)S(1)}, f32[64]{0:T(128)S(1)}, u32[]{:S(2)}, u32[]{:S(2)}) collective-permute-start(f32[64]{0:T(128)S(1)} %get-tuple-element.30), channel_id=1, source_target_pairs={{0,969},{1,64},{64,1},{65,128},{128,65},{129,192},{192,129},{193,2... | collective-permute-start | bytes 776 | tf_op jit(solution)/shard_map/ppermute | solution.py:276
  111.5 2.3 %collective-permute-start.9 = (f32[64]{0:T(128)S(1)}, f32[64]{0:T(128)S(1)}, u32[]{:S(2)}, u32[]{:S(2)}) collective-permute-start(f32[64]{0:T(128)S(1)} %get-tuple-element.31), channel_id=1, source_target_pairs={{0,905},{1,128},{64,969},{65,192},{128,1},{129,256},{192,65},{193,... | collective-permute-start | bytes 776 | tf_op jit(solution)/shard_map/ppermute | solution.py:277
  113.8 4.4 %collective-permute-done.7 = f32[8,128]{1,0:T(8,128)S(1)} collective-permute-done((f32[8,128]{1,0:T(8,128)S(1)}, f32[8,128]{1,0:T(8,128)S(1)}, u32[]{:S(2)}, u32[]{:S(2)}) %collective-permute-start.7) | collective-permute-done | bytes 4128 | tf_op jit(solution)/shard_map/ppermute | solution.py:272
  118.2 0.6 add_subtract_fusion
  118.9 0.5 log_add_fusion.3
  (33 shorter events, 0.4 us)
Async XLA Ops:
  0.6 1.3 %copy-start = (bf16[1024,512]{1,0:T(8,128)(2,1)S(1)}, bf16[1024,512]{1,0:T(8,128)(2,1)}, u32[]{:S(2)}) copy-start(bf16[1024,512]{1,0:T(8,128)(2,1)} %param.8) | copy-start | bytes 3145732
  0.6 9.5 %copy-start.2 = (s32[512]{0:T(512)S(1)}, s32[512]{0:T(512)}, u32[]{:S(2)}) copy-start(s32[512]{0:T(512)} %param.11) | copy-start | bytes 6148
  0.7 31.0 %copy-start.1 = (bf16[512,512]{1,0:T(8,128)(2,1)S(1)}, bf16[512,512]{1,0:T(8,128)(2,1)}, u32[]{:S(2)}) copy-start(bf16[512,512]{1,0:T(8,128)(2,1)} %param.10) | copy-start | bytes 1572868
  5.2 7.0 %collective-permute-start = (bf16[72,512]{1,0:T(8,128)(2,1)S(1)}, bf16[72,512]{1,0:T(8,128)(2,1)S(1)}, u32[]{:S(2)}, u32[]{:S(2)}) collective-permute-start(bf16[72,512]{1,0:T(8,128)(2,1)S(1)} %fusion.7), channel_id=1, source_target_pairs={{0,969},{1,64},{64,1},{65,128},{128,65},{129,192},{192,129},{193,2... | collective-permute-start | bytes 221192 | tf_op jit(solution)/shard_map/ppermute | solution.py:223
  12.4 26.1 %collective-permute-start.1 = (bf16[144,512]{1,0:T(8,128)(2,1)S(1)}, bf16[144,512]{1,0:T(8,128)(2,1)S(1)}, u32[]{:S(2)}, u32[]{:S(2)}) collective-permute-start(bf16[144,512]{1,0:T(8,128)(2,1)S(1)} %fusion.4.first_ref), channel_id=1, source_target_pairs={{0,256},{1,777},{64,320},{65,841},{128,384},{129,905},{192,448},{1... | collective-permute-start | bytes 442376 | tf_op jit(solution)/shard_map/ppermute | solution.py:234
  33.2 29.6 %all-to-all-start = ((bf16[4,528,512]{2,1,0:T(8,128)(2,1)}), bf16[4,528,512]{2,1,0:T(8,128)(2,1)S(1)}, u32[]{:S(2)}, u32[]{:S(2)}) async-start(bf16[4,528,512]{2,1,0:T(8,128)(2,1)} %tile.2), calls=%async_computation | async-start | bytes 4325376 | tf_op jit(solution)/shard_map/all_to_all | solution.py:236
  38.5 11.6 %collective-permute-start.2 = (bf16[288,512]{1,0:T(8,128)(2,1)S(1)}, bf16[288,512]{1,0:T(8,128)(2,1)S(1)}, u32[]{:S(2)}, u32[]{:S(2)}) collective-permute-start(bf16[288,512]{1,0:T(8,128)(2,1)S(1)} %shard_map.77.first_ref), channel_id=1, source_target_pairs={{0,128},{1,905},{64,192},{65,969},{128,256},{129,1},{192,320},{193... | collective-permute-start | bytes 884744 | tf_op jit(solution)/shard_map/ppermute | solution.py:238
  51.0 15.9 %collective-permute-start.3 = (bf16[576,512]{1,0:T(8,128)(2,1)}, bf16[576,512]{1,0:T(8,128)(2,1)}, u32[]{:S(2)}, u32[]{:S(2)}) collective-permute-start(bf16[576,512]{1,0:T(8,128)(2,1)} %shard_map.78.refs_0_), channel_id=1, source_target_pairs={{0,64},{1,969},{64,128},{65,1},{128,192},{129,65},{192,256},{193,1... | collective-permute-start | bytes 1769480 | tf_op jit(solution)/shard_map/ppermute | solution.py:239
  71.7 16.1 %collective-permute-start.4 = (f32[4,128]{1,0:T(4,128)S(1)}, f32[4,128]{1,0:T(4,128)S(1)}, u32[]{:S(2)}, u32[]{:S(2)}) collective-permute-start(f32[4,128]{1,0:T(4,128)S(1)} %slice.80), channel_id=1, source_target_pairs={{0,776},{1,257},{64,840},{65,321},{128,904},{129,385},{192,968},{1... | collective-permute-start | bytes 6152 | tf_op jit(solution)/shard_map/ppermute | solution.py:264
  73.6 21.8 %all-to-all-start.1 = ((f32[32,8,128]{2,1,0:T(8,128)}), f32[32,8,128]{2,1,0:T(8,128)S(1)}, u32[]{:S(2)}, u32[]{:S(2)}) async-start(f32[32,8,128]{2,1,0:T(8,128)} %bitcast.20), calls=%async_computation.1 | async-start | bytes 262144 | tf_op jit(solution)/shard_map/all_to_all | solution.py:263
  87.9 17.4 %collective-permute-start.5 = (f32[2,128]{1,0:T(2,128)S(1)}, f32[2,128]{1,0:T(2,128)S(1)}, u32[]{:S(2)}, u32[]{:S(2)}) collective-permute-start(f32[2,128]{1,0:T(2,128)S(1)} %slice.67), channel_id=1, source_target_pairs={{0,904},{1,129},{64,968},{65,193},{128,0},{129,257},{192,64},{193,... | collective-permute-start | bytes 3080 | tf_op jit(solution)/shard_map/ppermute | solution.py:271
  95.6 22.7 %collective-permute-start.7 = (f32[8,128]{1,0:T(8,128)S(1)}, f32[8,128]{1,0:T(8,128)S(1)}, u32[]{:S(2)}, u32[]{:S(2)}) collective-permute-start(f32[8,128]{1,0:T(8,128)S(1)} %pad_maximum_fusion.2), channel_id=1, source_target_pairs={{0,8},{8,0},{1,9},{9,1},{2,10},{10,2},{3,11},{11,3},{4,12},{12,4},... | collective-permute-start | bytes 12296 | tf_op jit(solution)/shard_map/ppermute | solution.py:272
  105.4 13.5 %collective-permute-start.6 = (f32[64]{0:T(128)S(1)}, f32[64]{0:T(128)S(1)}, u32[]{:S(2)}, u32[]{:S(2)}) collective-permute-start(f32[64]{0:T(128)S(1)} %get-tuple-element.32), channel_id=1, source_target_pairs={{0,968},{1,65},{64,0},{65,129},{128,64},{129,193},{192,128},{193,2... | collective-permute-start | bytes 776 | tf_op jit(solution)/shard_map/ppermute | solution.py:275
  107.8 11.1 %collective-permute-start.8 = (f32[64]{0:T(128)S(1)}, f32[64]{0:T(128)S(1)}, u32[]{:S(2)}, u32[]{:S(2)}) collective-permute-start(f32[64]{0:T(128)S(1)} %get-tuple-element.30), channel_id=1, source_target_pairs={{0,969},{1,64},{64,1},{65,128},{128,65},{129,192},{192,129},{193,2... | collective-permute-start | bytes 776 | tf_op jit(solution)/shard_map/ppermute | solution.py:276
  111.5 7.3 %collective-permute-start.9 = (f32[64]{0:T(128)S(1)}, f32[64]{0:T(128)S(1)}, u32[]{:S(2)}, u32[]{:S(2)}) collective-permute-start(f32[64]{0:T(128)S(1)} %get-tuple-element.31), channel_id=1, source_target_pairs={{0,905},{1,128},{64,969},{65,192},{128,1},{129,256},{192,65},{193,... | collective-permute-start | bytes 776 | tf_op jit(solution)/shard_map/ppermute | solution.py:277

commit v6 on v5

--- a/solution.py
+++ b/solution.py
@@ -267,10 +267,10 @@
     top = jnp.max(lse, axis=0)
     lse = top + jnp.log(jnp.sum(jnp.exp(lse - top), axis=0))
     mine = jnp.concatenate([lse, jnp.sum(positive, axis=0)], axis=0)
+    came4, mine = lax.optimization_barrier((came4, mine))
     four = join(stacked[:, :HALF], came4)
+    other = lax.ppermute(mine, "zh", [(0, 1), (1, 0)])
     came2 = lax.ppermute(four[2:], ZC, along(-2))
-    other = lax.ppermute(mine, "zh", [(0, 1), (1, 0)])
-    came2, _ = lax.optimization_barrier((came2, mine))
     two = join(four[:2], came2)
     one_away = lax.ppermute(two[1, :BLOCK], ZC, along(-1))
     cross_one = lax.ppermute(two[0, BLOCK:], ZC, across(1))

time: 120 us -> 120 us (level)
  waiting for transfers between devices: 26.1 us -> 24.2 us
  starting transfers between devices: 74.3 us -> 75.6 us
    all_to_all x1, starting transfers between devices: 14.2 us -> 7.59 us  [on_device(): plane = lax.all_to_all(past, PLANE, 0, 0, tiled=True).reshape(32, 8, 128)]
    ppermute x1, starting transfers between devices: 9.72 us -> 14.9 us  [on_device(): other = lax.ppermute(mine, 'zh', [(0, 1), (1, 0)])]
    ppermute x1, waiting for transfers between devices: 4.42 us -> 0.01 us  [on_device(): other = lax.ppermute(mine, 'zh', [(0, 1), (1, 0)])]
    ppermute x1, starting transfers between devices: 2.27 us -> 4.11 us  [on_device(): cross_two = lax.ppermute(two[1, BLOCK:], ZC, across(2))]
    ppermute x1, waiting for transfers between devices: 0.01 us -> 1.53 us  [on_device(): came4 = lax.ppermute(stacked[:, HALF:], ZC, along(-4))]
  transfers between devices with their start and end apart: 12 -> 12, of which waited for: 6 -> 7; matrix products, arithmetic and copies ran while one was open for 2% -> 2% of each run, Pallas kernels for 4% -> 4%
where the time goes in v6:
time: 120 us; the launch traced here: 119 us
  starting transfers between devices  75.6 us (63%)
  waiting for transfers between devices  24.2 us (20%)
  Pallas kernels  9.7 us (8%)
  matrix products  3.3 us (3%)
  other arithmetic  2.32 us (2%)
  local copies, waits for them, and re-layouts  2.25 us (2%)
  between operations  1.51 us (1%)
    ppermute x1, starting transfers between devices, on_device(): far = lax.ppermute(near, ZC, along(4))  19.3 us
    ppermute x1, starting transfers between devices, on_device(): other = lax.ppermute(mine, 'zh', [(0, 1), (1, 0)])  14.9 us
    pallas_call x2, Pallas kernels, score_call(): pl.pallas_call(functools.partial(score_kernel, first, last, count), out_s...  8.82 us
    all_to_all x1, starting transfers between devices, on_device(): plane = lax.all_to_all(past, PLANE, 0, 0, tiled=True).reshape(32, 8, 128)  7.59 us
    ppermute x1, waiting for transfers between devices, on_device(): evens = stack_call(pair, lax.ppermute(pair, ZC, along(2)), 10 ** 6)  7.28 us
    all_to_all x1, waiting for transfers between devices, on_device(): users = lax.all_to_all(jnp.tile(own, (Y, 1)), 'y', 0, 0, tiled=True)  5.68 us
    all_to_all x1, waiting for transfers between devices, on_device(): plane = lax.all_to_all(past, PLANE, 0, 0, tiled=True).reshape(32, 8, 128)  5.65 us
    ppermute x1, starting transfers between devices, on_device(): odds = lax.ppermute(evens, ZC, along(1))  5.38 us
  transfers between devices with their start and end apart: 12, of which 7 were waited for; matrix products, arithmetic and copies ran while one was open for 2% of the time, Pallas kernels for 4%

profile of v6, /device:TPU:1, one launch (start us, length us, event | category | flops | bytes accessed | tf_op | source)
XLA Modules:
  0.0 118.9 jit_solution(5299347245446335154)
XLA Ops:
  0.7 0.8 fusion.25
  1.5 0.1 maximum_bitcast_fusion
  1.5 0.4 copy-done
  1.9 3.3 %fusion.2 = bf16[64,512]{1,0:T(8,128)(2,1)S(1)} fusion(bf16[1024,512]{1,0:T(8,128)(2,1)S(1)} %copy-done, bf16[64,2048]{1,0:T(8,128)(2,1)} %param.6, bf16[2048,1024]{1,0:T(8,128)(2,1)} %param.7), kind=kOutput, calls=%fused_computation.3 | convolution fusion | flops 335708160 | bytes 5570560 | tf_op jit(solution)/shard_map/dot_general | solution.py:213
  5.2 4.9 %collective-permute-start = (bf16[72,512]{1,0:T(8,128)(2,1)S(1)}, bf16[72,512]{1,0:T(8,128)(2,1)S(1)}, u32[]{:S(2)}, u32[]{:S(2)}) collective-permute-start(bf16[72,512]{1,0:T(8,128)(2,1)S(1)} %fusion.7), channel_id=1, source_target_pairs={{0,969},{1,64},{64,1},{65,128},{128,65},{129,192},{192,129},{193,2... | collective-permute-start | bytes 221192 | tf_op jit(solution)/shard_map/ppermute | solution.py:223
  10.2 2.0 %collective-permute-done = bf16[72,512]{1,0:T(8,128)(2,1)S(1)} collective-permute-done((bf16[72,512]{1,0:T(8,128)(2,1)S(1)}, bf16[72,512]{1,0:T(8,128)(2,1)S(1)}, u32[]{:S(2)}, u32[]{:S(2)}) %collective-permute-start) | collective-permute-done | bytes 73760 | tf_op jit(solution)/shard_map/ppermute | solution.py:223
  12.3 0.1 pad_maximum_fusion.3
  12.4 19.3 %collective-permute-start.1 = (bf16[144,512]{1,0:T(8,128)(2,1)S(1)}, bf16[144,512]{1,0:T(8,128)(2,1)S(1)}, u32[]{:S(2)}, u32[]{:S(2)}) collective-permute-start(bf16[144,512]{1,0:T(8,128)(2,1)S(1)} %fusion.4.first_ref), channel_id=1, source_target_pairs={{0,256},{1,777},{64,320},{65,841},{128,384},{129,905},{192,448},{1... | collective-permute-start | bytes 442376 | tf_op jit(solution)/shard_map/ppermute | solution.py:234
  31.7 1.5 %tile.2 = bf16[4,528,512]{2,1,0:T(8,128)(2,1)} broadcast(bf16[528,512]{1,0:T(8,128)(2,1)S(1)} %pad_maximum_fusion), dimensions={1,2} | broadcast | bytes 2703360 | tf_op jit(solution)/shard_map/tile | solution.py:236
  33.2 4.2 %all-to-all-start = ((bf16[4,528,512]{2,1,0:T(8,128)(2,1)}), bf16[4,528,512]{2,1,0:T(8,128)(2,1)S(1)}, u32[]{:S(2)}, u32[]{:S(2)}) async-start(bf16[4,528,512]{2,1,0:T(8,128)(2,1)} %tile.2), calls=%async_computation | async-start | bytes 4325376 | tf_op jit(solution)/shard_map/all_to_all | solution.py:236
  37.4 1.0 collective-permute-done.1.second_ref
  38.5 4.3 %collective-permute-start.2 = (bf16[288,512]{1,0:T(8,128)(2,1)S(1)}, bf16[288,512]{1,0:T(8,128)(2,1)S(1)}, u32[]{:S(2)}, u32[]{:S(2)}) collective-permute-start(bf16[288,512]{1,0:T(8,128)(2,1)S(1)} %shard_map.77.first_ref), channel_id=1, source_target_pairs={{0,128},{1,905},{64,192},{65,969},{128,256},{129,1},{192,320},{193... | collective-permute-start | bytes 884744 | tf_op jit(solution)/shard_map/ppermute | solution.py:238
  42.8 7.3 %collective-permute-done.2.second_ref = bf16[288,512]{1,0:T(8,128)(2,1)S(1)} collective-permute-done((bf16[288,512]{1,0:T(8,128)(2,1)S(1)}, bf16[288,512]{1,0:T(8,128)(2,1)S(1)}, u32[]{:S(2)}, u32[]{:S(2)}) %collective-permute-start.2) | collective-permute-done | bytes 294944 | tf_op jit(solution)/shard_map/ppermute | solution.py:238
  50.1 0.9 shard_map.78.refs_0_
  51.0 5.4 %collective-permute-start.3 = (bf16[576,512]{1,0:T(8,128)(2,1)}, bf16[576,512]{1,0:T(8,128)(2,1)}, u32[]{:S(2)}, u32[]{:S(2)}) collective-permute-start(bf16[576,512]{1,0:T(8,128)(2,1)} %shard_map.78.refs_0_), channel_id=1, source_target_pairs={{0,64},{1,969},{64,128},{65,1},{128,192},{129,65},{192,256},{193,1... | collective-permute-start | bytes 1769480 | tf_op jit(solution)/shard_map/ppermute | solution.py:239
  57.0 0.1 stack.74.base_ref
  57.0 0.1 stack.86.base_ref
  57.1 5.7 %all-to-all-done = bf16[4,528,512]{2,1,0:T(8,128)(2,1)S(1)} async-done(((bf16[4,528,512]{2,1,0:T(8,128)(2,1)}), bf16[4,528,512]{2,1,0:T(8,128)(2,1)S(1)}, u32[]{:S(2)}, u32[]{:S(2)}) %all-to-all-start) | async-done | bytes 2162720 | tf_op jit(solution)/shard_map/all_to_all | solution.py:236
  62.8 4.1 %shard_map.79 = (f32[1,512]{1,0:T(1,128)S(1)}, f32[8,2048]{1,0:T(8,128)S(1)}) custom-call(s32[8]{0:T(128)S(1)} %stack.74.base_ref, bf16[576,512]{1,0:T(8,128)(2,1)} %shard_map.78.refs_0_, bf16[2112,512]{1,0:T(8,128)(2,1)S(1)} %bitcast.51), custom_call_target="tpu_custom_call" | custom-call | flops 1073741824 | bytes 4194304 | tf_op jit(solution)/shard_map/pallas_call | solution.py:162
  66.9 4.7 %shard_map.80 = (f32[1,512]{1,0:T(1,128)S(1)}, f32[256,128]{1,0:T(8,128)}) custom-call(s32[8]{0:T(128)S(1)} %stack.86.base_ref, bf16[576,512]{1,0:T(8,128)(2,1)} %collective-permute-done.3.refs_0_, bf16[2112,512]{1,0:T(8,128)(2,1)S(1)} %bitcast.52, f32[8,2048]{1,0:T(8,128)S(1)} %get-tuple-element.15.refs_2_), custom_call_target="tpu_custom_call" | custom-call | flops 1073741824 | bytes 4194304 | tf_op jit(solution)/shard_map/pallas_call | solution.py:162
  71.7 7.6 %all-to-all-start.1 = ((f32[32,8,128]{2,1,0:T(8,128)}), f32[32,8,128]{2,1,0:T(8,128)S(1)}, u32[]{:S(2)}, u32[]{:S(2)}) async-start(f32[32,8,128]{2,1,0:T(8,128)} %bitcast.20), calls=%async_computation.1 | async-start | bytes 262144 | tf_op jit(solution)/shard_map/all_to_all | solution.py:263
  79.3 1.9 %collective-permute-start.4 = (f32[4,128]{1,0:T(4,128)S(1)}, f32[4,128]{1,0:T(4,128)S(1)}, u32[]{:S(2)}, u32[]{:S(2)}) collective-permute-start(f32[4,128]{1,0:T(4,128)S(1)} %slice.88), channel_id=1, source_target_pairs={{0,776},{1,257},{64,840},{65,321},{128,904},{129,385},{192,968},{1... | collective-permute-start | bytes 6152 | tf_op jit(solution)/shard_map/ppermute | solution.py:264
  81.2 5.6 %all-to-all-done.1 = f32[32,8,128]{2,1,0:T(8,128)S(1)} async-done(((f32[32,8,128]{2,1,0:T(8,128)}), f32[32,8,128]{2,1,0:T(8,128)S(1)}, u32[]{:S(2)}, u32[]{:S(2)}) %all-to-all-start.1) | async-done | bytes 131104 | tf_op jit(solution)/shard_map/all_to_all | solution.py:263
  87.0 1.5 %collective-permute-done.4 = f32[4,128]{1,0:T(4,128)S(1)} collective-permute-done((f32[4,128]{1,0:T(4,128)S(1)}, f32[4,128]{1,0:T(4,128)S(1)}, u32[]{:S(2)}, u32[]{:S(2)}) %collective-permute-start.4) | collective-permute-done | bytes 2080 | tf_op jit(solution)/shard_map/ppermute | solution.py:264
  88.5 1.9 %collective-permute-start.5 = (f32[2,128]{1,0:T(2,128)S(1)}, f32[2,128]{1,0:T(2,128)S(1)}, u32[]{:S(2)}, u32[]{:S(2)}) collective-permute-start(f32[2,128]{1,0:T(2,128)S(1)} %slice.75), channel_id=1, source_target_pairs={{0,904},{1,129},{64,968},{65,193},{128,0},{129,257},{192,64},{193,... | collective-permute-start | bytes 3080 | tf_op jit(solution)/shard_map/ppermute | solution.py:273
  90.5 14.9 %collective-permute-start.7 = (f32[8,128]{1,0:T(8,128)S(1)}, f32[8,128]{1,0:T(8,128)S(1)}, u32[]{:S(2)}, u32[]{:S(2)}) collective-permute-start(f32[8,128]{1,0:T(8,128)S(1)} %pad_maximum_fusion.2), channel_id=1, source_target_pairs={{0,8},{8,0},{1,9},{9,1},{2,10},{10,2},{3,11},{11,3},{4,12},{12,4},... | collective-permute-start | bytes 12296 | tf_op jit(solution)/shard_map/ppermute | solution.py:272
  105.5 2.5 %collective-permute-start.6 = (f32[64]{0:T(128)S(1)}, f32[64]{0:T(128)S(1)}, u32[]{:S(2)}, u32[]{:S(2)}) collective-permute-start(f32[64]{0:T(128)S(1)} %get-tuple-element.34), channel_id=1, source_target_pairs={{0,968},{1,65},{64,0},{65,129},{128,64},{129,193},{192,128},{193,2... | collective-permute-start | bytes 776 | tf_op jit(solution)/shard_map/ppermute | solution.py:275
  108.0 4.6 %collective-permute-start.8 = (f32[64]{0:T(128)S(1)}, f32[64]{0:T(128)S(1)}, u32[]{:S(2)}, u32[]{:S(2)}) collective-permute-start(f32[64]{0:T(128)S(1)} %get-tuple-element.32), channel_id=1, source_target_pairs={{0,969},{1,64},{64,1},{65,128},{128,65},{129,192},{192,129},{193,2... | collective-permute-start | bytes 776 | tf_op jit(solution)/shard_map/ppermute | solution.py:276
  112.6 4.1 %collective-permute-start.9 = (f32[64]{0:T(128)S(1)}, f32[64]{0:T(128)S(1)}, u32[]{:S(2)}, u32[]{:S(2)}) collective-permute-start(f32[64]{0:T(128)S(1)} %get-tuple-element.33), channel_id=1, source_target_pairs={{0,905},{1,128},{64,969},{65,192},{128,1},{129,256},{192,65},{193,... | collective-permute-start | bytes 776 | tf_op jit(solution)/shard_map/ppermute | solution.py:277
  116.7 0.6 add_subtract_fusion
  117.3 1.0 collective-permute-done.9
  118.3 0.5 log_add_fusion.3
  (33 shorter events, 0.5 us)
Async XLA Ops:
  0.6 1.3 %copy-start = (bf16[1024,512]{1,0:T(8,128)(2,1)S(1)}, bf16[1024,512]{1,0:T(8,128)(2,1)}, u32[]{:S(2)}) copy-start(bf16[1024,512]{1,0:T(8,128)(2,1)} %param.8) | copy-start | bytes 3145732
  0.6 9.5 %copy-start.2 = (s32[512]{0:T(512)S(1)}, s32[512]{0:T(512)}, u32[]{:S(2)}) copy-start(s32[512]{0:T(512)} %param.11) | copy-start | bytes 6148
  0.7 31.0 %copy-start.1 = (bf16[512,512]{1,0:T(8,128)(2,1)S(1)}, bf16[512,512]{1,0:T(8,128)(2,1)}, u32[]{:S(2)}) copy-start(bf16[512,512]{1,0:T(8,128)(2,1)} %param.10) | copy-start | bytes 1572868
  5.2 7.0 %collective-permute-start = (bf16[72,512]{1,0:T(8,128)(2,1)S(1)}, bf16[72,512]{1,0:T(8,128)(2,1)S(1)}, u32[]{:S(2)}, u32[]{:S(2)}) collective-permute-start(bf16[72,512]{1,0:T(8,128)(2,1)S(1)} %fusion.7), channel_id=1, source_target_pairs={{0,969},{1,64},{64,1},{65,128},{128,65},{129,192},{192,129},{193,2... | collective-permute-start | bytes 221192 | tf_op jit(solution)/shard_map/ppermute | solution.py:223
  12.4 26.1 %collective-permute-start.1 = (bf16[144,512]{1,0:T(8,128)(2,1)S(1)}, bf16[144,512]{1,0:T(8,128)(2,1)S(1)}, u32[]{:S(2)}, u32[]{:S(2)}) collective-permute-start(bf16[144,512]{1,0:T(8,128)(2,1)S(1)} %fusion.4.first_ref), channel_id=1, source_target_pairs={{0,256},{1,777},{64,320},{65,841},{128,384},{129,905},{192,448},{1... | collective-permute-start | bytes 442376 | tf_op jit(solution)/shard_map/ppermute | solution.py:234
  33.2 29.6 %all-to-all-start = ((bf16[4,528,512]{2,1,0:T(8,128)(2,1)}), bf16[4,528,512]{2,1,0:T(8,128)(2,1)S(1)}, u32[]{:S(2)}, u32[]{:S(2)}) async-start(bf16[4,528,512]{2,1,0:T(8,128)(2,1)} %tile.2), calls=%async_computation | async-start | bytes 4325376 | tf_op jit(solution)/shard_map/all_to_all | solution.py:236
  38.5 11.6 %collective-permute-start.2 = (bf16[288,512]{1,0:T(8,128)(2,1)S(1)}, bf16[288,512]{1,0:T(8,128)(2,1)S(1)}, u32[]{:S(2)}, u32[]{:S(2)}) collective-permute-start(bf16[288,512]{1,0:T(8,128)(2,1)S(1)} %shard_map.77.first_ref), channel_id=1, source_target_pairs={{0,128},{1,905},{64,192},{65,969},{128,256},{129,1},{192,320},{193... | collective-permute-start | bytes 884744 | tf_op jit(solution)/shard_map/ppermute | solution.py:238
  51.0 15.9 %collective-permute-start.3 = (bf16[576,512]{1,0:T(8,128)(2,1)}, bf16[576,512]{1,0:T(8,128)(2,1)}, u32[]{:S(2)}, u32[]{:S(2)}) collective-permute-start(bf16[576,512]{1,0:T(8,128)(2,1)} %shard_map.78.refs_0_), channel_id=1, source_target_pairs={{0,64},{1,969},{64,128},{65,1},{128,192},{129,65},{192,256},{193,1... | collective-permute-start | bytes 1769480 | tf_op jit(solution)/shard_map/ppermute | solution.py:239
  71.7 15.2 %all-to-all-start.1 = ((f32[32,8,128]{2,1,0:T(8,128)}), f32[32,8,128]{2,1,0:T(8,128)S(1)}, u32[]{:S(2)}, u32[]{:S(2)}) async-start(f32[32,8,128]{2,1,0:T(8,128)} %bitcast.20), calls=%async_computation.1 | async-start | bytes 262144 | tf_op jit(solution)/shard_map/all_to_all | solution.py:263
  79.3 9.2 %collective-permute-start.4 = (f32[4,128]{1,0:T(4,128)S(1)}, f32[4,128]{1,0:T(4,128)S(1)}, u32[]{:S(2)}, u32[]{:S(2)}) collective-permute-start(f32[4,128]{1,0:T(4,128)S(1)} %slice.88), channel_id=1, source_target_pairs={{0,776},{1,257},{64,840},{65,321},{128,904},{129,385},{192,968},{1... | collective-permute-start | bytes 6152 | tf_op jit(solution)/shard_map/ppermute | solution.py:264
  88.5 16.8 %collective-permute-start.5 = (f32[2,128]{1,0:T(2,128)S(1)}, f32[2,128]{1,0:T(2,128)S(1)}, u32[]{:S(2)}, u32[]{:S(2)}) collective-permute-start(f32[2,128]{1,0:T(2,128)S(1)} %slice.75), channel_id=1, source_target_pairs={{0,904},{1,129},{64,968},{65,193},{128,0},{129,257},{192,64},{193,... | collective-permute-start | bytes 3080 | tf_op jit(solution)/shard_map/ppermute | solution.py:273
  90.5 26.2 %collective-permute-start.7 = (f32[8,128]{1,0:T(8,128)S(1)}, f32[8,128]{1,0:T(8,128)S(1)}, u32[]{:S(2)}, u32[]{:S(2)}) collective-permute-start(f32[8,128]{1,0:T(8,128)S(1)} %pad_maximum_fusion.2), channel_id=1, source_target_pairs={{0,8},{8,0},{1,9},{9,1},{2,10},{10,2},{3,11},{11,3},{4,12},{12,4},... | collective-permute-start | bytes 12296 | tf_op jit(solution)/shard_map/ppermute | solution.py:272
  105.5 11.9 %collective-permute-start.6 = (f32[64]{0:T(128)S(1)}, f32[64]{0:T(128)S(1)}, u32[]{:S(2)}, u32[]{:S(2)}) collective-permute-start(f32[64]{0:T(128)S(1)} %get-tuple-element.34), channel_id=1, source_target_pairs={{0,968},{1,65},{64,0},{65,129},{128,64},{129,193},{192,128},{193,2... | collective-permute-start | bytes 776 | tf_op jit(solution)/shard_map/ppermute | solution.py:275
  108.0 9.3 %collective-permute-start.8 = (f32[64]{0:T(128)S(1)}, f32[64]{0:T(128)S(1)}, u32[]{:S(2)}, u32[]{:S(2)}) collective-permute-start(f32[64]{0:T(128)S(1)} %get-tuple-element.32), channel_id=1, source_target_pairs={{0,969},{1,64},{64,1},{65,128},{128,65},{129,192},{192,129},{193,2... | collective-permute-start | bytes 776 | tf_op jit(solution)/shard_map/ppermute | solution.py:276
  112.6 5.8 %collective-permute-start.9 = (f32[64]{0:T(128)S(1)}, f32[64]{0:T(128)S(1)}, u32[]{:S(2)}, u32[]{:S(2)}) collective-permute-start(f32[64]{0:T(128)S(1)} %get-tuple-element.33), channel_id=1, source_target_pairs={{0,905},{1,128},{64,969},{65,192},{128,1},{129,256},{192,65},{193,... | collective-permute-start | bytes 776 | tf_op jit(solution)/shard_map/ppermute | solution.py:277
